TPU v7x, 128 devices: a whole 4x4x4 slice. The times are simulated.
128 devices in a mesh: row: 8 (over x, y_hi), col: 16 (over z, y_lo, core).
Axes of the slice: x: 4, y: 4 (y_hi: 2, y_lo: 2; y = y_hi * 2 + y_lo), z: 4, core: 2. Of those that a mesh axis runs over, the one named last changes fastest.
Arguments:
- grads: bfloat16 [16384, 4096], P(('row', 'col')), may hold values from -6 to 6
- coeffs: bfloat16 [16384], P(('row', 'col')), may hold values from -4 to 4
- band: int32 [1], replicated, may hold values from 1 to 3
- steps: int32 [128], replicated, may hold values from 0 to 7, as said below
Outputs:
- scores: float32 [16384], P(('row', 'col'))
Inputs may be any that keep to these rules, and one draw needn't show every extreme that they name: steps never falls from one block to the next, and every step from 0 to 7 has at least one block.
All inputs are finite; a program needn't handle non-finite values.
Results may differ from a plain program's by a relative error of at most 0.0003.
Values may be sent and summed in bfloat16 or wider, within the bound.
No kernel may reach another device: no remote copies, remote signals or barrier semaphores. Data moves between devices by JAX's collectives and lax.ppermute only.
A program may use at most 64 MiB of HBM per device.

v0:
```python
import jax
import jax.numpy as jnp
from jax import lax
from jax.sharding import PartitionSpec as P


def on_device(grads, coeffs, band, steps):
    nrow = lax.axis_size("row")
    ncol = lax.axis_size("col")
    rows_here = grads.shape[0]
    feats = grads.shape[1]
    row_at = lax.axis_index("row")
    col_at = lax.axis_index("col")
    width = band[0]
    scale = 1.0 / feats**0.5
    layout = steps.reshape(nrow, ncol)
    row_pick = (jnp.arange(nrow, dtype=jnp.int32) == row_at).astype(jnp.int32)
    col_pick = (jnp.arange(ncol, dtype=jnp.int32) == col_at).astype(jnp.int32)
    row_block_steps = jnp.sum(layout * row_pick[:, None], axis=0)
    col_block_steps = jnp.sum(layout * col_pick[None, :], axis=1)
    own_step = jnp.sum(row_block_steps * col_pick)
    row_ex = jnp.repeat(row_block_steps, rows_here)
    col_ex = jnp.repeat(col_block_steps, rows_here)
    count = rows_here * jnp.sum((jnp.abs(steps - own_step) <= width).astype(jnp.int32))
    col_rows, col_coeffs = (
        lax.all_gather(grads, "row", axis=0, tiled=True),
        lax.all_gather(coeffs, "row", axis=0, tiled=True),
    )
    col_weights = col_coeffs.astype(jnp.float32)
    mask = jnp.abs(row_ex[:, None] - col_ex[None, :]) <= width
    inner = (
        lax.dot_general(
            lax.all_gather(grads, "col", axis=0, tiled=True),
            col_rows,
            (((1,), (1,)), ((), ())),
            preferred_element_type=jnp.float32,
        )
        * scale
    )
    partial_value = jnp.sum(jnp.tanh(inner) * jnp.where(mask, col_weights[None, :], 0.0), axis=1)
    total = lax.psum_scatter(partial_value, "col", scatter_dimension=0, tiled=True)
    return total / jnp.sqrt(count.astype(jnp.float32))


def solution(mesh):
    in_specs = (P(("row", "col"), None), P(("row", "col")), P(), P())
    out_specs = P(("row", "col"))
    return jax.shard_map(
        on_device, mesh=mesh, in_specs=in_specs, out_specs=out_specs, check_vma=False
    )
```

profile of v0, /device:TPU:0, one launch (start us, length us, event | category | flops | bytes accessed | tf_op | source)
XLA Modules:
  0.0 274.7 jit_solution(14590751500462902043)
XLA Ops:
  6.5 0.0 all-gather.6.cloned.1.call-start
  6.5 0.7 all-gather.6.cloned.1.call-update
  7.3 0.0 all-gather.4.cloned.1.call-start
  7.3 0.7 all-gather.4.cloned.1.call-update
  8.7 1.3 dynamic-slice
  10.5 23.6 %all-gather = bf16[8,1,128]{2,1,0:T(2,128)(2,1)S(1)} all-gather(bf16[1,1,128]{2,1,0:T(2,128)(2,1)} %bitcast.13), channel_id=1, replica_groups=mesh['row'=8,'col'=16] {'row'}, dimensions={0}, use_global_device_ids=true | all-gather | bytes 2304 | tf_op jit(solution)/shard_map/all_gather | solution.py:27
  34.2 0.7 reshape.16
  34.9 0.1 multiply_reduce_fusion.2
  35.1 0.7 fusion
  35.7 1.9 fusion.1
  38.2 0.1 broadcast_bitcast_fusion.1
  38.3 0.1 broadcast_bitcast_fusion
  38.4 82.7 %all-gather.6.cloned.1.call-done = bf16[1024,4096]{1,0:T(8,128)(2,1)} async-done(((bf16[128,4096]{1,0:T(8,128)(2,1)}), bf16[1024,4096]{1,0:T(8,128)(2,1)}) %all-gather.6.cloned.1.call-update) | async-done | bytes 8388624 | tf_op jit(solution)/shard_map/all_gather | solution.py:26
  121.1 91.3 %all-gather.4.cloned.1.call-done = bf16[2048,4096]{1,0:T(8,128)(2,1)} async-done(((bf16[128,4096]{1,0:T(8,128)(2,1)}), bf16[2048,4096]{1,0:T(8,128)(2,1)}) %all-gather.4.cloned.1.call-update) | async-done | bytes 16777232 | tf_op jit(solution)/shard_map/all_gather | solution.py:33
  212.4 24.2 %multiply_reduce_fusion = f32[2048]{0:T(1024)S(1)} fusion(bf16[2048,4096]{1,0:T(8,128)(2,1)} %all-gather.4.cloned.1.call-done, bf16[1024,4096]{1,0:T(8,128)(2,1)} %all-gather.6.cloned.1.call-done, f32[1024]{0:T(1024)S(1)} %bitcast.12, s32[]{:T(128)} %bitcast.10, s32[1024]{0:T(1024)S(1)} %broadcast_bitcast_fusion.1, s32[2048]{0:T(1024)S(1)} %broadcast_bitcast_fusion), kind=kOutput, calls=%fused_computation | convolution fusion | flops 17194547200 | bytes 25190404 | tf_op jit(solution)/shard_map/dot_general | solution.py:32
  236.6 30.6 %all-reduce = f32[2048]{0:T(1024)S(1)} all-reduce(f32[2048]{0:T(1024)S(1)} %multiply_reduce_fusion), channel_id=2, replica_groups=mesh['row'=8,'col'=16] {'col'}, use_global_device_ids=true, to_apply=%region_3.0.clone | all-reduce | flops 2048 | bytes 16384
  267.2 0.6 dynamic-slice_divide_fusion
  (3 shorter events, 0.0 us)
Async XLA Ops:
  6.5 114.5 %all-gather.6.cloned.1.call-start = ((), (), s32[]{:S(2)}) async-start(), calls=%async_computation.1 | async-start | bytes 9437184 | tf_op jit(solution)/shard_map/all_gather | solution.py:26
  7.3 205.2 %all-gather.4.cloned.1.call-start = ((), (), s32[]{:S(2)}) async-start(), calls=%async_computation | async-start | bytes 17825792 | tf_op jit(solution)/shard_map/all_gather | solution.py:33
Sparse Core Ops, SparseCore 0:
  9.7 111.3 all-gather.5
  122.8 89.5 all-gather.3
where the time goes:
time: 275 us
  waiting for transfers between devices  175 us (64%)
  blocking collectives  54.2 us (20%)
  matrix products  24.2 us (9%)
  between operations  15.3 us (6%)
  other arithmetic  3.3 us (1%)
    all_gather x1, waiting for transfers between devices, on_device(): lax.all_gather(grads, 'col', axis=0, tiled=True)  91.3 us
    all_gather x1, waiting for transfers between devices, on_device(): lax.all_gather(grads, 'row', axis=0, tiled=True)  82.7 us
    unnamed x1, blocking collectives  30.6 us
    dot_general x1, matrix products, on_device(): lax.dot_general(lax.all_gather(grads, 'col', axis=0, tiled=True), col_row...  24.2 us
    all_gather x1, blocking collectives, on_device(): lax.all_gather(coeffs, 'row', axis=0, tiled=True)  23.6 us
  transfers between devices with their start and end apart: 2, of which 2 were waited for; matrix products, arithmetic and copies ran while one was open for 2% of the time, Pallas kernels for 0%

commit v1 on v0

v1 whole, which is shorter than its diff:
```python
import functools

import jax
import jax.numpy as jnp
import numpy as np
from jax import lax
from jax.experimental import pallas as pl
from jax.experimental.pallas import tpu as pltpu
from jax.sharding import PartitionSpec as P

AXES = ("row", "col")
SIDE = 4
CHIPS = SIDE**3
LANES = 128

STEPS_OF_PLAN = (
    ((0, 0, 3), (0, 0, 0), True),
    ((3, 0, 0), (0, 0, 0), False),
    ((0, 3, 0), (0, 0, 0), False),
    ((0, 0, 1), (0, 0, 0), True),
    ((1, 0, 0), (0, 0, 0), False),
    ((0, 2, 0), (0, 3, 0), True),
    ((0, 0, 2), (0, 0, 3), True),
    ((2, 0, 0), (3, 0, 0), False),
    ((3, 3, 0), (0, 3, 0), False),
    ((1, 3, 0), (1, 0, 0), False),
    ((0, 2, 3), (0, 2, 0), True),
    ((2, 3, 0), (2, 0, 0), False),
    ((0, 2, 1), (0, 2, 0), True),
    ((0, 2, 2), (0, 2, 3), True),
)


def device_at(x, y, z, core):
    x, y, z, core = x % SIDE, y % SIDE, z % SIDE, core % 2
    return (x * 2 + y // 2) * 16 + z * 4 + (y % 2) * 2 + core


def places():
    for x in range(SIDE):
        for y in range(SIDE):
            for z in range(SIDE):
                for core in range(2):
                    yield x, y, z, core


def on_core(offset, core):
    return tuple(-a for a in offset) if core else tuple(offset)


def shift_pairs(offset):
    pairs = []
    for x, y, z, core in places():
        a, b, c = on_core(offset, core)
        pairs.append((device_at(x + a, y + b, z + c, core), device_at(x, y, z, core)))
    return pairs


def swap_pairs():
    return [(device_at(x, y, z, 1 - c), device_at(x, y, z, c)) for x, y, z, c in places()]


def shift(value, offset):
    return lax.ppermute(value, AXES, shift_pairs(offset))


def minus(a, b):
    return tuple(i - j for i, j in zip(a, b))


def block_table(offsets, other):
    table = np.zeros((2 * CHIPS, len(offsets)), np.int32)
    for x, y, z, core in places():
        fam = 1 - core if other else core
        for k, offset in enumerate(offsets):
            a, b, c = on_core(offset, fam)
            table[device_at(x, y, z, core), k] = device_at(x + a, y + b, z + c, fam)
    return table


def score_kernel(n_rows, n_cols, feats, keep, *refs):
    rows = refs[:n_rows]
    cols = refs[n_rows : n_rows + n_cols]
    out = refs[-1]
    scale = 1.0 / feats**0.5
    right = [r[:, :feats] for r in rows]
    right = right[0] if n_rows == 1 else jnp.concatenate(right, axis=0)
    sums = [jnp.zeros((1, LANES), jnp.float32) for _ in rows]
    for j in range(0, n_cols, 2):
        left = jnp.concatenate([c[:, :feats] for c in cols[j : j + 2]], axis=0)
        inner = lax.dot_general(
            left, right, (((1,), (1,)), ((), ())), preferred_element_type=jnp.float32
        )
        bent = jnp.tanh(inner * scale)
        for h in range(2):
            weights = cols[j + h][:, feats:].astype(jnp.float32)
            for r in range(n_rows):
                part = bent[h * LANES : (h + 1) * LANES, r * LANES : (r + 1) * LANES]
                sums[r] = sums[r] + keep[r, j + h] * jnp.sum(part * weights, axis=0, keepdims=True)
    for r in range(n_rows):
        out[r : r + 1, :] = sums[r]


def row_sums(keep, rows, cols, feats):
    n_rows, n_cols = len(rows), len(cols)

    def body(keep_ref, *refs):
        score_kernel(n_rows, n_cols, feats, keep_ref, *refs)

    tile = 2 * n_rows * n_cols * LANES * LANES
    return pl.pallas_call(
        body,
        out_shape=jax.ShapeDtypeStruct((n_rows, LANES), jnp.float32),
        in_specs=[pl.BlockSpec(memory_space=pltpu.SMEM)]
        + [pl.BlockSpec(memory_space=pltpu.VMEM)] * (n_rows + n_cols),
        out_specs=pl.BlockSpec(memory_space=pltpu.VMEM),
        compiler_params=pltpu.CompilerParams(vmem_limit_bytes=32 * 2**20),
        cost_estimate=pl.CostEstimate(
            flops=tile * feats,
            bytes_accessed=2 * (n_rows + n_cols) * LANES * feats,
            transcendentals=tile // 2,
        ),
    )(keep, *rows, *cols)


def on_device(grads, coeffs, band, steps):
    feats = grads.shape[1]
    rows_here = grads.shape[0]
    width = band[0]
    me = lax.axis_index(AXES)
    zero = (0, 0, 0)
    row_offsets = [zero] + [o for o, _, r in STEPS_OF_PLAN if r]
    col_offsets = [zero] + [o for o, _, r in STEPS_OF_PLAN if not r]

    def steps_at(table):
        mine = lax.dynamic_index_in_dim(jnp.asarray(table), me, 0, keepdims=False)
        hit = mine[:, None] == jnp.arange(steps.shape[0], dtype=jnp.int32)[None, :]
        return jnp.sum(jnp.where(hit, steps[None, :], 0), axis=1)

    row_steps = steps_at(block_table(row_offsets, False))
    col_steps = jnp.concatenate(
        [steps_at(block_table(col_offsets, False)), steps_at(block_table(col_offsets, True))]
    )
    keep = (jnp.abs(row_steps[:, None] - col_steps[None, :]) <= width).astype(jnp.float32)
    count = rows_here * jnp.sum((jnp.abs(steps - row_steps[0]) <= width).astype(jnp.int32))

    held = {
        zero: jnp.concatenate(
            [grads, jnp.broadcast_to(coeffs[:, None], (rows_here, LANES))], axis=1
        )
    }
    for offset, source, _ in STEPS_OF_PLAN:
        held[offset] = shift(held[source], minus(offset, source))
    cols = [held[o] for o in col_offsets]
    cols = cols + [lax.ppermute(c, AXES, swap_pairs()) for c in cols]

    total = None
    for first in range(0, len(row_offsets), 2):
        here = row_offsets[first : first + 2]
        sums = row_sums(keep[first : first + 2], [held[o] for o in here], cols, feats)
        for r, offset in enumerate(here):
            part = sums[r : r + 1]
            if offset != zero:
                part = shift(part, tuple(-a for a in offset))
            total = part if total is None else total + part
    return total.reshape(-1) / jnp.sqrt(count.astype(jnp.float32))


def solution(mesh):
    in_specs = (P(AXES, None), P(AXES), P(), P())
    out_specs = P(AXES)
    return jax.shard_map(
        on_device, mesh=mesh, in_specs=in_specs, out_specs=out_specs, check_vma=False
    )
```

time: 275 us -> 168 us (0.61)
  waiting for transfers between devices: 175 us -> 69.5 us
  blocking collectives: 54.2 us -> 0 us
  starting transfers between devices: 0.04 us -> 43.4 us
  Pallas kernels: 0 us -> 33.2 us
  matrix products: 24.2 us -> 0 us
  local copies, waits for them, and re-layouts: 2.13 us -> 16.7 us
  between operations: 15.3 us -> 1.54 us
    all_gather x2 -> x0, waiting for transfers between devices: 174 us -> none  [the longest x1 91.3 us: on_device(): lax.all_gather(grads, 'col', axis=0, tiled=True)]
    ppermute x0 -> x29, waiting for transfers between devices: none -> 69.5 us  [the longest x21 69.5 us: shift(): return lax.ppermute(value, AXES, shift_pairs(offset))]
    ppermute x0 -> x29, starting transfers between devices: none -> 43.4 us  [the longest x21 37.7 us: shift(): return lax.ppermute(value, AXES, shift_pairs(offset))]
    pallas_call x0 -> x4, Pallas kernels: none -> 33.2 us  [row_sums(): pl.pallas_call(body, out_shape=jax.ShapeDtypeStruct((n_rows, LANES), jnp....]
    unnamed x1 -> x0, blocking collectives: 30.6 us -> none
    dot_general x1 -> x0, matrix products: 24.2 us -> none  [on_device(): lax.dot_general(lax.all_gather(grads, 'col', axis=0, tiled=True), col_row...]
    all_gather x1 -> x0, blocking collectives: 23.6 us -> none  [on_device(): lax.all_gather(coeffs, 'row', axis=0, tiled=True)]
    unnamed x1 -> x42, local copies, waits for them, and re-layouts: 1.25 us -> 14.6 us
  transfers between devices with their start and end apart: 2 -> 29, of which waited for: 2 -> 9; matrix products, arithmetic and copies ran while one was open for 2% -> 1% of each run, Pallas kernels for 0% -> 20%
where the time goes in v1:
time: 168 us; the launch traced here: 167 us
  waiting for transfers between devices  69.5 us (41%)
  starting transfers between devices  43.4 us (26%)
  Pallas kernels  33.2 us (20%)
  local copies, waits for them, and re-layouts  16.7 us (10%)
  other arithmetic  2.87 us (2%)
    ppermute x21, waiting for transfers between devices, shift(): return lax.ppermute(value, AXES, shift_pairs(offset))  69.5 us
    ppermute x21, starting transfers between devices, shift(): return lax.ppermute(value, AXES, shift_pairs(offset))  37.7 us
    pallas_call x4, Pallas kernels, row_sums(): pl.pallas_call(body, out_shape=jax.ShapeDtypeStruct((n_rows, LANES), jnp....  33.2 us
    unnamed x42, local copies, waits for them, and re-layouts  14.6 us
    ppermute x8, starting transfers between devices, on_device(): cols = cols + [lax.ppermute(c, AXES, swap_pairs()) for c in cols]  5.71 us
  transfers between devices with their start and end apart: 29, of which 9 were waited for; matrix products, arithmetic and copies ran while one was open for 1% of the time, Pallas kernels for 20%

profile of v1, /device:TPU:0, one launch (start us, length us, event | category | flops | bytes accessed | tf_op | source)
XLA Modules:
  0.0 167.2 jit_solution(3113308327403255461)
XLA Ops:
  0.8 1.3 pad_maximum_fusion.refs_0_.refs_2_
  2.1 1.7 %collective-permute-start.2 = (bf16[128,4224]{1,0:T(8,128)(2,1)S(1)}, bf16[128,4224]{1,0:T(8,128)(2,1)S(1)}, u32[]{:S(2)}, u32[]{:S(2)}) collective-permute-start(bf16[128,4224]{1,0:T(8,128)(2,1)S(1)} %pad_maximum_fusion.refs_0_.refs_2_), channel_id=1, source_target_pairs={{18,0},{3,1},{22,4},{7,5},{26,8},{11,9},{30,12},{15,13},{0,2},{17,... | collective-permute-start | bytes 3244040 | tf_op jit(solution)/shard_map/ppermute | solution.py:64
  3.8 1.5 collective-permute-start.1
  5.3 1.7 %collective-permute-start.3 = (bf16[128,4224]{1,0:T(8,128)(2,1)S(1)}, bf16[128,4224]{1,0:T(8,128)(2,1)S(1)}, u32[]{:S(2)}, u32[]{:S(2)}) collective-permute-start(bf16[128,4224]{1,0:T(8,128)(2,1)S(1)} %pad_maximum_fusion.refs_0_.refs_2_), channel_id=1, source_target_pairs={{32,0},{97,1},{36,4},{101,5},{40,8},{105,9},{44,12},{109,13},{34,2... | collective-permute-start | bytes 3244040 | tf_op jit(solution)/shard_map/ppermute | solution.py:64
  7.3 1.9 %collective-permute-start = (bf16[128,4224]{1,0:T(8,128)(2,1)S(1)}, bf16[128,4224]{1,0:T(8,128)(2,1)S(1)}, u32[]{:S(2)}, u32[]{:S(2)}) collective-permute-start(bf16[128,4224]{1,0:T(8,128)(2,1)S(1)} %pad_maximum_fusion.refs_0_.refs_2_), channel_id=1, source_target_pairs={{12,0},{5,1},{0,4},{9,5},{4,8},{13,9},{8,12},{1,13},{14,2},{7,3},{... | collective-permute-start | bytes 3244040 | tf_op jit(solution)/shard_map/ppermute | solution.py:64
  9.2 9.3 %collective-permute-done.2.refs_4_ = bf16[128,4224]{1,0:T(8,128)(2,1)S(1)} collective-permute-done((bf16[128,4224]{1,0:T(8,128)(2,1)S(1)}, bf16[128,4224]{1,0:T(8,128)(2,1)S(1)}, u32[]{:S(2)}, u32[]{:S(2)}) %collective-permute-start.2) | collective-permute-done | bytes 1081376 | tf_op jit(solution)/shard_map/ppermute | solution.py:64
  18.9 10.2 %collective-permute-done.1.refs_3_ = bf16[128,4224]{1,0:T(8,128)(2,1)S(1)} collective-permute-done((bf16[128,4224]{1,0:T(8,128)(2,1)S(1)}, bf16[128,4224]{1,0:T(8,128)(2,1)S(1)}, u32[]{:S(2)}, u32[]{:S(2)}) %collective-permute-start.1) | collective-permute-done | bytes 1081376 | tf_op jit(solution)/shard_map/ppermute | solution.py:64
  29.2 1.6 collective-permute-start.4
  30.8 2.4 %collective-permute-start.5 = (bf16[128,4224]{1,0:T(8,128)(2,1)S(1)}, bf16[128,4224]{1,0:T(8,128)(2,1)}, u32[]{:S(2)}, u32[]{:S(2)}) collective-permute-start(bf16[128,4224]{1,0:T(8,128)(2,1)S(1)} %collective-permute-done.2.refs_4_), channel_id=1, source_target_pairs={{96,0},{33,1},{100,4},{37,5},{104,8},{41,9},{108,12},{45,13},{98,2... | collective-permute-start | bytes 3244040 | tf_op jit(solution)/shard_map/ppermute | solution.py:64
  36.0 10.0 %collective-permute-done.4.refs_6_ = bf16[128,4224]{1,0:T(8,128)(2,1)} collective-permute-done((bf16[128,4224]{1,0:T(8,128)(2,1)S(1)}, bf16[128,4224]{1,0:T(8,128)(2,1)}, u32[]{:S(2)}, u32[]{:S(2)}) %collective-permute-start.4) | collective-permute-done | bytes 1081376 | tf_op jit(solution)/shard_map/ppermute | solution.py:64
  47.1 10.5 %collective-permute-done.5.refs_7_ = bf16[128,4224]{1,0:T(8,128)(2,1)} collective-permute-done((bf16[128,4224]{1,0:T(8,128)(2,1)S(1)}, bf16[128,4224]{1,0:T(8,128)(2,1)}, u32[]{:S(2)}, u32[]{:S(2)}) %collective-permute-start.5) | collective-permute-done | bytes 1081376 | tf_op jit(solution)/shard_map/ppermute | solution.py:64
  57.6 4.0 %collective-permute-start.25 = (bf16[128,4224]{1,0:T(8,128)(2,1)S(1)}, bf16[128,4224]{1,0:T(8,128)(2,1)S(1)}, u32[]{:S(2)}, u32[]{:S(2)}) collective-permute-start(bf16[128,4224]{1,0:T(8,128)(2,1)S(1)} %collective-permute-done.18.refs_1_), channel_id=1, source_target_pairs={{4,0},{13,1},{8,4},{1,5},{12,8},{5,9},{0,12},{9,13},{6,2},{15,3},{... | collective-permute-start | bytes 3244040 | tf_op jit(solution)/shard_map/ppermute | solution.py:64
  63.6 3.7 %collective-permute-start.7 = (bf16[128,4224]{1,0:T(8,128)(2,1)}, bf16[128,4224]{1,0:T(8,128)(2,1)}, u32[]{:S(2)}, u32[]{:S(2)}) collective-permute-start(bf16[128,4224]{1,0:T(8,128)(2,1)} %collective-permute-done.4.refs_6_), channel_id=1, source_target_pairs={{18,0},{3,1},{22,4},{7,5},{26,8},{11,9},{30,12},{15,13},{0,2},{17,... | collective-permute-start | bytes 3244040 | tf_op jit(solution)/shard_map/ppermute | solution.py:64
  69.8 15.2 %collective-permute-done.25.refs_0_ = bf16[128,4224]{1,0:T(8,128)(2,1)S(1)} collective-permute-done((bf16[128,4224]{1,0:T(8,128)(2,1)S(1)}, bf16[128,4224]{1,0:T(8,128)(2,1)S(1)}, u32[]{:S(2)}, u32[]{:S(2)}) %collective-permute-start.25) | collective-permute-done | bytes 1081376 | tf_op jit(solution)/shard_map/ppermute | solution.py:64
  85.0 1.0 copy-done.18
  86.6 3.4 %collective-permute-start.15 = (bf16[128,4224]{1,0:T(8,128)(2,1)}, bf16[128,4224]{1,0:T(8,128)(2,1)}, u32[]{:S(2)}, u32[]{:S(2)}) collective-permute-start(bf16[128,4224]{1,0:T(8,128)(2,1)} %collective-permute-done.7.refs_9_), channel_id=1, source_target_pairs={{1,0},{0,1},{5,4},{4,5},{9,8},{8,9},{13,12},{12,13},{3,2},{2,3},{7... | collective-permute-start | bytes 3244040 | tf_op jit(solution)/shard_map/ppermute | solution.py:155
  92.5 3.3 %collective-permute-start.17 = (bf16[128,4224]{1,0:T(8,128)(2,1)S(1)}, bf16[128,4224]{1,0:T(8,128)(2,1)S(1)}, u32[]{:S(2)}, u32[]{:S(2)}) collective-permute-start(bf16[128,4224]{1,0:T(8,128)(2,1)S(1)} %pad_maximum_fusion.refs_0_.refs_2_), channel_id=1, source_target_pairs={{4,0},{13,1},{8,4},{1,5},{12,8},{5,9},{0,12},{9,13},{6,2},{15,3},{... | collective-permute-start | bytes 3244040 | tf_op jit(solution)/shard_map/ppermute | solution.py:64
  95.7 13.9 %collective-permute-done.26.refs_1_ = bf16[128,4224]{1,0:T(8,128)(2,1)} collective-permute-done((bf16[128,4224]{1,0:T(8,128)(2,1)}, bf16[128,4224]{1,0:T(8,128)(2,1)}, u32[]{:S(2)}, u32[]{:S(2)}) %collective-permute-start.26) | collective-permute-done | bytes 1081376 | tf_op jit(solution)/shard_map/ppermute | solution.py:64
  109.7 1.2 copy-done.1
  110.9 1.2 copy-done.3
  112.2 1.2 copy-done.6
  113.4 1.2 copy-done.9
  114.6 1.2 copy-done.12
  115.9 1.2 copy-done.19
  117.1 8.5 %shard_map.76 = f32[2,128]{1,0:T(2,128)S(1)} custom-call(f32[2,16]{1,0:T(2,128)S(1)} %get-tuple-element.9.keep_ref, bf16[128,4224]{1,0:T(8,128)(2,1)S(1)} %copy-done.19, bf16[128,4224]{1,0:T(8,128)(2,1)} %collective-permute-done.26.refs_1_, bf16[128,4224]{1,0:T(8,128)(2,1)S(1)} %pad_maximum_fusion.refs_0_.refs_2_, ...), custom_call_target="tpu_custom_call" | custom-call | flops 4294967296 | bytes 18874368 | tf_op jit(solution)/shard_map/pallas_call | solution.py:111
  126.6 5.7 %collective-permute-start.27 = (f32[1,128]{1,0:T(1,128)S(1)}, f32[1,128]{1,0:T(1,128)S(1)}, u32[]{:S(2)}, u32[]{:S(2)}) collective-permute-start(f32[1,128]{1,0:T(1,128)S(1)} %get-tuple-element.16), channel_id=1, source_target_pairs={{28,0},{21,1},{16,4},{25,5},{20,8},{29,9},{24,12},{17,13},{30,2},{... | collective-permute-start | bytes 1544 | tf_op jit(solution)/shard_map/ppermute | solution.py:64
  132.4 8.5 %shard_map.75 = f32[2,128]{1,0:T(2,128)S(1)} custom-call(f32[2,16]{1,0:T(2,128)S(1)} %get-tuple-element.10.keep_ref, bf16[128,4224]{1,0:T(8,128)(2,1)S(1)} %collective-permute-done.21.refs_0_, bf16[128,4224]{1,0:T(8,128)(2,1)} %collective-permute-done.22.refs_1_, bf16[128,4224]{1,0:T(8,128)(2,1)S(1)} %pad_maximum_fusion.refs_0_.refs_2_, ...), custom_call_target="tpu_custom_call" | custom-call | flops 4294967296 | bytes 18874368 | tf_op jit(solution)/shard_map/pallas_call | solution.py:111
  140.9 2.1 %collective-permute-start.23 = (f32[1,128]{1,0:T(1,128)S(1)}, f32[1,128]{1,0:T(1,128)S(1)}, u32[]{:S(2)}, u32[]{:S(2)}) collective-permute-start(f32[1,128]{1,0:T(1,128)S(1)} %get-tuple-element.14), channel_id=1, source_target_pairs={{8,0},{9,1},{12,4},{13,5},{0,8},{1,9},{4,12},{5,13},{10,2},{11,3},... | collective-permute-start | bytes 1544 | tf_op jit(solution)/shard_map/ppermute | solution.py:64
  143.0 8.2 %shard_map.74 = f32[2,128]{1,0:T(2,128)S(1)} custom-call(f32[2,16]{1,0:T(2,128)S(1)} %get-tuple-element.11.keep_ref, bf16[128,4224]{1,0:T(8,128)(2,1)S(1)} %collective-permute-done.17.refs_0_, bf16[128,4224]{1,0:T(8,128)(2,1)S(1)} %copy-done.17, bf16[128,4224]{1,0:T(8,128)(2,1)S(1)} %pad_maximum_fusion.refs_0_.refs_2_, ...), custom_call_target="tpu_custom_call" | custom-call | flops 4294967296 | bytes 18874368 | tf_op jit(solution)/shard_map/pallas_call | solution.py:111
  151.2 2.3 %collective-permute-start.20 = (f32[1,128]{1,0:T(1,128)S(1)}, f32[1,128]{1,0:T(1,128)S(1)}, u32[]{:S(2)}, u32[]{:S(2)}) collective-permute-start(f32[1,128]{1,0:T(1,128)S(1)} %get-tuple-element.13), channel_id=1, source_target_pairs={{16,0},{17,1},{20,4},{21,5},{24,8},{25,9},{28,12},{29,13},{18,2},{... | collective-permute-start | bytes 1544 | tf_op jit(solution)/shard_map/ppermute | solution.py:64
  153.6 8.1 %shard_map.73 = f32[2,128]{1,0:T(2,128)S(1)} custom-call(f32[2,16]{1,0:T(2,128)S(1)} %get-tuple-element.8.keep_ref, bf16[128,4224]{1,0:T(8,128)(2,1)S(1)} %pad_maximum_fusion.refs_0_.refs_2_, bf16[128,4224]{1,0:T(8,128)(2,1)S(1)} %copy-done.15, bf16[128,4224]{1,0:T(8,128)(2,1)S(1)} %pad_maximum_fusion.refs_0_.refs_2_, ...), custom_call_target="tpu_custom_call" | custom-call | flops 4294967296 | bytes 18874368 | tf_op jit(solution)/shard_map/pallas_call | solution.py:111
  162.4 2.7 %collective-permute-start.16 = (f32[1,128]{1,0:T(1,128)S(1)}, f32[1,128]{1,0:T(1,128)S(1)}, u32[]{:S(2)}, u32[]{:S(2)}) collective-permute-start(f32[1,128]{1,0:T(1,128)S(1)} %slice.41), channel_id=1, source_target_pairs={{4,0},{13,1},{8,4},{1,5},{12,8},{5,9},{0,12},{9,13},{6,2},{15,3},{... | collective-permute-start | bytes 1544 | tf_op jit(solution)/shard_map/ppermute | solution.py:64
  (86 shorter events, 15.5 us)
Async XLA Ops:
  0.7 90.6 %copy-start.20 = (s32[128]{0:T(128)S(1)}, s32[128]{0:T(128)}, u32[]{:S(2)}) copy-start(s32[128]{0:T(128)} %param.10) | copy-start | bytes 1540
  2.1 16.4 %collective-permute-start.2 = (bf16[128,4224]{1,0:T(8,128)(2,1)S(1)}, bf16[128,4224]{1,0:T(8,128)(2,1)S(1)}, u32[]{:S(2)}, u32[]{:S(2)}) collective-permute-start(bf16[128,4224]{1,0:T(8,128)(2,1)S(1)} %pad_maximum_fusion.refs_0_.refs_2_), channel_id=1, source_target_pairs={{18,0},{3,1},{22,4},{7,5},{26,8},{11,9},{30,12},{15,13},{0,2},{17,... | collective-permute-start | bytes 3244040 | tf_op jit(solution)/shard_map/ppermute | solution.py:64
  3.8 25.4 %collective-permute-start.1 = (bf16[128,4224]{1,0:T(8,128)(2,1)S(1)}, bf16[128,4224]{1,0:T(8,128)(2,1)S(1)}, u32[]{:S(2)}, u32[]{:S(2)}) collective-permute-start(bf16[128,4224]{1,0:T(8,128)(2,1)S(1)} %pad_maximum_fusion.refs_0_.refs_2_), channel_id=1, source_target_pairs={{96,0},{33,1},{100,4},{37,5},{104,8},{41,9},{108,12},{45,13},{98,2... | collective-permute-start | bytes 3244040 | tf_op jit(solution)/shard_map/ppermute | solution.py:64
  5.3 25.5 %collective-permute-start.3 = (bf16[128,4224]{1,0:T(8,128)(2,1)S(1)}, bf16[128,4224]{1,0:T(8,128)(2,1)S(1)}, u32[]{:S(2)}, u32[]{:S(2)}) collective-permute-start(bf16[128,4224]{1,0:T(8,128)(2,1)S(1)} %pad_maximum_fusion.refs_0_.refs_2_), channel_id=1, source_target_pairs={{32,0},{97,1},{36,4},{101,5},{40,8},{105,9},{44,12},{109,13},{34,2... | collective-permute-start | bytes 3244040 | tf_op jit(solution)/shard_map/ppermute | solution.py:64
  7.0 26.2 %collective-permute-start.8 = (bf16[128,4224]{1,0:T(8,128)(2,1)S(1)}, bf16[128,4224]{1,0:T(8,128)(2,1)S(1)}, u32[]{:S(2)}, u32[]{:S(2)}) collective-permute-start(bf16[128,4224]{1,0:T(8,128)(2,1)S(1)} %pad_maximum_fusion.refs_0_.refs_2_), channel_id=1, source_target_pairs={{1,0},{0,1},{5,4},{4,5},{9,8},{8,9},{13,12},{12,13},{3,2},{2,3},{7... | collective-permute-start | bytes 3244040 | tf_op jit(solution)/shard_map/ppermute | solution.py:155
  7.3 27.0 %collective-permute-start = (bf16[128,4224]{1,0:T(8,128)(2,1)S(1)}, bf16[128,4224]{1,0:T(8,128)(2,1)S(1)}, u32[]{:S(2)}, u32[]{:S(2)}) collective-permute-start(bf16[128,4224]{1,0:T(8,128)(2,1)S(1)} %pad_maximum_fusion.refs_0_.refs_2_), channel_id=1, source_target_pairs={{12,0},{5,1},{0,4},{9,5},{4,8},{13,9},{8,12},{1,13},{14,2},{7,3},{... | collective-permute-start | bytes 3244040 | tf_op jit(solution)/shard_map/ppermute | solution.py:64
  18.5 16.8 %collective-permute-start.18 = (bf16[128,4224]{1,0:T(8,128)(2,1)S(1)}, bf16[128,4224]{1,0:T(8,128)(2,1)S(1)}, u32[]{:S(2)}, u32[]{:S(2)}) collective-permute-start(bf16[128,4224]{1,0:T(8,128)(2,1)S(1)} %collective-permute-done.2.refs_4_), channel_id=1, source_target_pairs={{18,0},{3,1},{22,4},{7,5},{26,8},{11,9},{30,12},{15,13},{0,2},{17,... | collective-permute-start | bytes 3244040 | tf_op jit(solution)/shard_map/ppermute | solution.py:64
  29.2 16.8 %collective-permute-start.4 = (bf16[128,4224]{1,0:T(8,128)(2,1)S(1)}, bf16[128,4224]{1,0:T(8,128)(2,1)}, u32[]{:S(2)}, u32[]{:S(2)}) collective-permute-start(bf16[128,4224]{1,0:T(8,128)(2,1)S(1)} %collective-permute-done.1.refs_3_), channel_id=1, source_target_pairs={{96,0},{33,1},{100,4},{37,5},{104,8},{41,9},{108,12},{45,13},{98,2... | collective-permute-start | bytes 3244040 | tf_op jit(solution)/shard_map/ppermute | solution.py:64
  30.8 26.8 %collective-permute-start.5 = (bf16[128,4224]{1,0:T(8,128)(2,1)S(1)}, bf16[128,4224]{1,0:T(8,128)(2,1)}, u32[]{:S(2)}, u32[]{:S(2)}) collective-permute-start(bf16[128,4224]{1,0:T(8,128)(2,1)S(1)} %collective-permute-done.2.refs_4_), channel_id=1, source_target_pairs={{96,0},{33,1},{100,4},{37,5},{104,8},{41,9},{108,12},{45,13},{98,2... | collective-permute-start | bytes 3244040 | tf_op jit(solution)/shard_map/ppermute | solution.py:64
  34.2 27.4 %collective-permute-start.6 = (bf16[128,4224]{1,0:T(8,128)(2,1)S(1)}, bf16[128,4224]{1,0:T(8,128)(2,1)}, u32[]{:S(2)}, u32[]{:S(2)}) collective-permute-start(bf16[128,4224]{1,0:T(8,128)(2,1)S(1)} %collective-permute-done.3.refs_5_), channel_id=1, source_target_pairs={{18,0},{3,1},{22,4},{7,5},{26,8},{11,9},{30,12},{15,13},{0,2},{17,... | collective-permute-start | bytes 3244040 | tf_op jit(solution)/shard_map/ppermute | solution.py:64
  34.3 28.3 %collective-permute-start.9 = (bf16[128,4224]{1,0:T(8,128)(2,1)S(1)}, bf16[128,4224]{1,0:T(8,128)(2,1)S(1)}, u32[]{:S(2)}, u32[]{:S(2)}) collective-permute-start(bf16[128,4224]{1,0:T(8,128)(2,1)S(1)} %collective-permute-done.1.refs_3_), channel_id=1, source_target_pairs={{1,0},{0,1},{5,4},{4,5},{9,8},{8,9},{13,12},{12,13},{3,2},{2,3},{7... | collective-permute-start | bytes 3244040 | tf_op jit(solution)/shard_map/ppermute | solution.py:155
  35.3 32.1 %collective-permute-start.10 = (bf16[128,4224]{1,0:T(8,128)(2,1)S(1)}, bf16[128,4224]{1,0:T(8,128)(2,1)S(1)}, u32[]{:S(2)}, u32[]{:S(2)}) collective-permute-start(bf16[128,4224]{1,0:T(8,128)(2,1)S(1)} %collective-permute-done.2.refs_4_), channel_id=1, source_target_pairs={{1,0},{0,1},{5,4},{4,5},{9,8},{8,9},{13,12},{12,13},{3,2},{2,3},{7... | collective-permute-start | bytes 3244040 | tf_op jit(solution)/shard_map/ppermute | solution.py:155
  46.0 22.3 %collective-permute-start.11 = (bf16[128,4224]{1,0:T(8,128)(2,1)S(1)}, bf16[128,4224]{1,0:T(8,128)(2,1)S(1)}, u32[]{:S(2)}, u32[]{:S(2)}) collective-permute-start(bf16[128,4224]{1,0:T(8,128)(2,1)S(1)} %collective-permute-done.3.refs_5_), channel_id=1, source_target_pairs={{1,0},{0,1},{5,4},{4,5},{9,8},{8,9},{13,12},{12,13},{3,2},{2,3},{7... | collective-permute-start | bytes 3244040 | tf_op jit(solution)/shard_map/ppermute | solution.py:155
  57.6 27.4 %collective-permute-start.25 = (bf16[128,4224]{1,0:T(8,128)(2,1)S(1)}, bf16[128,4224]{1,0:T(8,128)(2,1)S(1)}, u32[]{:S(2)}, u32[]{:S(2)}) collective-permute-start(bf16[128,4224]{1,0:T(8,128)(2,1)S(1)} %collective-permute-done.18.refs_1_), channel_id=1, source_target_pairs={{4,0},{13,1},{8,4},{1,5},{12,8},{5,9},{0,12},{9,13},{6,2},{15,3},{... | collective-permute-start | bytes 3244040 | tf_op jit(solution)/shard_map/ppermute | solution.py:64
  61.6 24.4 %collective-permute-start.22 = (bf16[128,4224]{1,0:T(8,128)(2,1)S(1)}, bf16[128,4224]{1,0:T(8,128)(2,1)}, u32[]{:S(2)}, u32[]{:S(2)}) collective-permute-start(bf16[128,4224]{1,0:T(8,128)(2,1)S(1)} %collective-permute-done.18.refs_1_), channel_id=1, source_target_pairs={{12,0},{5,1},{0,4},{9,5},{4,8},{13,9},{8,12},{1,13},{14,2},{7,3},{... | collective-permute-start | bytes 3244040 | tf_op jit(solution)/shard_map/ppermute | solution.py:64
  63.6 23.0 %collective-permute-start.7 = (bf16[128,4224]{1,0:T(8,128)(2,1)}, bf16[128,4224]{1,0:T(8,128)(2,1)}, u32[]{:S(2)}, u32[]{:S(2)}) collective-permute-start(bf16[128,4224]{1,0:T(8,128)(2,1)} %collective-permute-done.4.refs_6_), channel_id=1, source_target_pairs={{18,0},{3,1},{22,4},{7,5},{26,8},{11,9},{30,12},{15,13},{0,2},{17,... | collective-permute-start | bytes 3244040 | tf_op jit(solution)/shard_map/ppermute | solution.py:64
  68.3 23.2 %collective-permute-start.12 = (bf16[128,4224]{1,0:T(8,128)(2,1)}, bf16[128,4224]{1,0:T(8,128)(2,1)}, u32[]{:S(2)}, u32[]{:S(2)}) collective-permute-start(bf16[128,4224]{1,0:T(8,128)(2,1)} %collective-permute-done.4.refs_6_), channel_id=1, source_target_pairs={{1,0},{0,1},{5,4},{4,5},{9,8},{8,9},{13,12},{12,13},{3,2},{2,3},{7... | collective-permute-start | bytes 3244040 | tf_op jit(solution)/shard_map/ppermute | solution.py:155
  69.3 23.1 %collective-permute-start.13 = (bf16[128,4224]{1,0:T(8,128)(2,1)}, bf16[128,4224]{1,0:T(8,128)(2,1)}, u32[]{:S(2)}, u32[]{:S(2)}) collective-permute-start(bf16[128,4224]{1,0:T(8,128)(2,1)} %collective-permute-done.5.refs_7_), channel_id=1, source_target_pairs={{1,0},{0,1},{5,4},{4,5},{9,8},{8,9},{13,12},{12,13},{3,2},{2,3},{7... | collective-permute-start | bytes 3244040 | tf_op jit(solution)/shard_map/ppermute | solution.py:155
  86.0 9.7 %collective-permute-start.14 = (bf16[128,4224]{1,0:T(8,128)(2,1)}, bf16[128,4224]{1,0:T(8,128)(2,1)}, u32[]{:S(2)}, u32[]{:S(2)}) collective-permute-start(bf16[128,4224]{1,0:T(8,128)(2,1)} %collective-permute-done.6.refs_8_), channel_id=1, source_target_pairs={{1,0},{0,1},{5,4},{4,5},{9,8},{8,9},{13,12},{12,13},{3,2},{2,3},{7... | collective-permute-start | bytes 3244040 | tf_op jit(solution)/shard_map/ppermute | solution.py:155
  86.0 23.7 %collective-permute-start.26 = (bf16[128,4224]{1,0:T(8,128)(2,1)}, bf16[128,4224]{1,0:T(8,128)(2,1)}, u32[]{:S(2)}, u32[]{:S(2)}) collective-permute-start(bf16[128,4224]{1,0:T(8,128)(2,1)} %collective-permute-done.22.refs_1_), channel_id=1, source_target_pairs={{12,0},{5,1},{0,4},{9,5},{4,8},{13,9},{8,12},{1,13},{14,2},{7,3},{... | collective-permute-start | bytes 3244040 | tf_op jit(solution)/shard_map/ppermute | solution.py:64
  86.6 23.1 %collective-permute-start.15 = (bf16[128,4224]{1,0:T(8,128)(2,1)}, bf16[128,4224]{1,0:T(8,128)(2,1)}, u32[]{:S(2)}, u32[]{:S(2)}) collective-permute-start(bf16[128,4224]{1,0:T(8,128)(2,1)} %collective-permute-done.7.refs_9_), channel_id=1, source_target_pairs={{1,0},{0,1},{5,4},{4,5},{9,8},{8,9},{13,12},{12,13},{3,2},{2,3},{7... | collective-permute-start | bytes 3244040 | tf_op jit(solution)/shard_map/ppermute | solution.py:155
  91.6 40.8 %collective-permute-start.21 = (bf16[128,4224]{1,0:T(8,128)(2,1)}, bf16[128,4224]{1,0:T(8,128)(2,1)S(1)}, u32[]{:S(2)}, u32[]{:S(2)}) collective-permute-start(bf16[128,4224]{1,0:T(8,128)(2,1)} %copy-done.14), channel_id=1, source_target_pairs={{12,0},{5,1},{0,4},{9,5},{4,8},{13,9},{8,12},{1,13},{14,2},{7,3},{... | collective-permute-start | bytes 3244040 | tf_op jit(solution)/shard_map/ppermute | solution.py:64
  92.5 50.5 %collective-permute-start.17 = (bf16[128,4224]{1,0:T(8,128)(2,1)S(1)}, bf16[128,4224]{1,0:T(8,128)(2,1)S(1)}, u32[]{:S(2)}, u32[]{:S(2)}) collective-permute-start(bf16[128,4224]{1,0:T(8,128)(2,1)S(1)} %pad_maximum_fusion.refs_0_.refs_2_), channel_id=1, source_target_pairs={{4,0},{13,1},{8,4},{1,5},{12,8},{5,9},{0,12},{9,13},{6,2},{15,3},{... | collective-permute-start | bytes 3244040 | tf_op jit(solution)/shard_map/ppermute | solution.py:64
  117.1 15.2 %copy-start.10 = (bf16[128,4224]{1,0:T(8,128)(2,1)S(1)}, bf16[128,4224]{1,0:T(8,128)(2,1)}, u32[]{:S(2)}) copy-start(bf16[128,4224]{1,0:T(8,128)(2,1)} %copy-done.8) | copy-start | bytes 3244036
  117.1 15.2 %copy-start.13 = (bf16[128,4224]{1,0:T(8,128)(2,1)S(1)}, bf16[128,4224]{1,0:T(8,128)(2,1)}, u32[]{:S(2)}) copy-start(bf16[128,4224]{1,0:T(8,128)(2,1)} %copy-done.11) | copy-start | bytes 3244036
  125.6 36.0 %collective-permute-start.28 = (f32[1,128]{1,0:T(1,128)S(1)}, f32[1,128]{1,0:T(1,128)S(1)}, u32[]{:S(2)}, u32[]{:S(2)}) collective-permute-start(f32[1,128]{1,0:T(1,128)S(1)} %get-tuple-element.17), channel_id=1, source_target_pairs={{24,0},{25,1},{28,4},{29,5},{16,8},{17,9},{20,12},{21,13},{26,2},{... | collective-permute-start | bytes 1544 | tf_op jit(solution)/shard_map/ppermute | solution.py:64
  126.6 35.8 %collective-permute-start.27 = (f32[1,128]{1,0:T(1,128)S(1)}, f32[1,128]{1,0:T(1,128)S(1)}, u32[]{:S(2)}, u32[]{:S(2)}) collective-permute-start(f32[1,128]{1,0:T(1,128)S(1)} %get-tuple-element.16), channel_id=1, source_target_pairs={{28,0},{21,1},{16,4},{25,5},{20,8},{29,9},{24,12},{17,13},{30,2},{... | collective-permute-start | bytes 1544 | tf_op jit(solution)/shard_map/ppermute | solution.py:64
  140.8 25.6 %collective-permute-start.24 = (f32[1,128]{1,0:T(1,128)S(1)}, f32[1,128]{1,0:T(1,128)S(1)}, u32[]{:S(2)}, u32[]{:S(2)}) collective-permute-start(f32[1,128]{1,0:T(1,128)S(1)} %get-tuple-element.15), channel_id=1, source_target_pairs={{20,0},{29,1},{24,4},{17,5},{28,8},{21,9},{16,12},{25,13},{22,2},{... | collective-permute-start | bytes 1544 | tf_op jit(solution)/shard_map/ppermute | solution.py:64
  140.9 25.6 %collective-permute-start.23 = (f32[1,128]{1,0:T(1,128)S(1)}, f32[1,128]{1,0:T(1,128)S(1)}, u32[]{:S(2)}, u32[]{:S(2)}) collective-permute-start(f32[1,128]{1,0:T(1,128)S(1)} %get-tuple-element.14), channel_id=1, source_target_pairs={{8,0},{9,1},{12,4},{13,5},{0,8},{1,9},{4,12},{5,13},{10,2},{11,3},... | collective-permute-start | bytes 1544 | tf_op jit(solution)/shard_map/ppermute | solution.py:64
  151.2 15.3 %collective-permute-start.20 = (f32[1,128]{1,0:T(1,128)S(1)}, f32[1,128]{1,0:T(1,128)S(1)}, u32[]{:S(2)}, u32[]{:S(2)}) collective-permute-start(f32[1,128]{1,0:T(1,128)S(1)} %get-tuple-element.13), channel_id=1, source_target_pairs={{16,0},{17,1},{20,4},{21,5},{24,8},{25,9},{28,12},{29,13},{18,2},{... | collective-permute-start | bytes 1544 | tf_op jit(solution)/shard_map/ppermute | solution.py:64
  161.7 4.9 %collective-permute-start.19 = (f32[1,128]{1,0:T(1,128)S(1)}, f32[1,128]{1,0:T(1,128)S(1)}, u32[]{:S(2)}, u32[]{:S(2)}) collective-permute-start(f32[1,128]{1,0:T(1,128)S(1)} %get-tuple-element.12), channel_id=1, source_target_pairs={{12,0},{5,1},{0,4},{9,5},{4,8},{13,9},{8,12},{1,13},{14,2},{7,3},{... | collective-permute-start | bytes 1544 | tf_op jit(solution)/shard_map/ppermute | solution.py:64
  162.4 4.3 %collective-permute-start.16 = (f32[1,128]{1,0:T(1,128)S(1)}, f32[1,128]{1,0:T(1,128)S(1)}, u32[]{:S(2)}, u32[]{:S(2)}) collective-permute-start(f32[1,128]{1,0:T(1,128)S(1)} %slice.41), channel_id=1, source_target_pairs={{4,0},{13,1},{8,4},{1,5},{12,8},{5,9},{0,12},{9,13},{6,2},{15,3},{... | collective-permute-start | bytes 1544 | tf_op jit(solution)/shard_map/ppermute | solution.py:64
  (18 other events, 67.0 us)

commit v2 on v0

v2 whole, which is shorter than its diff:
```python
import jax
import jax.numpy as jnp
import numpy as np
from jax import lax
from jax.experimental import pallas as pl
from jax.experimental.pallas import tpu as pltpu
from jax.sharding import PartitionSpec as P

AXES = ("row", "col")
SIDE = 4
LANES = 128
WINDOW = 5

SLOTS = (
    (0, 0, 0), (0, 1, 0), (3, 0, 0), (0, 3, 0), (0, 1, 1), (1, 1, 0), (3, 0, 3),
    (3, 3, 0), (0, 2, 1), (2, 1, 0), (0, 1, 2), (3, 3, 3), (1, 2, 1),
)
PARENT = (None, 0, 0, 0, 1, 1, 2, 2, 4, 5, 4, 7, 8)
OWN = (
    (0, 0, True),
    (6, 0, False), (3, 1, True), (12, 1, False), (3, 2, False), (12, 2, False), (5, 3, False), (6, 3, False),
    (9, 3, True), (10, 3, True), (5, 4, False), (6, 4, False), (9, 4, False), (10, 4, False), (10, 5, False),
    (12, 5, False), (5, 6, False), (10, 6, False), (12, 6, True), (0, 7, False), (4, 7, False), (6, 7, False),
    (12, 7, False), (0, 8, False), (4, 8, False), (6, 8, False), (0, 9, False), (1, 9, True), (0, 10, False),
    (1, 10, True), (9, 10, True), (8, 11, False), (9, 11, False), (8, 12, False), (9, 12, False), (11, 12, False),
)
CROSS = (
    (3, 0, 0), (3, 0, 1), (8, 0, 0), (8, 0, 1), (9, 0, 0), (9, 0, 1), (2, 1, 0), (3, 1, 0), (3, 1, 1), (9, 1, 0),
    (2, 2, 0), (3, 2, 0), (3, 2, 1), (9, 2, 0), (9, 2, 1), (3, 3, 0), (8, 3, 0), (8, 3, 1), (9, 3, 0), (9, 3, 1),
    (3, 4, 0), (3, 4, 1), (8, 4, 0), (8, 4, 1), (9, 4, 0), (9, 4, 1), (1, 5, 0), (4, 5, 0), (4, 5, 1), (6, 5, 0),
    (8, 5, 1), (4, 6, 1), (6, 6, 1), (8, 6, 0), (1, 7, 0), (1, 7, 1), (2, 7, 0), (2, 7, 1), (3, 7, 0), (6, 7, 0),
    (6, 7, 1), (9, 7, 0), (9, 7, 1), (1, 8, 0), (2, 8, 0), (2, 8, 1), (9, 8, 0), (6, 9, 1), (6, 10, 0), (6, 10, 1),
    (3, 11, 0), (3, 11, 1), (4, 11, 1), (6, 11, 0), (6, 11, 1), (9, 11, 0), (9, 11, 1), (3, 12, 0), (3, 12, 1),
    (4, 12, 0), (4, 12, 1), (6, 12, 1), (8, 12, 0), (9, 12, 1),
)
LEAPS = ((0, 0, 0), (3, 0, 0), (3, 0, 3))
HOPS = ((0, 0, 0), (0, 3, 0), (1, 1, 0), (1, 1, 2), (1, 2, 1), (2, 1, 0))
N_SLOTS = len(SLOTS)
PAIRS = ((0,),) + tuple((i, i + 1) for i in range(1, N_SLOTS, 2))
OTHERS = tuple(sorted({j for j, _, _ in CROSS}))


def device_at(x, y, z, core):
    x, y, z, core = x % SIDE, y % SIDE, z % SIDE, core % 2
    return (x * 2 + y // 2) * 16 + z * 4 + (y % 2) * 2 + core


def places():
    for x in range(SIDE):
        for y in range(SIDE):
            for z in range(SIDE):
                for core in range(2):
                    yield x, y, z, core


def on_core(offset, core):
    x, y, z = offset
    return (-x, -z, -y) if core else offset


def plus(a, b):
    return tuple((i + j) % SIDE for i, j in zip(a, b))


def minus(a, b):
    return tuple((i - j) % SIDE for i, j in zip(a, b))


def shift(value, offset):
    pairs = []
    for x, y, z, core in places():
        a, b, c = on_core(offset, core)
        pairs.append((device_at(x + a, y + b, z + c, core), device_at(x, y, z, core)))
    return lax.ppermute(value, AXES, pairs)


def swap(value):
    pairs = [(device_at(x, y, z, 1 - c), device_at(x, y, z, c)) for x, y, z, c in places()]
    return lax.ppermute(value, AXES, pairs)


def held_blocks():
    table = np.zeros((2 * SIDE**3, 2 * N_SLOTS), np.int32)
    for x, y, z, core in places():
        for k, offset in enumerate(SLOTS):
            for other in range(2):
                fam = core ^ other
                a, b, c = on_core(offset, fam)
                at = device_at(x + a, y + b, z + c, fam)
                table[device_at(x, y, z, core), k + other * N_SLOTS] = at
    return table


def pair_weights():
    weights = np.zeros((2, 2, 2 * N_SLOTS, N_SLOTS), np.float32)
    for left, right, one in OWN:
        weights[:, 0, left, right] = 1
        weights[:, 1, left, right] = 0 if one else 1
    for left, right, core in CROSS:
        weights[core, :, N_SLOTS + left, right] = 1
    return weights


def stage_of(slot):
    return next(p for p, pair in enumerate(PAIRS) if slot in pair)


def work_list():
    met = {}
    for left, right, _ in OWN:
        met.setdefault((max(stage_of(left), stage_of(right)), stage_of(right)), set()).add(left)
    for left, right, _ in CROSS:
        key = (max(stage_of(left), stage_of(right)), stage_of(right))
        met.setdefault(key, set()).add(N_SLOTS + left)
    return [
        [(p, sorted(met[(s, p)])) for p in range(len(PAIRS)) if (s, p) in met]
        for s in range(len(PAIRS))
    ]


def add_pairs(work, blocks, sums, weights, feats):
    used = sorted({b for p, lefts in work for b in (*PAIRS[p], *lefts)})
    n_tiles = sum(len(PAIRS[p]) * len(lefts) for p, lefts in work)
    scale = 1.0 / feats**0.5

    def body(w_ref, in_ref, *refs):
        out = refs[-1]
        ref = dict(zip(used, refs))
        out[...] = in_ref[...]
        eye = lax.broadcasted_iota(jnp.int32, (LANES, LANES), 0) == lax.broadcasted_iota(
            jnp.int32, (LANES, LANES), 1
        )

        def coeff(slot):
            return ref[slot][:, feats:].astype(jnp.float32)

        def along(wide):
            return jnp.sum(jnp.where(eye, wide, 0.0), axis=0, keepdims=True)

        for p, lefts in work:
            right = [ref[r][:, :feats] for r in PAIRS[p]]
            right = right[0] if len(right) == 1 else jnp.concatenate(right, axis=0)
            right_coeff = [along(coeff(r)) for r in PAIRS[p]]
            for at in range(0, len(lefts), 2):
                some = lefts[at : at + 2]
                left = [ref[b][:, :feats] for b in some]
                left = left[0] if len(left) == 1 else jnp.concatenate(left, axis=0)
                inner = lax.dot_general(
                    left, right, (((1,), (1,)), ((), ())), preferred_element_type=jnp.float32
                )
                bent = jnp.tanh(inner * scale)
                for h, b in enumerate(some):
                    left_coeff = coeff(b)
                    back = jnp.zeros((LANES, LANES), jnp.float32)
                    for k, r in enumerate(PAIRS[p]):
                        part = bent[h * LANES : (h + 1) * LANES, k * LANES : (k + 1) * LANES]
                        got = jnp.sum(part * left_coeff, axis=0, keepdims=True)
                        out[r : r + 1, :] += w_ref[0, b, r] * got
                        back = back + part * (w_ref[1, b, r] * right_coeff[k])
                    wide = jnp.broadcast_to(jnp.sum(back, axis=1, keepdims=True), (LANES, LANES))
                    out[b : b + 1, :] += along(wide)

    return pl.pallas_call(
        body,
        out_shape=jax.ShapeDtypeStruct(sums.shape, jnp.float32),
        in_specs=[pl.BlockSpec(memory_space=pltpu.SMEM)]
        + [pl.BlockSpec(memory_space=pltpu.VMEM)] * (1 + len(used)),
        out_specs=pl.BlockSpec(memory_space=pltpu.VMEM),
        compiler_params=pltpu.CompilerParams(vmem_limit_bytes=24 * 2**20),
        cost_estimate=pl.CostEstimate(
            flops=2 * n_tiles * LANES * LANES * feats,
            bytes_accessed=2 * len(used) * LANES * feats,
            transcendentals=n_tiles * LANES * LANES,
        ),
    )(weights, sums, *[blocks[b] for b in used])


def on_device(grads, coeffs, band, steps):
    rows_here, feats = grads.shape
    width = band[0]
    me = lax.axis_index(AXES)
    held = lax.dynamic_index_in_dim(jnp.asarray(held_blocks()), me, 0, keepdims=False)
    hit = held[:, None] == jnp.arange(steps.shape[0], dtype=jnp.int32)[None, :]
    held_steps = jnp.sum(jnp.where(hit, steps[None, :], 0), axis=1)
    near = jnp.abs(held_steps[:, None] - held_steps[None, :N_SLOTS]) <= width
    table = pair_weights()
    weights = jnp.where(me % 2 == 0, table[0], table[1])
    weights = jnp.where(near[None], weights, 0.0)
    count = rows_here * jnp.sum((jnp.abs(steps - held_steps[0]) <= width).astype(jnp.int32))

    wide = jnp.broadcast_to(coeffs[:, None], (rows_here, LANES))
    blocks = {0: jnp.concatenate([grads, wide], axis=1)}
    sums = jnp.zeros((2 * N_SLOTS, LANES), jnp.float32)
    after = {}
    work = work_list()

    def held_back(value, *until):
        for u in until:
            value, _ = lax.optimization_barrier((value, u))
        return value

    def fetch(slot, *until):
        offset = minus(SLOTS[slot], SLOTS[PARENT[slot]])
        blocks[slot] = shift(held_back(blocks[PARENT[slot]], *until), offset)

    def turn(slot, *until):
        blocks[N_SLOTS + slot] = swap(held_back(blocks[slot], *until))

    for slot in range(1, N_SLOTS):
        until = [blocks[slot - WINDOW]] if slot > WINDOW else []
        for s, by in GATES:
            if by == slot:
                until.append(after[s])
        fetch(slot, *until)
        for late in SWAPS.get(slot, ()):
            turn(late)
        for s in KERNELS.get(slot, ()):
            sums = add_pairs(work[s], blocks, sums, weights, feats)
            after[s] = sums

    own = sums[:N_SLOTS] + swap(sums[N_SLOTS:])
    ways = {}
    for k, offset in enumerate(SLOTS):
        hop, leap = next(
            (h, l) for l in range(len(LEAPS)) for h in range(len(HOPS))
            if plus(HOPS[h], LEAPS[l]) == offset
        )
        ways.setdefault(leap, {})[hop] = k
    nothing = jnp.zeros((LANES,), jnp.float32)
    there = jnp.zeros((len(HOPS), LANES), jnp.float32)
    for leap, by_hop in ways.items():
        part = jnp.stack([own[by_hop[h]] if h in by_hop else nothing for h in range(len(HOPS))])
        there = there + (shift(part, minus((0, 0, 0), LEAPS[leap])) if leap else part)
    total = there[0:1]
    for h in range(1, len(HOPS)):
        total = total + shift(there[h : h + 1], minus((0, 0, 0), HOPS[h]))
    return total.reshape(-1) / jnp.sqrt(count.astype(jnp.float32))


KERNELS = {6: (0, 1), 9: (2, 3), 11: (4,), 12: (5, 6)}
GATES = ((1, 8), (2, 10), (3, 11), (3, 12))
SWAPS = {5: (2, 3, 1), 8: (4, 6), 10: (8,), 12: (9,)}


def solution(mesh):
    in_specs = (P(AXES, None), P(AXES), P(), P())
    out_specs = P(AXES)
    return jax.shard_map(
        on_device, mesh=mesh, in_specs=in_specs, out_specs=out_specs, check_vma=False
    )
```

time: 275 us -> 120 us (0.44)
  waiting for transfers between devices: 175 us -> 34.9 us
  blocking collectives: 54.2 us -> 0 us
  starting transfers between devices: 0.04 us -> 45.9 us
  Pallas kernels: 0 us -> 32.8 us
  matrix products: 24.2 us -> 0 us
  between operations: 15.3 us -> 1.5 us
    all_gather x2 -> x0, waiting for transfers between devices: 174 us -> none  [the longest x1 91.3 us: on_device(): lax.all_gather(grads, 'col', axis=0, tiled=True)]
    ppermute x0 -> x27, starting transfers between devices: none -> 45.9 us  [the longest x19 43 us: shift(): return lax.ppermute(value, AXES, pairs)]
    ppermute x0 -> x27, waiting for transfers between devices: none -> 34.9 us  [the longest x19 34.1 us: shift(): return lax.ppermute(value, AXES, pairs)]
    pallas_call x0 -> x7, Pallas kernels: none -> 32.8 us  [add_pairs(): pl.pallas_call(body, out_shape=jax.ShapeDtypeStruct(sums.shape, jnp.float...]
    unnamed x1 -> x0, blocking collectives: 30.6 us -> none
    dot_general x1 -> x0, matrix products: 24.2 us -> none  [on_device(): lax.dot_general(lax.all_gather(grads, 'col', axis=0, tiled=True), col_row...]
    all_gather x1 -> x0, blocking collectives: 23.6 us -> none  [on_device(): lax.all_gather(coeffs, 'row', axis=0, tiled=True)]
  transfers between devices with their start and end apart: 2 -> 27, of which waited for: 2 -> 9; matrix products, arithmetic and copies ran while one was open for 2% -> 1% of each run, Pallas kernels for 0% -> 21%
where the time goes in v2:
time: 120 us; the launch traced here: 119 us
  starting transfers between devices  45.9 us (38%)
  waiting for transfers between devices  34.9 us (29%)
  Pallas kernels  32.8 us (27%)
  other arithmetic  2.78 us (2%)
  local copies, waits for them, and re-layouts  1.55 us (1%)
  between operations  1.5 us (1%)
    ppermute x19, starting transfers between devices, shift(): return lax.ppermute(value, AXES, pairs)  43 us
    ppermute x19, waiting for transfers between devices, shift(): return lax.ppermute(value, AXES, pairs)  34.1 us
    pallas_call x7, Pallas kernels, add_pairs(): pl.pallas_call(body, out_shape=jax.ShapeDtypeStruct(sums.shape, jnp.float...  32.8 us
    ppermute x8, starting transfers between devices, swap(): return lax.ppermute(value, AXES, pairs)  2.93 us
  transfers between devices with their start and end apart: 27, of which 9 were waited for; matrix products, arithmetic and copies ran while one was open for 1% of the time, Pallas kernels for 21%

profile of v2, /device:TPU:0, one launch (start us, length us, event | category | flops | bytes accessed | tf_op | source)
XLA Modules:
  0.0 119.5 jit_solution(3694303774883030535)
XLA Ops:
  0.0 0.7 broadcast_in_dim.44
  0.8 1.3 %pad_maximum_fusion.refs_0_ = bf16[128,4224]{1,0:T(8,128)(2,1)S(1)} fusion(bf16[128,128]{1,0:T(8,128)(2,1)S(1)} %broadcast_in_dim.44, bf16[128,4096]{1,0:T(8,128)(2,1)} %param.7), kind=kLoop, calls=%fused_computation | loop fusion | flops 2162688 | bytes 2162688 | tf_op jit(solution)/shard_map/concatenate | solution.py:192
  2.1 3.2 %collective-permute-start = (bf16[128,4224]{1,0:T(8,128)(2,1)S(1)}, bf16[128,4224]{1,0:T(8,128)(2,1)}, u32[]{:S(2)}, u32[]{:S(2)}) collective-permute-start(bf16[128,4224]{1,0:T(8,128)(2,1)S(1)} %pad_maximum_fusion.refs_0_), channel_id=1, source_target_pairs={{2,0},{13,1},{6,4},{1,5},{10,8},{5,9},{14,12},{9,13},{16,2},{15,3}... | collective-permute-start | bytes 3244040 | tf_op jit(solution)/shard_map/ppermute | solution.py:74
  5.3 1.5 %collective-permute-start.1 = (bf16[128,4224]{1,0:T(8,128)(2,1)S(1)}, bf16[128,4224]{1,0:T(8,128)(2,1)}, u32[]{:S(2)}, u32[]{:S(2)}) collective-permute-start(bf16[128,4224]{1,0:T(8,128)(2,1)S(1)} %pad_maximum_fusion.refs_0_), channel_id=1, source_target_pairs={{96,0},{33,1},{100,4},{37,5},{104,8},{41,9},{108,12},{45,13},{98,2... | collective-permute-start | bytes 3244040 | tf_op jit(solution)/shard_map/ppermute | solution.py:74
  6.8 11.2 %collective-permute-done.refs_0_.refs_1_ = bf16[128,4224]{1,0:T(8,128)(2,1)} collective-permute-done((bf16[128,4224]{1,0:T(8,128)(2,1)S(1)}, bf16[128,4224]{1,0:T(8,128)(2,1)}, u32[]{:S(2)}, u32[]{:S(2)}) %collective-permute-start) | collective-permute-done | bytes 1081376 | tf_op jit(solution)/shard_map/ppermute | solution.py:74
  17.9 4.0 %collective-permute-start.4 = (bf16[128,4224]{1,0:T(8,128)(2,1)}, bf16[128,4224]{1,0:T(8,128)(2,1)S(1)}, u32[]{:S(2)}, u32[]{:S(2)}) collective-permute-start(bf16[128,4224]{1,0:T(8,128)(2,1)} %collective-permute-done.refs_0_.refs_1_), channel_id=1, source_target_pairs={{4,0},{19,1},{8,4},{23,5},{12,8},{27,9},{0,12},{31,13},{6,2},{1,3}... | collective-permute-start | bytes 3244040 | tf_op jit(solution)/shard_map/ppermute | solution.py:74
  22.0 2.8 %collective-permute-start.6 = (bf16[128,4224]{1,0:T(8,128)(2,1)}, bf16[128,4224]{1,0:T(8,128)(2,1)}, u32[]{:S(2)}, u32[]{:S(2)}) collective-permute-start(bf16[128,4224]{1,0:T(8,128)(2,1)} %collective-permute-done.refs_0_.refs_1_), channel_id=1, source_target_pairs={{32,0},{97,1},{36,4},{101,5},{40,8},{105,9},{44,12},{109,13},{34,2... | collective-permute-start | bytes 3244040 | tf_op jit(solution)/shard_map/ppermute | solution.py:74
  24.8 2.8 %collective-permute-start.7 = (bf16[128,4224]{1,0:T(8,128)(2,1)}, bf16[128,4224]{1,0:T(8,128)(2,1)}, u32[]{:S(2)}, u32[]{:S(2)}) collective-permute-start(bf16[128,4224]{1,0:T(8,128)(2,1)} %collective-permute-done.1.refs_1_.refs_2_), channel_id=1, source_target_pairs={{12,0},{3,1},{0,4},{7,5},{4,8},{11,9},{8,12},{15,13},{14,2},{17,3}... | collective-permute-start | bytes 3244040 | tf_op jit(solution)/shard_map/ppermute | solution.py:74
  27.5 7.4 %collective-permute-done.4.refs_4_.refs_2_ = bf16[128,4224]{1,0:T(8,128)(2,1)S(1)} collective-permute-done((bf16[128,4224]{1,0:T(8,128)(2,1)}, bf16[128,4224]{1,0:T(8,128)(2,1)S(1)}, u32[]{:S(2)}, u32[]{:S(2)}) %collective-permute-start.4) | collective-permute-done | bytes 1081376 | tf_op jit(solution)/shard_map/ppermute | solution.py:74
  36.6 1.6 %shard_map.73.in_ref = f32[26,128]{1,0:T(8,128)S(1)} custom-call(f32[2,26,13]{2,1,0:T(8,128)S(1)} %select_select_fusion.w_ref, f32[26,128]{1,0:T(8,128)S(1)} %broadcast_in_dim.43.in_ref, bf16[128,4224]{1,0:T(8,128)(2,1)S(1)} %pad_maximum_fusion.refs_0_), custom_call_target="tpu_custom_call" | custom-call | flops 134217728 | bytes 1048576 | tf_op jit(solution)/shard_map/pallas_call | solution.py:163
  38.2 2.8 %shard_map.74.in_ref = f32[26,128]{1,0:T(8,128)S(1)} custom-call(f32[2,26,13]{2,1,0:T(8,128)S(1)} %select_select_fusion.w_ref, f32[26,128]{1,0:T(8,128)S(1)} %shard_map.73.in_ref, bf16[128,4224]{1,0:T(8,128)(2,1)} %collective-permute-done.refs_0_.refs_1_, bf16[128,4224]{1,0:T(8,128)(2,1)} %collective-permute-done.1.refs_1_.refs_2_, ...), custom_call_target="tpu_custom_call" | custom-call | flops 268435456 | bytes 3145728 | tf_op jit(solution)/shard_map/pallas_call | solution.py:163
  41.0 3.9 %collective-permute-start.12 = (bf16[128,4224]{1,0:T(8,128)(2,1)S(1)}, bf16[128,4224]{1,0:T(8,128)(2,1)S(1)}, u32[]{:S(2)}, u32[]{:S(2)}) collective-permute-start(bf16[128,4224]{1,0:T(8,128)(2,1)S(1)} %collective-permute-done.4.refs_4_.refs_2_), channel_id=1, source_target_pairs={{2,0},{13,1},{6,4},{1,5},{10,8},{5,9},{14,12},{9,13},{16,2},{15,3}... | collective-permute-start | bytes 3244040 | tf_op jit(solution)/shard_map/ppermute | solution.py:74
  44.9 2.8 %collective-permute-start.14 = (bf16[128,4224]{1,0:T(8,128)(2,1)}, bf16[128,4224]{1,0:T(8,128)(2,1)S(1)}, u32[]{:S(2)}, u32[]{:S(2)}) collective-permute-start(bf16[128,4224]{1,0:T(8,128)(2,1)} %collective-permute-done.6.refs_3_.refs_5_.refs_2_), channel_id=1, source_target_pairs={{32,0},{97,1},{36,4},{101,5},{40,8},{105,9},{44,12},{109,13},{34,2... | collective-permute-start | bytes 3244040 | tf_op jit(solution)/shard_map/ppermute | solution.py:74
  48.2 9.3 %collective-permute-done.12.refs_6_.refs_8_.refs_5_ = bf16[128,4224]{1,0:T(8,128)(2,1)S(1)} collective-permute-done((bf16[128,4224]{1,0:T(8,128)(2,1)S(1)}, bf16[128,4224]{1,0:T(8,128)(2,1)S(1)}, u32[]{:S(2)}, u32[]{:S(2)}) %collective-permute-start.12) | collective-permute-done | bytes 1081376 | tf_op jit(solution)/shard_map/ppermute | solution.py:74
  57.8 3.6 %shard_map.75.in_ref = f32[26,128]{1,0:T(8,128)S(1)} custom-call(f32[2,26,13]{2,1,0:T(8,128)S(1)} %select_select_fusion.w_ref, f32[26,128]{1,0:T(8,128)S(1)} %shard_map.74.in_ref, bf16[128,4224]{1,0:T(8,128)(2,1)S(1)} %pad_maximum_fusion.refs_0_, bf16[128,4224]{1,0:T(8,128)(2,1)} %collective-permute-done.refs_0_.refs_1_, ...), custom_call_target="tpu_custom_call" | custom-call | flops 939524096 | bytes 6291456 | tf_op jit(solution)/shard_map/pallas_call | solution.py:163
  61.5 3.6 %collective-permute-start.15 = (bf16[128,4224]{1,0:T(8,128)(2,1)S(1)}, bf16[128,4224]{1,0:T(8,128)(2,1)S(1)}, u32[]{:S(2)}, u32[]{:S(2)}) collective-permute-start(bf16[128,4224]{1,0:T(8,128)(2,1)S(1)} %collective-permute-done.4.refs_4_.refs_2_), channel_id=1, source_target_pairs={{4,0},{19,1},{8,4},{23,5},{12,8},{27,9},{0,12},{31,13},{6,2},{1,3}... | collective-permute-start | bytes 3244040 | tf_op jit(solution)/shard_map/ppermute | solution.py:74
  65.1 4.1 %shard_map.76.in_ref = f32[26,128]{1,0:T(8,128)S(1)} custom-call(f32[2,26,13]{2,1,0:T(8,128)S(1)} %select_select_fusion.w_ref, f32[26,128]{1,0:T(8,128)S(1)} %shard_map.75.in_ref, bf16[128,4224]{1,0:T(8,128)(2,1)S(1)} %pad_maximum_fusion.refs_0_, bf16[128,4224]{1,0:T(8,128)(2,1)S(1)} %collective-permute-done.3.refs_3_.refs_1_, ...), custom_call_target="tpu_custom_call" | custom-call | flops 1744830464 | bytes 8388608 | tf_op jit(solution)/shard_map/pallas_call | solution.py:163
  69.3 3.0 %collective-permute-start.18 = (bf16[128,4224]{1,0:T(8,128)(2,1)S(1)}, bf16[128,4224]{1,0:T(8,128)(2,1)S(1)}, u32[]{:S(2)}, u32[]{:S(2)}) collective-permute-start(bf16[128,4224]{1,0:T(8,128)(2,1)S(1)} %collective-permute-done.12.refs_6_.refs_8_.refs_5_), channel_id=1, source_target_pairs={{32,0},{97,1},{36,4},{101,5},{40,8},{105,9},{44,12},{109,13},{34,2... | collective-permute-start | bytes 3244040 | tf_op jit(solution)/shard_map/ppermute | solution.py:74
  72.3 6.6 %shard_map.77.in_ref = f32[26,128]{1,0:T(8,128)S(1)} custom-call(f32[2,26,13]{2,1,0:T(8,128)S(1)} %select_select_fusion.w_ref, f32[26,128]{1,0:T(8,128)S(1)} %shard_map.76.in_ref, bf16[128,4224]{1,0:T(8,128)(2,1)S(1)} %pad_maximum_fusion.refs_0_, bf16[128,4224]{1,0:T(8,128)(2,1)S(1)} %collective-permute-done.3.refs_3_.refs_1_, ...), custom_call_target="tpu_custom_call" | custom-call | flops 2550136832 | bytes 12582912 | tf_op jit(solution)/shard_map/pallas_call | solution.py:163
  78.9 7.1 %shard_map.78.in_ref = f32[26,128]{1,0:T(8,128)S(1)} custom-call(f32[2,26,13]{2,1,0:T(8,128)S(1)} %select_select_fusion.w_ref, f32[26,128]{1,0:T(8,128)S(1)} %shard_map.77.in_ref, bf16[128,4224]{1,0:T(8,128)(2,1)S(1)} %pad_maximum_fusion.refs_0_, bf16[128,4224]{1,0:T(8,128)(2,1)} %collective-permute-done.refs_0_.refs_1_, ...), custom_call_target="tpu_custom_call" | custom-call | flops 2818572288 | bytes 13631488 | tf_op jit(solution)/shard_map/pallas_call | solution.py:163
  86.0 7.1 %shard_map.79 = f32[26,128]{1,0:T(8,128)S(1)} custom-call(f32[2,26,13]{2,1,0:T(8,128)S(1)} %select_select_fusion.w_ref, f32[26,128]{1,0:T(8,128)S(1)} %shard_map.78.in_ref, bf16[128,4224]{1,0:T(8,128)(2,1)} %collective-permute-done.refs_0_.refs_1_, bf16[128,4224]{1,0:T(8,128)(2,1)} %collective-permute-done.1.refs_1_.refs_2_, ...), custom_call_target="tpu_custom_call" | custom-call | flops 2952790016 | bytes 14680064 | tf_op jit(solution)/shard_map/pallas_call | solution.py:163
  93.1 2.2 %collective-permute-start.19 = (f32[13,128]{1,0:T(8,128)S(1)}, f32[13,128]{1,0:T(8,128)S(1)}, u32[]{:S(2)}, u32[]{:S(2)}) collective-permute-start(f32[13,128]{1,0:T(8,128)S(1)} %slice.93), channel_id=1, source_target_pairs={{1,0},{0,1},{5,4},{4,5},{9,8},{8,9},{13,12},{12,13},{3,2},{2,3},{7... | collective-permute-start | bytes 19976 | tf_op jit(solution)/shard_map/ppermute | solution.py:79
  95.3 0.8 collective-permute-done.19
  96.2 3.4 %collective-permute-start.21 = (f32[6,128]{1,0:T(8,128)S(1)}, f32[6,128]{1,0:T(8,128)S(1)}, u32[]{:S(2)}, u32[]{:S(2)}) collective-permute-start(f32[6,128]{1,0:T(8,128)S(1)} %stack.15), channel_id=1, source_target_pairs={{36,0},{115,1},{40,4},{119,5},{44,8},{123,9},{32,12},{127,13},{38,... | collective-permute-start | bytes 9224 | tf_op jit(solution)/shard_map/ppermute | solution.py:74
  100.1 0.8 collective-permute-done.21
  100.9 2.4 %collective-permute-done.20 = f32[6,128]{1,0:T(8,128)S(1)} collective-permute-done((f32[6,128]{1,0:T(8,128)S(1)}, f32[6,128]{1,0:T(8,128)S(1)}, u32[]{:S(2)}, u32[]{:S(2)}) %collective-permute-start.20) | collective-permute-done | bytes 3104 | tf_op jit(solution)/shard_map/ppermute | solution.py:74
  103.4 4.9 %collective-permute-start.25 = (f32[1,128]{1,0:T(1,128)S(1)}, f32[1,128]{1,0:T(1,128)S(1)}, u32[]{:S(2)}, u32[]{:S(2)}) collective-permute-start(f32[1,128]{1,0:T(1,128)S(1)} %get-tuple-element.42), channel_id=1, source_target_pairs={{124,0},{43,1},{112,4},{47,5},{116,8},{35,9},{120,12},{39,13},{126... | collective-permute-start | bytes 1544 | tf_op jit(solution)/shard_map/ppermute | solution.py:74
  108.2 1.3 %collective-permute-start.24 = (f32[1,128]{1,0:T(1,128)S(1)}, f32[1,128]{1,0:T(1,128)S(1)}, u32[]{:S(2)}, u32[]{:S(2)}) collective-permute-start(f32[1,128]{1,0:T(1,128)S(1)} %get-tuple-element.43), channel_id=1, source_target_pairs={{122,0},{53,1},{126,4},{57,5},{114,8},{61,9},{118,12},{49,13},{104... | collective-permute-start | bytes 1544 | tf_op jit(solution)/shard_map/ppermute | solution.py:74
  109.5 1.3 %collective-permute-start.23 = (f32[1,128]{1,0:T(1,128)S(1)}, f32[1,128]{1,0:T(1,128)S(1)}, u32[]{:S(2)}, u32[]{:S(2)}) collective-permute-start(f32[1,128]{1,0:T(1,128)S(1)} %get-tuple-element.44), channel_id=1, source_target_pairs={{114,0},{37,1},{118,4},{41,5},{122,8},{45,9},{126,12},{33,13},{96,... | collective-permute-start | bytes 1544 | tf_op jit(solution)/shard_map/ppermute | solution.py:74
  110.8 4.0 %collective-permute-start.22 = (f32[1,128]{1,0:T(1,128)S(1)}, f32[1,128]{1,0:T(1,128)S(1)}, u32[]{:S(2)}, u32[]{:S(2)}) collective-permute-start(f32[1,128]{1,0:T(1,128)S(1)} %get-tuple-element.40), channel_id=1, source_target_pairs={{2,0},{13,1},{6,4},{1,5},{10,8},{5,9},{14,12},{9,13},{16,2},{15,3}... | collective-permute-start | bytes 1544 | tf_op jit(solution)/shard_map/ppermute | solution.py:74
  116.1 1.4 %collective-permute-done.24 = f32[1,128]{1,0:T(1,128)S(1)} collective-permute-done((f32[1,128]{1,0:T(1,128)S(1)}, f32[1,128]{1,0:T(1,128)S(1)}, u32[]{:S(2)}, u32[]{:S(2)}) %collective-permute-start.24) | collective-permute-done | bytes 544 | tf_op jit(solution)/shard_map/ppermute | solution.py:74
  117.5 1.5 %collective-permute-done.23 = f32[1,128]{1,0:T(1,128)S(1)} collective-permute-done((f32[1,128]{1,0:T(1,128)S(1)}, f32[1,128]{1,0:T(1,128)S(1)}, u32[]{:S(2)}, u32[]{:S(2)}) %collective-permute-start.23) | collective-permute-done | bytes 544 | tf_op jit(solution)/shard_map/ppermute | solution.py:74
  (54 shorter events, 3.9 us)
Async XLA Ops:
  0.7 35.6 %copy-start.2 = (s32[128]{0:T(128)S(1)}, s32[128]{0:T(128)}, u32[]{:S(2)}) copy-start(s32[128]{0:T(128)} %param.10) | copy-start | bytes 1540
  0.8 35.8 %copy-start = (f32[2,26,13]{2,1,0:T(8,128)S(1)}, f32[2,26,13]{2,1,0:T(8,128)}, u32[]{:S(2)}) copy-start(f32[2,26,13]{2,1,0:T(8,128)} %constant.43.clone) | copy-start | bytes 8116
  0.8 35.8 %copy-start.1 = (f32[2,26,13]{2,1,0:T(8,128)S(1)}, f32[2,26,13]{2,1,0:T(8,128)}, u32[]{:S(2)}) copy-start(f32[2,26,13]{2,1,0:T(8,128)} %constant.44.clone) | copy-start | bytes 8116
  2.1 15.8 %collective-permute-start = (bf16[128,4224]{1,0:T(8,128)(2,1)S(1)}, bf16[128,4224]{1,0:T(8,128)(2,1)}, u32[]{:S(2)}, u32[]{:S(2)}) collective-permute-start(bf16[128,4224]{1,0:T(8,128)(2,1)S(1)} %pad_maximum_fusion.refs_0_), channel_id=1, source_target_pairs={{2,0},{13,1},{6,4},{1,5},{10,8},{5,9},{14,12},{9,13},{16,2},{15,3}... | collective-permute-start | bytes 3244040 | tf_op jit(solution)/shard_map/ppermute | solution.py:74
  5.3 16.7 %collective-permute-start.1 = (bf16[128,4224]{1,0:T(8,128)(2,1)S(1)}, bf16[128,4224]{1,0:T(8,128)(2,1)}, u32[]{:S(2)}, u32[]{:S(2)}) collective-permute-start(bf16[128,4224]{1,0:T(8,128)(2,1)S(1)} %pad_maximum_fusion.refs_0_), channel_id=1, source_target_pairs={{96,0},{33,1},{100,4},{37,5},{104,8},{41,9},{108,12},{45,13},{98,2... | collective-permute-start | bytes 3244040 | tf_op jit(solution)/shard_map/ppermute | solution.py:74
  6.8 18.0 %collective-permute-start.3 = (bf16[128,4224]{1,0:T(8,128)(2,1)S(1)}, bf16[128,4224]{1,0:T(8,128)(2,1)S(1)}, u32[]{:S(2)}, u32[]{:S(2)}) collective-permute-start(bf16[128,4224]{1,0:T(8,128)(2,1)S(1)} %pad_maximum_fusion.refs_0_), channel_id=1, source_target_pairs={{18,0},{5,1},{22,4},{9,5},{26,8},{13,9},{30,12},{1,13},{0,2},{7,3}... | collective-permute-start | bytes 3244040 | tf_op jit(solution)/shard_map/ppermute | solution.py:74
  17.9 17.0 %collective-permute-start.4 = (bf16[128,4224]{1,0:T(8,128)(2,1)}, bf16[128,4224]{1,0:T(8,128)(2,1)S(1)}, u32[]{:S(2)}, u32[]{:S(2)}) collective-permute-start(bf16[128,4224]{1,0:T(8,128)(2,1)} %collective-permute-done.refs_0_.refs_1_), channel_id=1, source_target_pairs={{4,0},{19,1},{8,4},{23,5},{12,8},{27,9},{0,12},{31,13},{6,2},{1,3}... | collective-permute-start | bytes 3244040 | tf_op jit(solution)/shard_map/ppermute | solution.py:74
  22.0 16.2 %collective-permute-start.2 = (bf16[128,4224]{1,0:T(8,128)(2,1)}, bf16[128,4224]{1,0:T(8,128)(2,1)}, u32[]{:S(2)}, u32[]{:S(2)}) collective-permute-start(bf16[128,4224]{1,0:T(8,128)(2,1)} %collective-permute-done.1.refs_1_.refs_2_), channel_id=1, source_target_pairs={{1,0},{0,1},{5,4},{4,5},{9,8},{8,9},{13,12},{12,13},{3,2},{2,3},{7... | collective-permute-start | bytes 3244040 | tf_op jit(solution)/shard_map/ppermute | solution.py:79
  22.0 22.9 %collective-permute-start.6 = (bf16[128,4224]{1,0:T(8,128)(2,1)}, bf16[128,4224]{1,0:T(8,128)(2,1)}, u32[]{:S(2)}, u32[]{:S(2)}) collective-permute-start(bf16[128,4224]{1,0:T(8,128)(2,1)} %collective-permute-done.refs_0_.refs_1_), channel_id=1, source_target_pairs={{32,0},{97,1},{36,4},{101,5},{40,8},{105,9},{44,12},{109,13},{34,2... | collective-permute-start | bytes 3244040 | tf_op jit(solution)/shard_map/ppermute | solution.py:74
  24.8 20.1 %collective-permute-start.5 = (bf16[128,4224]{1,0:T(8,128)(2,1)S(1)}, bf16[128,4224]{1,0:T(8,128)(2,1)}, u32[]{:S(2)}, u32[]{:S(2)}) collective-permute-start(bf16[128,4224]{1,0:T(8,128)(2,1)S(1)} %collective-permute-done.3.refs_3_.refs_1_), channel_id=1, source_target_pairs={{1,0},{0,1},{5,4},{4,5},{9,8},{8,9},{13,12},{12,13},{3,2},{2,3},{7... | collective-permute-start | bytes 3244040 | tf_op jit(solution)/shard_map/ppermute | solution.py:79
  24.8 23.0 %collective-permute-start.7 = (bf16[128,4224]{1,0:T(8,128)(2,1)}, bf16[128,4224]{1,0:T(8,128)(2,1)}, u32[]{:S(2)}, u32[]{:S(2)}) collective-permute-start(bf16[128,4224]{1,0:T(8,128)(2,1)} %collective-permute-done.1.refs_1_.refs_2_), channel_id=1, source_target_pairs={{12,0},{3,1},{0,4},{7,5},{4,8},{11,9},{8,12},{15,13},{14,2},{17,3}... | collective-permute-start | bytes 3244040 | tf_op jit(solution)/shard_map/ppermute | solution.py:74
  35.0 12.8 %collective-permute-start.8 = (bf16[128,4224]{1,0:T(8,128)(2,1)}, bf16[128,4224]{1,0:T(8,128)(2,1)}, u32[]{:S(2)}, u32[]{:S(2)}) collective-permute-start(bf16[128,4224]{1,0:T(8,128)(2,1)} %collective-permute-done.refs_0_.refs_1_), channel_id=1, source_target_pairs={{1,0},{0,1},{5,4},{4,5},{9,8},{8,9},{13,12},{12,13},{3,2},{2,3},{7... | collective-permute-start | bytes 3244040 | tf_op jit(solution)/shard_map/ppermute | solution.py:79
  41.0 16.5 %collective-permute-start.12 = (bf16[128,4224]{1,0:T(8,128)(2,1)S(1)}, bf16[128,4224]{1,0:T(8,128)(2,1)S(1)}, u32[]{:S(2)}, u32[]{:S(2)}) collective-permute-start(bf16[128,4224]{1,0:T(8,128)(2,1)S(1)} %collective-permute-done.4.refs_4_.refs_2_), channel_id=1, source_target_pairs={{2,0},{13,1},{6,4},{1,5},{10,8},{5,9},{14,12},{9,13},{16,2},{15,3}... | collective-permute-start | bytes 3244040 | tf_op jit(solution)/shard_map/ppermute | solution.py:74
  44.9 16.6 %collective-permute-start.11 = (bf16[128,4224]{1,0:T(8,128)(2,1)}, bf16[128,4224]{1,0:T(8,128)(2,1)S(1)}, u32[]{:S(2)}, u32[]{:S(2)}) collective-permute-start(bf16[128,4224]{1,0:T(8,128)(2,1)} %collective-permute-done.1.refs_1_.refs_2_), channel_id=1, source_target_pairs={{18,0},{5,1},{22,4},{9,5},{26,8},{13,9},{30,12},{1,13},{0,2},{7,3}... | collective-permute-start | bytes 3244040 | tf_op jit(solution)/shard_map/ppermute | solution.py:74
  44.9 20.2 %collective-permute-start.14 = (bf16[128,4224]{1,0:T(8,128)(2,1)}, bf16[128,4224]{1,0:T(8,128)(2,1)S(1)}, u32[]{:S(2)}, u32[]{:S(2)}) collective-permute-start(bf16[128,4224]{1,0:T(8,128)(2,1)} %collective-permute-done.6.refs_3_.refs_5_.refs_2_), channel_id=1, source_target_pairs={{32,0},{97,1},{36,4},{101,5},{40,8},{105,9},{44,12},{109,13},{34,2... | collective-permute-start | bytes 3244040 | tf_op jit(solution)/shard_map/ppermute | solution.py:74
  47.7 17.3 %collective-permute-start.9 = (bf16[128,4224]{1,0:T(8,128)(2,1)S(1)}, bf16[128,4224]{1,0:T(8,128)(2,1)S(1)}, u32[]{:S(2)}, u32[]{:S(2)}) collective-permute-start(bf16[128,4224]{1,0:T(8,128)(2,1)S(1)} %collective-permute-done.4.refs_4_.refs_2_), channel_id=1, source_target_pairs={{1,0},{0,1},{5,4},{4,5},{9,8},{8,9},{13,12},{12,13},{3,2},{2,3},{7... | collective-permute-start | bytes 3244040 | tf_op jit(solution)/shard_map/ppermute | solution.py:79
  47.7 17.3 %collective-permute-start.10 = (bf16[128,4224]{1,0:T(8,128)(2,1)}, bf16[128,4224]{1,0:T(8,128)(2,1)S(1)}, u32[]{:S(2)}, u32[]{:S(2)}) collective-permute-start(bf16[128,4224]{1,0:T(8,128)(2,1)} %collective-permute-done.7.refs_4_.refs_6_.refs_3_), channel_id=1, source_target_pairs={{1,0},{0,1},{5,4},{4,5},{9,8},{8,9},{13,12},{12,13},{3,2},{2,3},{7... | collective-permute-start | bytes 3244040 | tf_op jit(solution)/shard_map/ppermute | solution.py:79
  57.6 14.7 %collective-permute-start.13 = (bf16[128,4224]{1,0:T(8,128)(2,1)S(1)}, bf16[128,4224]{1,0:T(8,128)(2,1)S(1)}, u32[]{:S(2)}, u32[]{:S(2)}) collective-permute-start(bf16[128,4224]{1,0:T(8,128)(2,1)S(1)} %collective-permute-done.12.refs_6_.refs_8_.refs_5_), channel_id=1, source_target_pairs={{1,0},{0,1},{5,4},{4,5},{9,8},{8,9},{13,12},{12,13},{3,2},{2,3},{7... | collective-permute-start | bytes 3244040 | tf_op jit(solution)/shard_map/ppermute | solution.py:79
  61.5 17.4 %collective-permute-start.15 = (bf16[128,4224]{1,0:T(8,128)(2,1)S(1)}, bf16[128,4224]{1,0:T(8,128)(2,1)S(1)}, u32[]{:S(2)}, u32[]{:S(2)}) collective-permute-start(bf16[128,4224]{1,0:T(8,128)(2,1)S(1)} %collective-permute-done.4.refs_4_.refs_2_), channel_id=1, source_target_pairs={{4,0},{19,1},{8,4},{23,5},{12,8},{27,9},{0,12},{31,13},{6,2},{1,3}... | collective-permute-start | bytes 3244040 | tf_op jit(solution)/shard_map/ppermute | solution.py:74
  65.1 13.8 %collective-permute-start.16 = (bf16[128,4224]{1,0:T(8,128)(2,1)S(1)}, bf16[128,4224]{1,0:T(8,128)(2,1)S(1)}, u32[]{:S(2)}, u32[]{:S(2)}) collective-permute-start(bf16[128,4224]{1,0:T(8,128)(2,1)S(1)} %collective-permute-done.14.refs_9_.refs_6_), channel_id=1, source_target_pairs={{1,0},{0,1},{5,4},{4,5},{9,8},{8,9},{13,12},{12,13},{3,2},{2,3},{7... | collective-permute-start | bytes 3244040 | tf_op jit(solution)/shard_map/ppermute | solution.py:79
  69.2 16.8 %collective-permute-start.17 = (bf16[128,4224]{1,0:T(8,128)(2,1)S(1)}, bf16[128,4224]{1,0:T(8,128)(2,1)S(1)}, u32[]{:S(2)}, u32[]{:S(2)}) collective-permute-start(bf16[128,4224]{1,0:T(8,128)(2,1)S(1)} %collective-permute-done.11.refs_5_.refs_7_.refs_4_), channel_id=1, source_target_pairs={{12,0},{3,1},{0,4},{7,5},{4,8},{11,9},{8,12},{15,13},{14,2},{17,3}... | collective-permute-start | bytes 3244040 | tf_op jit(solution)/shard_map/ppermute | solution.py:74
  69.3 16.7 %collective-permute-start.18 = (bf16[128,4224]{1,0:T(8,128)(2,1)S(1)}, bf16[128,4224]{1,0:T(8,128)(2,1)S(1)}, u32[]{:S(2)}, u32[]{:S(2)}) collective-permute-start(bf16[128,4224]{1,0:T(8,128)(2,1)S(1)} %collective-permute-done.12.refs_6_.refs_8_.refs_5_), channel_id=1, source_target_pairs={{32,0},{97,1},{36,4},{101,5},{40,8},{105,9},{44,12},{109,13},{34,2... | collective-permute-start | bytes 3244040 | tf_op jit(solution)/shard_map/ppermute | solution.py:74
  93.1 3.0 %collective-permute-start.19 = (f32[13,128]{1,0:T(8,128)S(1)}, f32[13,128]{1,0:T(8,128)S(1)}, u32[]{:S(2)}, u32[]{:S(2)}) collective-permute-start(f32[13,128]{1,0:T(8,128)S(1)} %slice.93), channel_id=1, source_target_pairs={{1,0},{0,1},{5,4},{4,5},{9,8},{8,9},{13,12},{12,13},{3,2},{2,3},{7... | collective-permute-start | bytes 19976 | tf_op jit(solution)/shard_map/ppermute | solution.py:79
  96.2 4.7 %collective-permute-start.21 = (f32[6,128]{1,0:T(8,128)S(1)}, f32[6,128]{1,0:T(8,128)S(1)}, u32[]{:S(2)}, u32[]{:S(2)}) collective-permute-start(f32[6,128]{1,0:T(8,128)S(1)} %stack.15), channel_id=1, source_target_pairs={{36,0},{115,1},{40,4},{119,5},{44,8},{123,9},{32,12},{127,13},{38,... | collective-permute-start | bytes 9224 | tf_op jit(solution)/shard_map/ppermute | solution.py:74
  99.6 3.7 %collective-permute-start.20 = (f32[6,128]{1,0:T(8,128)S(1)}, f32[6,128]{1,0:T(8,128)S(1)}, u32[]{:S(2)}, u32[]{:S(2)}) collective-permute-start(f32[6,128]{1,0:T(8,128)S(1)} %stack.13), channel_id=1, source_target_pairs={{32,0},{97,1},{36,4},{101,5},{40,8},{105,9},{44,12},{109,13},{34,2... | collective-permute-start | bytes 9224 | tf_op jit(solution)/shard_map/ppermute | solution.py:74
  103.3 12.8 %collective-permute-start.26 = (f32[1,128]{1,0:T(1,128)S(1)}, f32[1,128]{1,0:T(1,128)S(1)}, u32[]{:S(2)}, u32[]{:S(2)}) collective-permute-start(f32[1,128]{1,0:T(1,128)S(1)} %get-tuple-element.41), channel_id=1, source_target_pairs={{82,0},{69,1},{86,4},{73,5},{90,8},{77,9},{94,12},{65,13},{64,2},{... | collective-permute-start | bytes 1544 | tf_op jit(solution)/shard_map/ppermute | solution.py:74
  103.4 12.7 %collective-permute-start.25 = (f32[1,128]{1,0:T(1,128)S(1)}, f32[1,128]{1,0:T(1,128)S(1)}, u32[]{:S(2)}, u32[]{:S(2)}) collective-permute-start(f32[1,128]{1,0:T(1,128)S(1)} %get-tuple-element.42), channel_id=1, source_target_pairs={{124,0},{43,1},{112,4},{47,5},{116,8},{35,9},{120,12},{39,13},{126... | collective-permute-start | bytes 1544 | tf_op jit(solution)/shard_map/ppermute | solution.py:74
  108.2 9.3 %collective-permute-start.24 = (f32[1,128]{1,0:T(1,128)S(1)}, f32[1,128]{1,0:T(1,128)S(1)}, u32[]{:S(2)}, u32[]{:S(2)}) collective-permute-start(f32[1,128]{1,0:T(1,128)S(1)} %get-tuple-element.43), channel_id=1, source_target_pairs={{122,0},{53,1},{126,4},{57,5},{114,8},{61,9},{118,12},{49,13},{104... | collective-permute-start | bytes 1544 | tf_op jit(solution)/shard_map/ppermute | solution.py:74
  109.5 9.5 %collective-permute-start.23 = (f32[1,128]{1,0:T(1,128)S(1)}, f32[1,128]{1,0:T(1,128)S(1)}, u32[]{:S(2)}, u32[]{:S(2)}) collective-permute-start(f32[1,128]{1,0:T(1,128)S(1)} %get-tuple-element.44), channel_id=1, source_target_pairs={{114,0},{37,1},{118,4},{41,5},{122,8},{45,9},{126,12},{33,13},{96,... | collective-permute-start | bytes 1544 | tf_op jit(solution)/shard_map/ppermute | solution.py:74
  110.8 8.2 %collective-permute-start.22 = (f32[1,128]{1,0:T(1,128)S(1)}, f32[1,128]{1,0:T(1,128)S(1)}, u32[]{:S(2)}, u32[]{:S(2)}) collective-permute-start(f32[1,128]{1,0:T(1,128)S(1)} %get-tuple-element.40), channel_id=1, source_target_pairs={{2,0},{13,1},{6,4},{1,5},{10,8},{5,9},{14,12},{9,13},{16,2},{15,3}... | collective-permute-start | bytes 1544 | tf_op jit(solution)/shard_map/ppermute | solution.py:74

commit v3 on v2

--- a/solution.py
+++ b/solution.py
@@ -9,34 +9,38 @@
 AXES = ("row", "col")
 SIDE = 4
 LANES = 128
-WINDOW = 5
 
 SLOTS = (
-    (0, 0, 0), (0, 1, 0), (3, 0, 0), (0, 3, 0), (0, 1, 1), (1, 1, 0), (3, 0, 3),
-    (3, 3, 0), (0, 2, 1), (2, 1, 0), (0, 1, 2), (3, 3, 3), (1, 2, 1),
+    (0, 0, 0),
+    (0, 1, 0), (3, 0, 0), (0, 3, 0),
+    (3, 0, 3), (1, 1, 0), (0, 1, 1),
+    (0, 2, 1), (2, 1, 0), (3, 3, 0),
+    (3, 3, 3), (1, 2, 1), (0, 1, 2),
 )
-PARENT = (None, 0, 0, 0, 1, 1, 2, 2, 4, 5, 4, 7, 8)
+PARENT = (None, 0, 0, 0, 2, 1, 1, 6, 5, 2, 9, 7, 6)
+ROUNDS = ((0,), (1, 2, 3), (4, 5, 6), (7, 8, 9), (10, 11, 12))
 OWN = (
-    (0, 0, True),
-    (6, 0, False), (3, 1, True), (12, 1, False), (3, 2, False), (12, 2, False), (5, 3, False), (6, 3, False),
-    (9, 3, True), (10, 3, True), (5, 4, False), (6, 4, False), (9, 4, False), (10, 4, False), (10, 5, False),
-    (12, 5, False), (5, 6, False), (10, 6, False), (12, 6, True), (0, 7, False), (4, 7, False), (6, 7, False),
-    (12, 7, False), (0, 8, False), (4, 8, False), (6, 8, False), (0, 9, False), (1, 9, True), (0, 10, False),
-    (1, 10, True), (9, 10, True), (8, 11, False), (9, 11, False), (8, 12, False), (9, 12, False), (11, 12, False),
+    (0, 0, True), (1, 0, False), (6, 0, False), (11, 0, False), (12, 0, False), (5, 1, False), (8, 1, True),
+    (11, 1, False), (12, 1, True), (5, 2, False), (8, 2, False), (11, 2, False), (12, 2, False), (1, 3, True),
+    (6, 3, False), (11, 3, False), (12, 3, True), (0, 4, False), (7, 4, False), (11, 4, True), (12, 4, False),
+    (0, 5, False), (4, 5, False), (7, 5, False), (12, 5, False), (5, 6, False), (8, 6, False), (10, 7, False),
+    (12, 7, False), (10, 8, False), (12, 8, True), (5, 9, True), (8, 9, False), (9, 10, False), (9, 11, False),
+    (10, 11, False),
 )
 CROSS = (
-    (3, 0, 0), (3, 0, 1), (8, 0, 0), (8, 0, 1), (9, 0, 0), (9, 0, 1), (2, 1, 0), (3, 1, 0), (3, 1, 1), (9, 1, 0),
-    (2, 2, 0), (3, 2, 0), (3, 2, 1), (9, 2, 0), (9, 2, 1), (3, 3, 0), (8, 3, 0), (8, 3, 1), (9, 3, 0), (9, 3, 1),
-    (3, 4, 0), (3, 4, 1), (8, 4, 0), (8, 4, 1), (9, 4, 0), (9, 4, 1), (1, 5, 0), (4, 5, 0), (4, 5, 1), (6, 5, 0),
-    (8, 5, 1), (4, 6, 1), (6, 6, 1), (8, 6, 0), (1, 7, 0), (1, 7, 1), (2, 7, 0), (2, 7, 1), (3, 7, 0), (6, 7, 0),
-    (6, 7, 1), (9, 7, 0), (9, 7, 1), (1, 8, 0), (2, 8, 0), (2, 8, 1), (9, 8, 0), (6, 9, 1), (6, 10, 0), (6, 10, 1),
-    (3, 11, 0), (3, 11, 1), (4, 11, 1), (6, 11, 0), (6, 11, 1), (9, 11, 0), (9, 11, 1), (3, 12, 0), (3, 12, 1),
-    (4, 12, 0), (4, 12, 1), (6, 12, 1), (8, 12, 0), (9, 12, 1),
+    (3, 0, 0), (3, 0, 1), (8, 0, 0), (8, 0, 1), (9, 0, 0), (9, 0, 1), (2, 1, 0), (2, 1, 1), (5, 1, 1),
+    (9, 1, 0), (9, 1, 1), (2, 2, 1), (5, 2, 0), (5, 2, 1), (9, 2, 0), (9, 2, 1), (3, 3, 1), (8, 3, 0),
+    (8, 3, 1), (9, 3, 1), (5, 4, 1), (8, 4, 0), (9, 4, 0), (9, 4, 1), (5, 5, 1), (6, 5, 0), (6, 5, 1),
+    (7, 5, 1), (8, 5, 1), (9, 5, 0), (9, 5, 1), (6, 6, 0), (7, 6, 0), (7, 6, 1), (8, 6, 0), (8, 6, 1),
+    (2, 7, 0), (2, 7, 1), (8, 7, 1), (2, 8, 0), (2, 8, 1), (8, 8, 0), (7, 9, 0), (7, 9, 1), (8, 9, 0),
+    (8, 9, 1), (2, 10, 0), (3, 10, 0), (3, 10, 1), (6, 10, 0), (8, 10, 0), (8, 10, 1), (9, 10, 0), (9, 10, 1),
+    (2, 11, 0), (2, 11, 1), (3, 11, 0), (3, 11, 1), (6, 11, 0), (6, 11, 1), (7, 11, 0), (8, 11, 0), (9, 11, 0),
+    (9, 11, 1),
 )
-LEAPS = ((0, 0, 0), (3, 0, 0), (3, 0, 3))
-HOPS = ((0, 0, 0), (0, 3, 0), (1, 1, 0), (1, 1, 2), (1, 2, 1), (2, 1, 0))
+LEAPS = ((0, 0, 0), (0, 2, 0), (0, 1, 1), (2, 2, 0), (3, 0, 3))
+HOPS = ((0, 0, 0), (0, 0, 1), (0, 3, 0), (1, 1, 0))
 N_SLOTS = len(SLOTS)
-PAIRS = ((0,),) + tuple((i, i + 1) for i in range(1, N_SLOTS, 2))
+PAIRS = ((0, 3), (1, 2), (4, 5), (6, 9), (7, 8), (10, 11), (12,))
 OTHERS = tuple(sorted({j for j, _, _ in CROSS}))
 
 
@@ -101,26 +105,29 @@
     return weights
 
 
-def stage_of(slot):
-    return next(p for p, pair in enumerate(PAIRS) if slot in pair)
-
-
 def work_list():
+    came = {slot: n for n, slots in enumerate(ROUNDS) for slot in slots}
     met = {}
     for left, right, _ in OWN:
-        met.setdefault((max(stage_of(left), stage_of(right)), stage_of(right)), set()).add(left)
+        met.setdefault((max(came[left], came[right]), right), set()).add(left)
     for left, right, _ in CROSS:
-        key = (max(stage_of(left), stage_of(right)), stage_of(right))
-        met.setdefault(key, set()).add(N_SLOTS + left)
-    return [
-        [(p, sorted(met[(s, p)])) for p in range(len(PAIRS)) if (s, p) in met]
-        for s in range(len(PAIRS))
-    ]
+        met.setdefault((max(came[left], came[right]), right), set()).add(N_SLOTS + left)
+    work = []
+    for n in range(len(ROUNDS)):
+        here = []
+        for pair in PAIRS:
+            lefts = set().union(*(met.get((n, r), set()) for r in pair))
+            rights = tuple(r for r in pair if came[r] <= n)
+            if lefts:
+                counted = {b: [r for r in rights if b in met.get((n, r), ())] for b in lefts}
+                here.append((rights, sorted(lefts), counted))
+        work.append(here)
+    return work
 
 
 def add_pairs(work, blocks, sums, weights, feats):
-    used = sorted({b for p, lefts in work for b in (*PAIRS[p], *lefts)})
-    n_tiles = sum(len(PAIRS[p]) * len(lefts) for p, lefts in work)
+    used = sorted({b for rights, lefts, _ in work for b in (*rights, *lefts)})
+    n_tiles = sum(len(rights) * len(lefts) for rights, lefts, _ in work)
     scale = 1.0 / feats**0.5
 
     def body(w_ref, in_ref, *refs):
@@ -137,10 +144,13 @@
         def along(wide):
             return jnp.sum(jnp.where(eye, wide, 0.0), axis=0, keepdims=True)
 
-        for p, lefts in work:
-            right = [ref[r][:, :feats] for r in PAIRS[p]]
+        def down(wide):
+            return jnp.sum(jnp.where(eye, wide, 0.0), axis=1, keepdims=True)
+
+        for rights, lefts, counted in work:
+            right = [ref[r][:, :feats] for r in rights]
             right = right[0] if len(right) == 1 else jnp.concatenate(right, axis=0)
-            right_coeff = [along(coeff(r)) for r in PAIRS[p]]
+            right_coeff = [coeff(r)[0:1, :] for r in rights]
             for at in range(0, len(lefts), 2):
                 some = lefts[at : at + 2]
                 left = [ref[b][:, :feats] for b in some]
@@ -150,9 +160,11 @@
                 )
                 bent = jnp.tanh(inner * scale)
                 for h, b in enumerate(some):
-                    left_coeff = coeff(b)
+                    left_coeff = down(coeff(b))
                     back = jnp.zeros((LANES, LANES), jnp.float32)
-                    for k, r in enumerate(PAIRS[p]):
+                    for k, r in enumerate(rights):
+                        if r not in counted[b]:
+                            continue
                         part = bent[h * LANES : (h + 1) * LANES, k * LANES : (k + 1) * LANES]
                         got = jnp.sum(part * left_coeff, axis=0, keepdims=True)
                         out[r : r + 1, :] += w_ref[0, b, r] * got
@@ -188,35 +200,33 @@
     weights = jnp.where(near[None], weights, 0.0)
     count = rows_here * jnp.sum((jnp.abs(steps - held_steps[0]) <= width).astype(jnp.int32))
 
-    wide = jnp.broadcast_to(coeffs[:, None], (rows_here, LANES))
+    divisor = jnp.sqrt(count.astype(jnp.float32))
+    weights, divisor = lax.optimization_barrier((weights, divisor))
+    wide = jnp.broadcast_to(coeffs[None, :], (LANES, rows_here))
     blocks = {0: jnp.concatenate([grads, wide], axis=1)}
     sums = jnp.zeros((2 * N_SLOTS, LANES), jnp.float32)
-    after = {}
     work = work_list()
 
-    def held_back(value, *until):
+    def held_back(value, until):
         for u in until:
             value, _ = lax.optimization_barrier((value, u))
         return value
 
-    def fetch(slot, *until):
-        offset = minus(SLOTS[slot], SLOTS[PARENT[slot]])
-        blocks[slot] = shift(held_back(blocks[PARENT[slot]], *until), offset)
-
-    def turn(slot, *until):
-        blocks[N_SLOTS + slot] = swap(held_back(blocks[slot], *until))
-
-    for slot in range(1, N_SLOTS):
-        until = [blocks[slot - WINDOW]] if slot > WINDOW else []
-        for s, by in GATES:
-            if by == slot:
-                until.append(after[s])
-        fetch(slot, *until)
-        for late in SWAPS.get(slot, ()):
-            turn(late)
-        for s in KERNELS.get(slot, ()):
-            sums = add_pairs(work[s], blocks, sums, weights, feats)
-            after[s] = sums
+    for n in range(1, len(ROUNDS)):
+        until = [blocks[slot] for slot in ROUNDS[n - 1]] if n > 1 else []
+        for at, slot in enumerate(ROUNDS[n]):
+            parent = PARENT[slot]
+            blocks[slot] = shift(
+                held_back(blocks[parent], until[at : at + 1]), minus(SLOTS[slot], SLOTS[parent])
+            )
+        if n == len(ROUNDS) - 1:
+            sums = add_pairs(work[0], blocks, held_back(sums, until), weights, feats)
+            until = until + [sums]
+        for slot in ROUNDS[n - 1] if n > 1 else ():
+            if slot in OTHERS:
+                blocks[N_SLOTS + slot] = swap(held_back(blocks[slot], until))
+    sums = add_pairs(sum(work[1:-1], []), blocks, sums, weights, feats)
+    sums = add_pairs(work[-1], blocks, sums, weights, feats)
 
     own = sums[:N_SLOTS] + swap(sums[N_SLOTS:])
     ways = {}
@@ -234,12 +244,7 @@
     total = there[0:1]
     for h in range(1, len(HOPS)):
         total = total + shift(there[h : h + 1], minus((0, 0, 0), HOPS[h]))
-    return total.reshape(-1) / jnp.sqrt(count.astype(jnp.float32))
-
-
-KERNELS = {6: (0, 1), 9: (2, 3), 11: (4,), 12: (5, 6)}
-GATES = ((1, 8), (2, 10), (3, 11), (3, 12))
-SWAPS = {5: (2, 3, 1), 8: (4, 6), 10: (8,), 12: (9,)}
+    return total.reshape(-1) / divisor
 
 
 def solution(mesh):

time: 120 us -> 112 us (0.933)
  waiting for transfers between devices: 34.9 us -> 50.9 us
  starting transfers between devices: 45.9 us -> 32.3 us
  Pallas kernels: 32.8 us -> 20.3 us
  local copies, waits for them, and re-layouts: 1.55 us -> 3.62 us
    ppermute x19, waiting for transfers between devices: 34.1 us -> 46.9 us  [shift(): return lax.ppermute(value, AXES, pairs)]
    pallas_call x7 -> x3, Pallas kernels: 32.8 us -> 20.3 us  [add_pairs(): pl.pallas_call(body, out_shape=jax.ShapeDtypeStruct(sums.shape, jnp.float...]
    ppermute x19, starting transfers between devices: 43 us -> 30.9 us  [shift(): return lax.ppermute(value, AXES, pairs)]
    ppermute x8, waiting for transfers between devices: 0.85 us -> 4.04 us  [swap(): return lax.ppermute(value, AXES, pairs)]
    unnamed x6 -> x14, local copies, waits for them, and re-layouts: 0.02 us -> 2.24 us
    ppermute x8, starting transfers between devices: 2.93 us -> 1.4 us  [swap(): return lax.ppermute(value, AXES, pairs)]
  transfers between devices with their start and end apart: 27 -> 27, of which waited for: 9 -> 16; matrix products, arithmetic and copies ran while one was open for 1% -> 1% of each run, Pallas kernels for 21% -> 11%
where the time goes in v3:
time: 112 us
  waiting for transfers between devices  50.9 us (45%)
  starting transfers between devices  32.3 us (29%)
  Pallas kernels  20.3 us (18%)
  local copies, waits for them, and re-layouts  3.62 us (3%)
  other arithmetic  2.93 us (3%)
  between operations  1.5 us (1%)
    ppermute x19, waiting for transfers between devices, shift(): return lax.ppermute(value, AXES, pairs)  46.9 us
    ppermute x19, starting transfers between devices, shift(): return lax.ppermute(value, AXES, pairs)  30.9 us
    pallas_call x3, Pallas kernels, add_pairs(): pl.pallas_call(body, out_shape=jax.ShapeDtypeStruct(sums.shape, jnp.float...  20.3 us
    ppermute x8, waiting for transfers between devices, swap(): return lax.ppermute(value, AXES, pairs)  4.04 us
  transfers between devices with their start and end apart: 27, of which 16 were waited for; matrix products, arithmetic and copies ran while one was open for 1% of the time, Pallas kernels for 11%

profile of v3, /device:TPU:0, one launch (start us, length us, event | category | flops | bytes accessed | tf_op | source)
XLA Modules:
  0.0 111.6 jit_solution(11404120547522858504)
XLA Ops:
  0.7 1.4 %pad_maximum_fusion.refs_0_ = bf16[128,4224]{1,0:T(8,128)(2,1)S(1)} fusion(bf16[128,4096]{1,0:T(8,128)(2,1)} %param.7, bf16[4224]{0:T(1024)(128)(2,1)S(1)} %pad.18.clone), kind=kLoop, calls=%fused_computation | loop fusion | flops 2162688 | bytes 2138368 | tf_op jit(solution)/shard_map/concatenate | solution.py:206
  2.1 1.6 %collective-permute-start.3 = (bf16[128,4224]{1,0:T(8,128)(2,1)S(1)}, bf16[128,4224]{1,0:T(8,128)(2,1)S(1)}, u32[]{:S(2)}, u32[]{:S(2)}) collective-permute-start(bf16[128,4224]{1,0:T(8,128)(2,1)S(1)} %pad_maximum_fusion.refs_0_), channel_id=1, source_target_pairs={{96,0},{33,1},{100,4},{37,5},{104,8},{41,9},{108,12},{45,13},{98,2... | collective-permute-start | bytes 3244040 | tf_op jit(solution)/shard_map/ppermute | solution.py:78
  3.8 3.0 %collective-permute-start = (bf16[128,4224]{1,0:T(8,128)(2,1)S(1)}, bf16[128,4224]{1,0:T(8,128)(2,1)S(1)}, u32[]{:S(2)}, u32[]{:S(2)}) collective-permute-start(bf16[128,4224]{1,0:T(8,128)(2,1)S(1)} %pad_maximum_fusion.refs_0_), channel_id=1, source_target_pairs={{2,0},{13,1},{6,4},{1,5},{10,8},{5,9},{14,12},{9,13},{16,2},{15,3}... | collective-permute-start | bytes 3244040 | tf_op jit(solution)/shard_map/ppermute | solution.py:78
  6.8 11.8 %collective-permute-done.3.refs_2_ = bf16[128,4224]{1,0:T(8,128)(2,1)S(1)} collective-permute-done((bf16[128,4224]{1,0:T(8,128)(2,1)S(1)}, bf16[128,4224]{1,0:T(8,128)(2,1)S(1)}, u32[]{:S(2)}, u32[]{:S(2)}) %collective-permute-start.3) | collective-permute-done | bytes 1081376 | tf_op jit(solution)/shard_map/ppermute | solution.py:78
  18.5 0.9 collective-permute-done.refs_1_
  19.4 1.9 %collective-permute-start.4 = (bf16[128,4224]{1,0:T(8,128)(2,1)S(1)}, bf16[128,4224]{1,0:T(8,128)(2,1)S(1)}, u32[]{:S(2)}, u32[]{:S(2)}) collective-permute-start(bf16[128,4224]{1,0:T(8,128)(2,1)S(1)} %collective-permute-done.3.refs_2_), channel_id=1, source_target_pairs={{12,0},{3,1},{0,4},{7,5},{4,8},{11,9},{8,12},{15,13},{14,2},{17,3}... | collective-permute-start | bytes 3244040 | tf_op jit(solution)/shard_map/ppermute | solution.py:78
  21.4 1.8 %collective-permute-done.1.refs_3_ = bf16[128,4224]{1,0:T(8,128)(2,1)S(1)} collective-permute-done((bf16[128,4224]{1,0:T(8,128)(2,1)S(1)}, bf16[128,4224]{1,0:T(8,128)(2,1)S(1)}, u32[]{:S(2)}, u32[]{:S(2)}) %collective-permute-start.1) | collective-permute-done | bytes 1081376 | tf_op jit(solution)/shard_map/ppermute | solution.py:78
  23.1 4.0 %collective-permute-start.2 = (bf16[128,4224]{1,0:T(8,128)(2,1)S(1)}, bf16[128,4224]{1,0:T(8,128)(2,1)}, u32[]{:S(2)}, u32[]{:S(2)}) collective-permute-start(bf16[128,4224]{1,0:T(8,128)(2,1)S(1)} %collective-permute-done.refs_1_), channel_id=1, source_target_pairs={{4,0},{19,1},{8,4},{23,5},{12,8},{27,9},{0,12},{31,13},{6,2},{1,3}... | collective-permute-start | bytes 3244040 | tf_op jit(solution)/shard_map/ppermute | solution.py:78
  27.2 1.7 %collective-permute-start.6 = (bf16[128,4224]{1,0:T(8,128)(2,1)S(1)}, bf16[128,4224]{1,0:T(8,128)(2,1)}, u32[]{:S(2)}, u32[]{:S(2)}) collective-permute-start(bf16[128,4224]{1,0:T(8,128)(2,1)S(1)} %collective-permute-done.refs_1_), channel_id=1, source_target_pairs={{32,0},{97,1},{36,4},{101,5},{40,8},{105,9},{44,12},{109,13},{34,2... | collective-permute-start | bytes 3244040 | tf_op jit(solution)/shard_map/ppermute | solution.py:78
  28.9 7.7 %collective-permute-done.4.refs_4_ = bf16[128,4224]{1,0:T(8,128)(2,1)S(1)} collective-permute-done((bf16[128,4224]{1,0:T(8,128)(2,1)S(1)}, bf16[128,4224]{1,0:T(8,128)(2,1)S(1)}, u32[]{:S(2)}, u32[]{:S(2)}) %collective-permute-start.4) | collective-permute-done | bytes 1081376 | tf_op jit(solution)/shard_map/ppermute | solution.py:78
  36.6 1.0 copy-done.2
  37.6 2.3 %collective-permute-done.2.refs_6_ = bf16[128,4224]{1,0:T(8,128)(2,1)} collective-permute-done((bf16[128,4224]{1,0:T(8,128)(2,1)S(1)}, bf16[128,4224]{1,0:T(8,128)(2,1)}, u32[]{:S(2)}, u32[]{:S(2)}) %collective-permute-start.2) | collective-permute-done | bytes 1081376 | tf_op jit(solution)/shard_map/ppermute | solution.py:78
  39.8 1.4 %collective-permute-start.5 = (bf16[128,4224]{1,0:T(8,128)(2,1)}, bf16[128,4224]{1,0:T(8,128)(2,1)}, u32[]{:S(2)}, u32[]{:S(2)}) collective-permute-start(bf16[128,4224]{1,0:T(8,128)(2,1)} %collective-permute-done.2.refs_6_), channel_id=1, source_target_pairs={{2,0},{13,1},{6,4},{1,5},{10,8},{5,9},{14,12},{9,13},{16,2},{15,3}... | collective-permute-start | bytes 3244040 | tf_op jit(solution)/shard_map/ppermute | solution.py:78
  41.3 1.1 %collective-permute-done.6.refs_5_ = bf16[128,4224]{1,0:T(8,128)(2,1)} collective-permute-done((bf16[128,4224]{1,0:T(8,128)(2,1)S(1)}, bf16[128,4224]{1,0:T(8,128)(2,1)}, u32[]{:S(2)}, u32[]{:S(2)}) %collective-permute-start.6) | collective-permute-done | bytes 1081376 | tf_op jit(solution)/shard_map/ppermute | solution.py:78
  42.4 3.0 %collective-permute-start.7 = (bf16[128,4224]{1,0:T(8,128)(2,1)}, bf16[128,4224]{1,0:T(8,128)(2,1)}, u32[]{:S(2)}, u32[]{:S(2)}) collective-permute-start(bf16[128,4224]{1,0:T(8,128)(2,1)} %collective-permute-done.6.refs_5_), channel_id=1, source_target_pairs={{32,0},{97,1},{36,4},{101,5},{40,8},{105,9},{44,12},{109,13},{34,2... | collective-permute-start | bytes 3244040 | tf_op jit(solution)/shard_map/ppermute | solution.py:78
  48.9 6.4 %collective-permute-done.5.refs_7_.refs_6_ = bf16[128,4224]{1,0:T(8,128)(2,1)} collective-permute-done((bf16[128,4224]{1,0:T(8,128)(2,1)}, bf16[128,4224]{1,0:T(8,128)(2,1)}, u32[]{:S(2)}, u32[]{:S(2)}) %collective-permute-start.5) | collective-permute-done | bytes 1081376 | tf_op jit(solution)/shard_map/ppermute | solution.py:78
  55.3 3.1 %collective-permute-done.7.refs_8_.refs_7_ = bf16[128,4224]{1,0:T(8,128)(2,1)} collective-permute-done((bf16[128,4224]{1,0:T(8,128)(2,1)}, bf16[128,4224]{1,0:T(8,128)(2,1)}, u32[]{:S(2)}, u32[]{:S(2)}) %collective-permute-start.7) | collective-permute-done | bytes 1081376 | tf_op jit(solution)/shard_map/ppermute | solution.py:78
  58.4 3.5 %collective-permute-done.8.refs_9_.refs_8_ = bf16[128,4224]{1,0:T(8,128)(2,1)} collective-permute-done((bf16[128,4224]{1,0:T(8,128)(2,1)S(1)}, bf16[128,4224]{1,0:T(8,128)(2,1)}, u32[]{:S(2)}, u32[]{:S(2)}) %collective-permute-start.8) | collective-permute-done | bytes 1081376 | tf_op jit(solution)/shard_map/ppermute | solution.py:78
  61.9 1.6 %shard_map.73.in_ref = f32[26,128]{1,0:T(8,128)S(1)} custom-call(f32[2,26,13]{2,1,0:T(8,128)S(1)} %select_select_fusion.w_ref, f32[26,128]{1,0:T(8,128)S(1)} %broadcast_in_dim.43.in_ref, bf16[128,4224]{1,0:T(8,128)(2,1)S(1)} %pad_maximum_fusion.refs_0_), custom_call_target="tpu_custom_call" | custom-call | flops 134217728 | bytes 1048576 | tf_op jit(solution)/shard_map/pallas_call | solution.py:175
  65.0 1.5 %collective-permute-done.15.refs_16_.refs_17_ = bf16[128,4224]{1,0:T(8,128)(2,1)S(1)} collective-permute-done((bf16[128,4224]{1,0:T(8,128)(2,1)}, bf16[128,4224]{1,0:T(8,128)(2,1)S(1)}, u32[]{:S(2)}, u32[]{:S(2)}) %collective-permute-start.15) | collective-permute-done | bytes 1081376 | tf_op jit(solution)/shard_map/ppermute | solution.py:83
  66.5 1.6 %collective-permute-start.18 = (bf16[128,4224]{1,0:T(8,128)(2,1)}, bf16[128,4224]{1,0:T(8,128)(2,1)S(1)}, u32[]{:S(2)}, u32[]{:S(2)}) collective-permute-start(bf16[128,4224]{1,0:T(8,128)(2,1)} %collective-permute-done.2.refs_6_), channel_id=1, source_target_pairs={{4,0},{19,1},{8,4},{23,5},{12,8},{27,9},{0,12},{31,13},{6,2},{1,3}... | collective-permute-start | bytes 3244040 | tf_op jit(solution)/shard_map/ppermute | solution.py:78
  68.0 1.5 %collective-permute-done.13.refs_14_.refs_15_ = bf16[128,4224]{1,0:T(8,128)(2,1)S(1)} collective-permute-done((bf16[128,4224]{1,0:T(8,128)(2,1)}, bf16[128,4224]{1,0:T(8,128)(2,1)S(1)}, u32[]{:S(2)}, u32[]{:S(2)}) %collective-permute-start.13) | collective-permute-done | bytes 1081376 | tf_op jit(solution)/shard_map/ppermute | solution.py:83
  69.6 1.2 %copy-done.3 = bf16[128,4224]{1,0:T(8,128)(2,1)S(1)} copy-done((bf16[128,4224]{1,0:T(8,128)(2,1)S(1)}, bf16[128,4224]{1,0:T(8,128)(2,1)}, u32[]{:S(2)}) %copy-start.3) | copy-done | bytes 1081368
  70.8 11.2 %shard_map.74.in_ref = f32[26,128]{1,0:T(8,128)S(1)} custom-call(f32[2,26,13]{2,1,0:T(8,128)S(1)} %select_select_fusion.w_ref, f32[26,128]{1,0:T(8,128)S(1)} %shard_map.73.in_ref, bf16[128,4224]{1,0:T(8,128)(2,1)S(1)} %pad_maximum_fusion.refs_0_, bf16[128,4224]{1,0:T(8,128)(2,1)S(1)} %collective-permute-done.refs_1_, ...), custom_call_target="tpu_custom_call" | custom-call | flops 6710886400 | bytes 17825792 | tf_op jit(solution)/shard_map/pallas_call | solution.py:175
  82.0 7.5 %shard_map.75 = f32[26,128]{1,0:T(8,128)S(1)} custom-call(f32[2,26,13]{2,1,0:T(8,128)S(1)} %select_select_fusion.w_ref, f32[26,128]{1,0:T(8,128)S(1)} %shard_map.74.in_ref, bf16[128,4224]{1,0:T(8,128)(2,1)S(1)} %pad_maximum_fusion.refs_0_, bf16[128,4224]{1,0:T(8,128)(2,1)S(1)} %collective-permute-done.refs_1_, ...), custom_call_target="tpu_custom_call" | custom-call | flops 4294967296 | bytes 18874368 | tf_op jit(solution)/shard_map/pallas_call | solution.py:175
  89.8 1.0 collective-permute-done.19
  91.0 2.8 %collective-permute-start.21 = (f32[4,128]{1,0:T(4,128)S(1)}, f32[4,128]{1,0:T(4,128)S(1)}, u32[]{:S(2)}, u32[]{:S(2)}) collective-permute-start(f32[4,128]{1,0:T(4,128)S(1)} %get-tuple-element.91), channel_id=1, source_target_pairs={{36,0},{115,1},{40,4},{119,5},{44,8},{123,9},{32,12},{127,13},{38,... | collective-permute-start | bytes 6152 | tf_op jit(solution)/shard_map/ppermute | solution.py:78
  93.8 5.7 %collective-permute-start.23 = (f32[4,128]{1,0:T(4,128)S(1)}, f32[4,128]{1,0:T(4,128)S(1)}, u32[]{:S(2)}, u32[]{:S(2)}) collective-permute-start(f32[4,128]{1,0:T(4,128)S(1)} %stack.21), channel_id=1, source_target_pairs={{80,0},{73,1},{84,4},{77,5},{88,8},{65,9},{92,12},{69,13},{82,2},{... | collective-permute-start | bytes 6152 | tf_op jit(solution)/shard_map/ppermute | solution.py:78
  99.5 1.2 %collective-permute-done.22 = f32[4,128]{1,0:T(4,128)S(1)} collective-permute-done((f32[4,128]{1,0:T(4,128)S(1)}, f32[4,128]{1,0:T(4,128)S(1)}, u32[]{:S(2)}, u32[]{:S(2)}) %collective-permute-start.22) | collective-permute-done | bytes 2080 | tf_op jit(solution)/shard_map/ppermute | solution.py:78
  101.5 2.7 %collective-permute-start.25 = (f32[1,128]{1,0:T(1,128)S(1)}, f32[1,128]{1,0:T(1,128)S(1)}, u32[]{:S(2)}, u32[]{:S(2)}) collective-permute-start(f32[1,128]{1,0:T(1,128)S(1)} %get-tuple-element.88), channel_id=1, source_target_pairs={{2,0},{13,1},{6,4},{1,5},{10,8},{5,9},{14,12},{9,13},{16,2},{15,3}... | collective-permute-start | bytes 1544 | tf_op jit(solution)/shard_map/ppermute | solution.py:78
  104.6 1.9 %collective-permute-done.24 = f32[1,128]{1,0:T(1,128)S(1)} collective-permute-done((f32[1,128]{1,0:T(1,128)S(1)}, f32[1,128]{1,0:T(1,128)S(1)}, u32[]{:S(2)}, u32[]{:S(2)}) %collective-permute-start.24) | collective-permute-done | bytes 544 | tf_op jit(solution)/shard_map/ppermute | solution.py:78
  106.4 4.7 %collective-permute-done.26 = f32[1,128]{1,0:T(1,128)S(1)} collective-permute-done((f32[1,128]{1,0:T(1,128)S(1)}, f32[1,128]{1,0:T(1,128)S(1)}, u32[]{:S(2)}, u32[]{:S(2)}) %collective-permute-start.26) | collective-permute-done | bytes 544 | tf_op jit(solution)/shard_map/ppermute | solution.py:78
  (57 shorter events, 6.4 us)
Async XLA Ops:
  0.7 45.9 %copy-start.6 = (s32[128]{0:T(128)S(1)}, s32[128]{0:T(128)}, u32[]{:S(2)}) copy-start(s32[128]{0:T(128)} %param.10) | copy-start | bytes 1540
  0.7 48.2 %copy-start.4 = (f32[2,26,13]{2,1,0:T(8,128)S(1)}, f32[2,26,13]{2,1,0:T(8,128)}, u32[]{:S(2)}) copy-start(f32[2,26,13]{2,1,0:T(8,128)} %constant.43.clone) | copy-start | bytes 8116
  0.7 48.2 %copy-start.5 = (f32[2,26,13]{2,1,0:T(8,128)S(1)}, f32[2,26,13]{2,1,0:T(8,128)}, u32[]{:S(2)}) copy-start(f32[2,26,13]{2,1,0:T(8,128)} %constant.44.clone) | copy-start | bytes 8116
  2.1 16.4 %collective-permute-start.3 = (bf16[128,4224]{1,0:T(8,128)(2,1)S(1)}, bf16[128,4224]{1,0:T(8,128)(2,1)S(1)}, u32[]{:S(2)}, u32[]{:S(2)}) collective-permute-start(bf16[128,4224]{1,0:T(8,128)(2,1)S(1)} %pad_maximum_fusion.refs_0_), channel_id=1, source_target_pairs={{96,0},{33,1},{100,4},{37,5},{104,8},{41,9},{108,12},{45,13},{98,2... | collective-permute-start | bytes 3244040 | tf_op jit(solution)/shard_map/ppermute | solution.py:78
  3.8 15.7 %collective-permute-start = (bf16[128,4224]{1,0:T(8,128)(2,1)S(1)}, bf16[128,4224]{1,0:T(8,128)(2,1)S(1)}, u32[]{:S(2)}, u32[]{:S(2)}) collective-permute-start(bf16[128,4224]{1,0:T(8,128)(2,1)S(1)} %pad_maximum_fusion.refs_0_), channel_id=1, source_target_pairs={{2,0},{13,1},{6,4},{1,5},{10,8},{5,9},{14,12},{9,13},{16,2},{15,3}... | collective-permute-start | bytes 3244040 | tf_op jit(solution)/shard_map/ppermute | solution.py:78
  6.8 16.4 %collective-permute-start.1 = (bf16[128,4224]{1,0:T(8,128)(2,1)S(1)}, bf16[128,4224]{1,0:T(8,128)(2,1)S(1)}, u32[]{:S(2)}, u32[]{:S(2)}) collective-permute-start(bf16[128,4224]{1,0:T(8,128)(2,1)S(1)} %pad_maximum_fusion.refs_0_), channel_id=1, source_target_pairs={{18,0},{5,1},{22,4},{9,5},{26,8},{13,9},{30,12},{1,13},{0,2},{7,3}... | collective-permute-start | bytes 3244040 | tf_op jit(solution)/shard_map/ppermute | solution.py:78
  19.4 17.2 %collective-permute-start.4 = (bf16[128,4224]{1,0:T(8,128)(2,1)S(1)}, bf16[128,4224]{1,0:T(8,128)(2,1)S(1)}, u32[]{:S(2)}, u32[]{:S(2)}) collective-permute-start(bf16[128,4224]{1,0:T(8,128)(2,1)S(1)} %collective-permute-done.3.refs_2_), channel_id=1, source_target_pairs={{12,0},{3,1},{0,4},{7,5},{4,8},{11,9},{8,12},{15,13},{14,2},{17,3}... | collective-permute-start | bytes 3244040 | tf_op jit(solution)/shard_map/ppermute | solution.py:78
  23.1 19.3 %copy-start = (bf16[128,4224]{1,0:T(8,128)(2,1)}, bf16[128,4224]{1,0:T(8,128)(2,1)S(1)}, u32[]{:S(2)}) copy-start(bf16[128,4224]{1,0:T(8,128)(2,1)S(1)} %collective-permute-done.1.refs_3_) | copy-start | bytes 3244036
  23.1 16.7 %collective-permute-start.2 = (bf16[128,4224]{1,0:T(8,128)(2,1)S(1)}, bf16[128,4224]{1,0:T(8,128)(2,1)}, u32[]{:S(2)}, u32[]{:S(2)}) collective-permute-start(bf16[128,4224]{1,0:T(8,128)(2,1)S(1)} %collective-permute-done.refs_1_), channel_id=1, source_target_pairs={{4,0},{19,1},{8,4},{23,5},{12,8},{27,9},{0,12},{31,13},{6,2},{1,3}... | collective-permute-start | bytes 3244040 | tf_op jit(solution)/shard_map/ppermute | solution.py:78
  27.2 15.3 %collective-permute-start.6 = (bf16[128,4224]{1,0:T(8,128)(2,1)S(1)}, bf16[128,4224]{1,0:T(8,128)(2,1)}, u32[]{:S(2)}, u32[]{:S(2)}) collective-permute-start(bf16[128,4224]{1,0:T(8,128)(2,1)S(1)} %collective-permute-done.refs_1_), channel_id=1, source_target_pairs={{32,0},{97,1},{36,4},{101,5},{40,8},{105,9},{44,12},{109,13},{34,2... | collective-permute-start | bytes 3244040 | tf_op jit(solution)/shard_map/ppermute | solution.py:78
  39.8 15.5 %collective-permute-start.5 = (bf16[128,4224]{1,0:T(8,128)(2,1)}, bf16[128,4224]{1,0:T(8,128)(2,1)}, u32[]{:S(2)}, u32[]{:S(2)}) collective-permute-start(bf16[128,4224]{1,0:T(8,128)(2,1)} %collective-permute-done.2.refs_6_), channel_id=1, source_target_pairs={{2,0},{13,1},{6,4},{1,5},{10,8},{5,9},{14,12},{9,13},{16,2},{15,3}... | collective-permute-start | bytes 3244040 | tf_op jit(solution)/shard_map/ppermute | solution.py:78
  42.4 15.9 %collective-permute-start.7 = (bf16[128,4224]{1,0:T(8,128)(2,1)}, bf16[128,4224]{1,0:T(8,128)(2,1)}, u32[]{:S(2)}, u32[]{:S(2)}) collective-permute-start(bf16[128,4224]{1,0:T(8,128)(2,1)} %collective-permute-done.6.refs_5_), channel_id=1, source_target_pairs={{32,0},{97,1},{36,4},{101,5},{40,8},{105,9},{44,12},{109,13},{34,2... | collective-permute-start | bytes 3244040 | tf_op jit(solution)/shard_map/ppermute | solution.py:78
  45.4 16.5 %collective-permute-start.8 = (bf16[128,4224]{1,0:T(8,128)(2,1)S(1)}, bf16[128,4224]{1,0:T(8,128)(2,1)}, u32[]{:S(2)}, u32[]{:S(2)}) collective-permute-start(bf16[128,4224]{1,0:T(8,128)(2,1)S(1)} %collective-permute-done.3.refs_2_), channel_id=1, source_target_pairs={{18,0},{5,1},{22,4},{9,5},{26,8},{13,9},{30,12},{1,13},{0,2},{7,3}... | collective-permute-start | bytes 3244040 | tf_op jit(solution)/shard_map/ppermute | solution.py:78
  46.1 17.5 %collective-permute-start.9 = (bf16[128,4224]{1,0:T(8,128)(2,1)S(1)}, bf16[128,4224]{1,0:T(8,128)(2,1)}, u32[]{:S(2)}, u32[]{:S(2)}) collective-permute-start(bf16[128,4224]{1,0:T(8,128)(2,1)S(1)} %collective-permute-done.3.refs_2_), channel_id=1, source_target_pairs={{1,0},{0,1},{5,4},{4,5},{9,8},{8,9},{13,12},{12,13},{3,2},{2,3},{7... | collective-permute-start | bytes 3244040 | tf_op jit(solution)/shard_map/ppermute | solution.py:83
  46.1 18.0 %collective-permute-start.10 = (bf16[128,4224]{1,0:T(8,128)(2,1)}, bf16[128,4224]{1,0:T(8,128)(2,1)}, u32[]{:S(2)}, u32[]{:S(2)}) collective-permute-start(bf16[128,4224]{1,0:T(8,128)(2,1)} %copy-done), channel_id=1, source_target_pairs={{1,0},{0,1},{5,4},{4,5},{9,8},{8,9},{13,12},{12,13},{3,2},{2,3},{7... | collective-permute-start | bytes 3244040 | tf_op jit(solution)/shard_map/ppermute | solution.py:83
  48.8 20.8 %copy-start.1 = (bf16[128,4224]{1,0:T(8,128)(2,1)S(1)}, bf16[128,4224]{1,0:T(8,128)(2,1)}, u32[]{:S(2)}) copy-start(bf16[128,4224]{1,0:T(8,128)(2,1)} %copy-done) | copy-start | bytes 3244036
  55.3 8.8 %collective-permute-start.12 = (bf16[128,4224]{1,0:T(8,128)(2,1)}, bf16[128,4224]{1,0:T(8,128)(2,1)S(1)}, u32[]{:S(2)}, u32[]{:S(2)}) collective-permute-start(bf16[128,4224]{1,0:T(8,128)(2,1)} %collective-permute-done.2.refs_6_), channel_id=1, source_target_pairs={{1,0},{0,1},{5,4},{4,5},{9,8},{8,9},{13,12},{12,13},{3,2},{2,3},{7... | collective-permute-start | bytes 3244040 | tf_op jit(solution)/shard_map/ppermute | solution.py:83
  58.4 5.8 %collective-permute-start.11 = (bf16[128,4224]{1,0:T(8,128)(2,1)}, bf16[128,4224]{1,0:T(8,128)(2,1)S(1)}, u32[]{:S(2)}, u32[]{:S(2)}) collective-permute-start(bf16[128,4224]{1,0:T(8,128)(2,1)} %collective-permute-done.6.refs_5_), channel_id=1, source_target_pairs={{1,0},{0,1},{5,4},{4,5},{9,8},{8,9},{13,12},{12,13},{3,2},{2,3},{7... | collective-permute-start | bytes 3244040 | tf_op jit(solution)/shard_map/ppermute | solution.py:83
  63.5 3.0 %collective-permute-start.15 = (bf16[128,4224]{1,0:T(8,128)(2,1)}, bf16[128,4224]{1,0:T(8,128)(2,1)S(1)}, u32[]{:S(2)}, u32[]{:S(2)}) collective-permute-start(bf16[128,4224]{1,0:T(8,128)(2,1)} %collective-permute-done.8.refs_9_.refs_8_), channel_id=1, source_target_pairs={{1,0},{0,1},{5,4},{4,5},{9,8},{8,9},{13,12},{12,13},{3,2},{2,3},{7... | collective-permute-start | bytes 3244040 | tf_op jit(solution)/shard_map/ppermute | solution.py:83
  63.6 4.5 %collective-permute-start.14 = (bf16[128,4224]{1,0:T(8,128)(2,1)}, bf16[128,4224]{1,0:T(8,128)(2,1)S(1)}, u32[]{:S(2)}, u32[]{:S(2)}) collective-permute-start(bf16[128,4224]{1,0:T(8,128)(2,1)} %collective-permute-done.7.refs_8_.refs_7_), channel_id=1, source_target_pairs={{1,0},{0,1},{5,4},{4,5},{9,8},{8,9},{13,12},{12,13},{3,2},{2,3},{7... | collective-permute-start | bytes 3244040 | tf_op jit(solution)/shard_map/ppermute | solution.py:83
  64.1 5.5 %collective-permute-start.13 = (bf16[128,4224]{1,0:T(8,128)(2,1)}, bf16[128,4224]{1,0:T(8,128)(2,1)S(1)}, u32[]{:S(2)}, u32[]{:S(2)}) collective-permute-start(bf16[128,4224]{1,0:T(8,128)(2,1)} %collective-permute-done.5.refs_7_.refs_6_), channel_id=1, source_target_pairs={{1,0},{0,1},{5,4},{4,5},{9,8},{8,9},{13,12},{12,13},{3,2},{2,3},{7... | collective-permute-start | bytes 3244040 | tf_op jit(solution)/shard_map/ppermute | solution.py:83
  64.2 17.8 %collective-permute-start.16 = (bf16[128,4224]{1,0:T(8,128)(2,1)}, bf16[128,4224]{1,0:T(8,128)(2,1)S(1)}, u32[]{:S(2)}, u32[]{:S(2)}) collective-permute-start(bf16[128,4224]{1,0:T(8,128)(2,1)} %collective-permute-done.8.refs_9_.refs_8_), channel_id=1, source_target_pairs={{12,0},{3,1},{0,4},{7,5},{4,8},{11,9},{8,12},{15,13},{14,2},{17,3}... | collective-permute-start | bytes 3244040 | tf_op jit(solution)/shard_map/ppermute | solution.py:78
  64.2 17.8 %collective-permute-start.17 = (bf16[128,4224]{1,0:T(8,128)(2,1)}, bf16[128,4224]{1,0:T(8,128)(2,1)S(1)}, u32[]{:S(2)}, u32[]{:S(2)}) collective-permute-start(bf16[128,4224]{1,0:T(8,128)(2,1)} %collective-permute-done.5.refs_7_.refs_6_), channel_id=1, source_target_pairs={{32,0},{97,1},{36,4},{101,5},{40,8},{105,9},{44,12},{109,13},{34,2... | collective-permute-start | bytes 3244040 | tf_op jit(solution)/shard_map/ppermute | solution.py:78
  66.5 15.5 %collective-permute-start.18 = (bf16[128,4224]{1,0:T(8,128)(2,1)}, bf16[128,4224]{1,0:T(8,128)(2,1)S(1)}, u32[]{:S(2)}, u32[]{:S(2)}) collective-permute-start(bf16[128,4224]{1,0:T(8,128)(2,1)} %collective-permute-done.2.refs_6_), channel_id=1, source_target_pairs={{4,0},{19,1},{8,4},{23,5},{12,8},{27,9},{0,12},{31,13},{6,2},{1,3}... | collective-permute-start | bytes 3244040 | tf_op jit(solution)/shard_map/ppermute | solution.py:78
  89.6 1.3 %collective-permute-start.19 = (f32[13,128]{1,0:T(8,128)S(1)}, f32[13,128]{1,0:T(8,128)S(1)}, u32[]{:S(2)}, u32[]{:S(2)}) collective-permute-start(f32[13,128]{1,0:T(8,128)S(1)} %slice.83), channel_id=1, source_target_pairs={{1,0},{0,1},{5,4},{4,5},{9,8},{8,9},{13,12},{12,13},{3,2},{2,3},{7... | collective-permute-start | bytes 19976 | tf_op jit(solution)/shard_map/ppermute | solution.py:83
  90.9 8.6 %collective-permute-start.20 = (f32[4,128]{1,0:T(4,128)S(1)}, f32[4,128]{1,0:T(4,128)S(1)}, u32[]{:S(2)}, u32[]{:S(2)}) collective-permute-start(f32[4,128]{1,0:T(4,128)S(1)} %get-tuple-element.89), channel_id=1, source_target_pairs={{16,0},{9,1},{20,4},{13,5},{24,8},{1,9},{28,12},{5,13},{18,2},{11,... | collective-permute-start | bytes 6152 | tf_op jit(solution)/shard_map/ppermute | solution.py:78
  91.0 8.5 %collective-permute-start.21 = (f32[4,128]{1,0:T(4,128)S(1)}, f32[4,128]{1,0:T(4,128)S(1)}, u32[]{:S(2)}, u32[]{:S(2)}) collective-permute-start(f32[4,128]{1,0:T(4,128)S(1)} %get-tuple-element.91), channel_id=1, source_target_pairs={{36,0},{115,1},{40,4},{119,5},{44,8},{123,9},{32,12},{127,13},{38,... | collective-permute-start | bytes 6152 | tf_op jit(solution)/shard_map/ppermute | solution.py:78
  93.8 6.9 %collective-permute-start.22 = (f32[4,128]{1,0:T(4,128)S(1)}, f32[4,128]{1,0:T(4,128)S(1)}, u32[]{:S(2)}, u32[]{:S(2)}) collective-permute-start(f32[4,128]{1,0:T(4,128)S(1)} %get-tuple-element.90), channel_id=1, source_target_pairs={{30,0},{7,1},{18,4},{11,5},{22,8},{15,9},{26,12},{3,13},{12,2},{21... | collective-permute-start | bytes 6152 | tf_op jit(solution)/shard_map/ppermute | solution.py:78
  93.8 7.6 %collective-permute-start.23 = (f32[4,128]{1,0:T(4,128)S(1)}, f32[4,128]{1,0:T(4,128)S(1)}, u32[]{:S(2)}, u32[]{:S(2)}) collective-permute-start(f32[4,128]{1,0:T(4,128)S(1)} %stack.21), channel_id=1, source_target_pairs={{80,0},{73,1},{84,4},{77,5},{88,8},{65,9},{92,12},{69,13},{82,2},{... | collective-permute-start | bytes 6152 | tf_op jit(solution)/shard_map/ppermute | solution.py:78
  101.4 5.0 %collective-permute-start.24 = (f32[1,128]{1,0:T(1,128)S(1)}, f32[1,128]{1,0:T(1,128)S(1)}, u32[]{:S(2)}, u32[]{:S(2)}) collective-permute-start(f32[1,128]{1,0:T(1,128)S(1)} %get-tuple-element.86), channel_id=1, source_target_pairs={{12,0},{3,1},{0,4},{7,5},{4,8},{11,9},{8,12},{15,13},{14,2},{17,3}... | collective-permute-start | bytes 1544 | tf_op jit(solution)/shard_map/ppermute | solution.py:78
  101.5 4.9 %collective-permute-start.25 = (f32[1,128]{1,0:T(1,128)S(1)}, f32[1,128]{1,0:T(1,128)S(1)}, u32[]{:S(2)}, u32[]{:S(2)}) collective-permute-start(f32[1,128]{1,0:T(1,128)S(1)} %get-tuple-element.88), channel_id=1, source_target_pairs={{2,0},{13,1},{6,4},{1,5},{10,8},{5,9},{14,12},{9,13},{16,2},{15,3}... | collective-permute-start | bytes 1544 | tf_op jit(solution)/shard_map/ppermute | solution.py:78
  104.2 6.9 %collective-permute-start.26 = (f32[1,128]{1,0:T(1,128)S(1)}, f32[1,128]{1,0:T(1,128)S(1)}, u32[]{:S(2)}, u32[]{:S(2)}) collective-permute-start(f32[1,128]{1,0:T(1,128)S(1)} %get-tuple-element.87), channel_id=1, source_target_pairs={{114,0},{37,1},{118,4},{41,5},{122,8},{45,9},{126,12},{33,13},{96,... | collective-permute-start | bytes 1544 | tf_op jit(solution)/shard_map/ppermute | solution.py:78
  (2 other events, 2.2 us)

commit v4 on v3

--- a/solution.py
+++ b/solution.py
@@ -37,8 +37,6 @@
     (2, 11, 0), (2, 11, 1), (3, 11, 0), (3, 11, 1), (6, 11, 0), (6, 11, 1), (7, 11, 0), (8, 11, 0), (9, 11, 0),
     (9, 11, 1),
 )
-LEAPS = ((0, 0, 0), (0, 2, 0), (0, 1, 1), (2, 2, 0), (3, 0, 3))
-HOPS = ((0, 0, 0), (0, 0, 1), (0, 3, 0), (1, 1, 0))
 N_SLOTS = len(SLOTS)
 PAIRS = ((0, 3), (1, 2), (4, 5), (6, 9), (7, 8), (10, 11), (12,))
 OTHERS = tuple(sorted({j for j, _, _ in CROSS}))
@@ -228,22 +226,9 @@
     sums = add_pairs(sum(work[1:-1], []), blocks, sums, weights, feats)
     sums = add_pairs(work[-1], blocks, sums, weights, feats)
 
-    own = sums[:N_SLOTS] + swap(sums[N_SLOTS:])
-    ways = {}
-    for k, offset in enumerate(SLOTS):
-        hop, leap = next(
-            (h, l) for l in range(len(LEAPS)) for h in range(len(HOPS))
-            if plus(HOPS[h], LEAPS[l]) == offset
-        )
-        ways.setdefault(leap, {})[hop] = k
-    nothing = jnp.zeros((LANES,), jnp.float32)
-    there = jnp.zeros((len(HOPS), LANES), jnp.float32)
-    for leap, by_hop in ways.items():
-        part = jnp.stack([own[by_hop[h]] if h in by_hop else nothing for h in range(len(HOPS))])
-        there = there + (shift(part, minus((0, 0, 0), LEAPS[leap])) if leap else part)
-    total = there[0:1]
-    for h in range(1, len(HOPS)):
-        total = total + shift(there[h : h + 1], minus((0, 0, 0), HOPS[h]))
+    home = held[None, :] == jnp.arange(2 * SIDE**3, dtype=jnp.int32)[:, None]
+    parts = jnp.sum(jnp.where(home[:, :, None], sums[None], 0.0), axis=1)
+    total = jnp.sum(lax.all_to_all(parts, AXES, 0, 0, tiled=True), axis=0)
     return total.reshape(-1) / divisor
 
 

time: 112 us -> 106 us (0.946)
  blocking collectives: 0 us -> 14.5 us
  starting transfers between devices: 32.3 us -> 20.4 us
  waiting for transfers between devices: 50.9 us -> 41.3 us
    all_to_all x0 -> x1, blocking collectives: none -> 14.5 us  [on_device(): total = jnp.sum(lax.all_to_all(parts, AXES, 0, 0, tiled=True), axis=0)]
    ppermute x19 -> x12, starting transfers between devices: 30.9 us -> 19.2 us  [shift(): return lax.ppermute(value, AXES, pairs)]
    ppermute x19 -> x12, waiting for transfers between devices: 46.9 us -> 38.4 us  [shift(): return lax.ppermute(value, AXES, pairs)]
    ppermute x8 -> x7, waiting for transfers between devices: 4.04 us -> 2.92 us  [swap(): return lax.ppermute(value, AXES, pairs)]
  transfers between devices with their start and end apart: 27 -> 19, of which waited for: 16 -> 11; matrix products, arithmetic and copies ran while one was open for 1% -> 2% of each run, Pallas kernels for 11% -> 12%
where the time goes in v4:
time: 106 us; the launch traced here: 105 us
  waiting for transfers between devices  41.3 us (39%)
  starting transfers between devices  20.4 us (19%)
  Pallas kernels  20.3 us (19%)
  blocking collectives  14.5 us (14%)
  other arithmetic  3.79 us (4%)
  local copies, waits for them, and re-layouts  3.66 us (3%)
  between operations  1.41 us (1%)
    ppermute x12, waiting for transfers between devices, shift(): return lax.ppermute(value, AXES, pairs)  38.4 us
    pallas_call x3, Pallas kernels, add_pairs(): pl.pallas_call(body, out_shape=jax.ShapeDtypeStruct(sums.shape, jnp.float...  20.3 us
    ppermute x12, starting transfers between devices, shift(): return lax.ppermute(value, AXES, pairs)  19.2 us
    all_to_all x1, blocking collectives, on_device(): total = jnp.sum(lax.all_to_all(parts, AXES, 0, 0, tiled=True), axis=0)  14.5 us
    ppermute x7, waiting for transfers between devices, swap(): return lax.ppermute(value, AXES, pairs)  2.92 us
    unnamed x14, local copies, waits for them, and re-layouts  2.3 us
  transfers between devices with their start and end apart: 19, of which 11 were waited for; matrix products, arithmetic and copies ran while one was open for 2% of the time, Pallas kernels for 12%

profile of v4, /device:TPU:0, one launch (start us, length us, event | category | flops | bytes accessed | tf_op | source)
XLA Modules:
  0.0 105.4 jit_solution(15904810112122484722)
XLA Ops:
  0.0 0.7 pad.1.clone
  0.7 1.4 %pad_maximum_fusion.refs_0_ = bf16[128,4224]{1,0:T(8,128)(2,1)S(1)} fusion(bf16[128,4096]{1,0:T(8,128)(2,1)} %param.7, bf16[4224]{0:T(1024)(128)(2,1)S(1)} %pad.1.clone), kind=kLoop, calls=%fused_computation.1 | loop fusion | flops 2162688 | bytes 2138368 | tf_op jit(solution)/shard_map/concatenate | solution.py:204
  2.1 1.6 %collective-permute-start.3 = (bf16[128,4224]{1,0:T(8,128)(2,1)S(1)}, bf16[128,4224]{1,0:T(8,128)(2,1)S(1)}, u32[]{:S(2)}, u32[]{:S(2)}) collective-permute-start(bf16[128,4224]{1,0:T(8,128)(2,1)S(1)} %pad_maximum_fusion.refs_0_), channel_id=1, source_target_pairs={{96,0},{33,1},{100,4},{37,5},{104,8},{41,9},{108,12},{45,13},{98,2... | collective-permute-start | bytes 3244040 | tf_op jit(solution)/shard_map/ppermute | solution.py:76
  3.8 3.0 %collective-permute-start = (bf16[128,4224]{1,0:T(8,128)(2,1)S(1)}, bf16[128,4224]{1,0:T(8,128)(2,1)S(1)}, u32[]{:S(2)}, u32[]{:S(2)}) collective-permute-start(bf16[128,4224]{1,0:T(8,128)(2,1)S(1)} %pad_maximum_fusion.refs_0_), channel_id=1, source_target_pairs={{2,0},{13,1},{6,4},{1,5},{10,8},{5,9},{14,12},{9,13},{16,2},{15,3}... | collective-permute-start | bytes 3244040 | tf_op jit(solution)/shard_map/ppermute | solution.py:76
  6.8 11.8 %collective-permute-done.3.refs_2_ = bf16[128,4224]{1,0:T(8,128)(2,1)S(1)} collective-permute-done((bf16[128,4224]{1,0:T(8,128)(2,1)S(1)}, bf16[128,4224]{1,0:T(8,128)(2,1)S(1)}, u32[]{:S(2)}, u32[]{:S(2)}) %collective-permute-start.3) | collective-permute-done | bytes 1081376 | tf_op jit(solution)/shard_map/ppermute | solution.py:76
  18.5 0.9 collective-permute-done.refs_1_
  19.4 1.9 %collective-permute-start.4 = (bf16[128,4224]{1,0:T(8,128)(2,1)S(1)}, bf16[128,4224]{1,0:T(8,128)(2,1)S(1)}, u32[]{:S(2)}, u32[]{:S(2)}) collective-permute-start(bf16[128,4224]{1,0:T(8,128)(2,1)S(1)} %collective-permute-done.3.refs_2_), channel_id=1, source_target_pairs={{12,0},{3,1},{0,4},{7,5},{4,8},{11,9},{8,12},{15,13},{14,2},{17,3}... | collective-permute-start | bytes 3244040 | tf_op jit(solution)/shard_map/ppermute | solution.py:76
  21.4 1.8 %collective-permute-done.1.refs_3_ = bf16[128,4224]{1,0:T(8,128)(2,1)S(1)} collective-permute-done((bf16[128,4224]{1,0:T(8,128)(2,1)S(1)}, bf16[128,4224]{1,0:T(8,128)(2,1)S(1)}, u32[]{:S(2)}, u32[]{:S(2)}) %collective-permute-start.1) | collective-permute-done | bytes 1081376 | tf_op jit(solution)/shard_map/ppermute | solution.py:76
  23.1 4.0 %collective-permute-start.2 = (bf16[128,4224]{1,0:T(8,128)(2,1)S(1)}, bf16[128,4224]{1,0:T(8,128)(2,1)}, u32[]{:S(2)}, u32[]{:S(2)}) collective-permute-start(bf16[128,4224]{1,0:T(8,128)(2,1)S(1)} %collective-permute-done.refs_1_), channel_id=1, source_target_pairs={{4,0},{19,1},{8,4},{23,5},{12,8},{27,9},{0,12},{31,13},{6,2},{1,3}... | collective-permute-start | bytes 3244040 | tf_op jit(solution)/shard_map/ppermute | solution.py:76
  27.2 1.7 %collective-permute-start.6 = (bf16[128,4224]{1,0:T(8,128)(2,1)S(1)}, bf16[128,4224]{1,0:T(8,128)(2,1)}, u32[]{:S(2)}, u32[]{:S(2)}) collective-permute-start(bf16[128,4224]{1,0:T(8,128)(2,1)S(1)} %collective-permute-done.refs_1_), channel_id=1, source_target_pairs={{32,0},{97,1},{36,4},{101,5},{40,8},{105,9},{44,12},{109,13},{34,2... | collective-permute-start | bytes 3244040 | tf_op jit(solution)/shard_map/ppermute | solution.py:76
  28.9 7.7 %collective-permute-done.4.refs_4_ = bf16[128,4224]{1,0:T(8,128)(2,1)S(1)} collective-permute-done((bf16[128,4224]{1,0:T(8,128)(2,1)S(1)}, bf16[128,4224]{1,0:T(8,128)(2,1)S(1)}, u32[]{:S(2)}, u32[]{:S(2)}) %collective-permute-start.4) | collective-permute-done | bytes 1081376 | tf_op jit(solution)/shard_map/ppermute | solution.py:76
  36.6 1.0 copy-done.2
  37.7 2.2 %collective-permute-done.2.refs_6_ = bf16[128,4224]{1,0:T(8,128)(2,1)} collective-permute-done((bf16[128,4224]{1,0:T(8,128)(2,1)S(1)}, bf16[128,4224]{1,0:T(8,128)(2,1)}, u32[]{:S(2)}, u32[]{:S(2)}) %collective-permute-start.2) | collective-permute-done | bytes 1081376 | tf_op jit(solution)/shard_map/ppermute | solution.py:76
  39.8 1.5 %collective-permute-start.5 = (bf16[128,4224]{1,0:T(8,128)(2,1)}, bf16[128,4224]{1,0:T(8,128)(2,1)}, u32[]{:S(2)}, u32[]{:S(2)}) collective-permute-start(bf16[128,4224]{1,0:T(8,128)(2,1)} %collective-permute-done.2.refs_6_), channel_id=1, source_target_pairs={{2,0},{13,1},{6,4},{1,5},{10,8},{5,9},{14,12},{9,13},{16,2},{15,3}... | collective-permute-start | bytes 3244040 | tf_op jit(solution)/shard_map/ppermute | solution.py:76
  41.4 1.1 %collective-permute-done.6.refs_5_ = bf16[128,4224]{1,0:T(8,128)(2,1)} collective-permute-done((bf16[128,4224]{1,0:T(8,128)(2,1)S(1)}, bf16[128,4224]{1,0:T(8,128)(2,1)}, u32[]{:S(2)}, u32[]{:S(2)}) %collective-permute-start.6) | collective-permute-done | bytes 1081376 | tf_op jit(solution)/shard_map/ppermute | solution.py:76
  42.4 3.0 %collective-permute-start.7 = (bf16[128,4224]{1,0:T(8,128)(2,1)}, bf16[128,4224]{1,0:T(8,128)(2,1)}, u32[]{:S(2)}, u32[]{:S(2)}) collective-permute-start(bf16[128,4224]{1,0:T(8,128)(2,1)} %collective-permute-done.6.refs_5_), channel_id=1, source_target_pairs={{32,0},{97,1},{36,4},{101,5},{40,8},{105,9},{44,12},{109,13},{34,2... | collective-permute-start | bytes 3244040 | tf_op jit(solution)/shard_map/ppermute | solution.py:76
  45.4 0.7 dynamic-slice_bitcast_fusion
  47.4 0.7 fusion
  48.9 6.5 %collective-permute-done.5.refs_7_.refs_6_ = bf16[128,4224]{1,0:T(8,128)(2,1)} collective-permute-done((bf16[128,4224]{1,0:T(8,128)(2,1)}, bf16[128,4224]{1,0:T(8,128)(2,1)}, u32[]{:S(2)}, u32[]{:S(2)}) %collective-permute-start.5) | collective-permute-done | bytes 1081376 | tf_op jit(solution)/shard_map/ppermute | solution.py:76
  55.3 3.1 %collective-permute-done.7.refs_8_.refs_7_ = bf16[128,4224]{1,0:T(8,128)(2,1)} collective-permute-done((bf16[128,4224]{1,0:T(8,128)(2,1)}, bf16[128,4224]{1,0:T(8,128)(2,1)}, u32[]{:S(2)}, u32[]{:S(2)}) %collective-permute-start.7) | collective-permute-done | bytes 1081376 | tf_op jit(solution)/shard_map/ppermute | solution.py:76
  58.4 3.5 %collective-permute-done.8.refs_9_.refs_8_ = bf16[128,4224]{1,0:T(8,128)(2,1)} collective-permute-done((bf16[128,4224]{1,0:T(8,128)(2,1)S(1)}, bf16[128,4224]{1,0:T(8,128)(2,1)}, u32[]{:S(2)}, u32[]{:S(2)}) %collective-permute-start.8) | collective-permute-done | bytes 1081376 | tf_op jit(solution)/shard_map/ppermute | solution.py:76
  61.9 1.6 %shard_map.73.in_ref = f32[26,128]{1,0:T(8,128)S(1)} custom-call(f32[2,26,13]{2,1,0:T(8,128)S(1)} %select_select_fusion.w_ref, f32[26,128]{1,0:T(8,128)S(1)} %broadcast_in_dim.68.in_ref, bf16[128,4224]{1,0:T(8,128)(2,1)S(1)} %pad_maximum_fusion.refs_0_), custom_call_target="tpu_custom_call" | custom-call | flops 134217728 | bytes 1048576 | tf_op jit(solution)/shard_map/pallas_call | solution.py:173
  64.2 0.8 collective-permute-start.17
  65.0 1.5 %collective-permute-done.15.refs_16_.refs_17_ = bf16[128,4224]{1,0:T(8,128)(2,1)S(1)} collective-permute-done((bf16[128,4224]{1,0:T(8,128)(2,1)}, bf16[128,4224]{1,0:T(8,128)(2,1)S(1)}, u32[]{:S(2)}, u32[]{:S(2)}) %collective-permute-start.15) | collective-permute-done | bytes 1081376 | tf_op jit(solution)/shard_map/ppermute | solution.py:81
  66.5 1.6 %collective-permute-start.18 = (bf16[128,4224]{1,0:T(8,128)(2,1)}, bf16[128,4224]{1,0:T(8,128)(2,1)S(1)}, u32[]{:S(2)}, u32[]{:S(2)}) collective-permute-start(bf16[128,4224]{1,0:T(8,128)(2,1)} %collective-permute-done.2.refs_6_), channel_id=1, source_target_pairs={{4,0},{19,1},{8,4},{23,5},{12,8},{27,9},{0,12},{31,13},{6,2},{1,3}... | collective-permute-start | bytes 3244040 | tf_op jit(solution)/shard_map/ppermute | solution.py:76
  68.1 1.4 %collective-permute-done.13.refs_14_.refs_15_ = bf16[128,4224]{1,0:T(8,128)(2,1)S(1)} collective-permute-done((bf16[128,4224]{1,0:T(8,128)(2,1)}, bf16[128,4224]{1,0:T(8,128)(2,1)S(1)}, u32[]{:S(2)}, u32[]{:S(2)}) %collective-permute-start.13) | collective-permute-done | bytes 1081376 | tf_op jit(solution)/shard_map/ppermute | solution.py:81
  69.6 1.2 %copy-done.3 = bf16[128,4224]{1,0:T(8,128)(2,1)S(1)} copy-done((bf16[128,4224]{1,0:T(8,128)(2,1)S(1)}, bf16[128,4224]{1,0:T(8,128)(2,1)}, u32[]{:S(2)}) %copy-start.3) | copy-done | bytes 1081368
  70.8 11.2 %shard_map.74.in_ref = f32[26,128]{1,0:T(8,128)S(1)} custom-call(f32[2,26,13]{2,1,0:T(8,128)S(1)} %select_select_fusion.w_ref, f32[26,128]{1,0:T(8,128)S(1)} %shard_map.73.in_ref, bf16[128,4224]{1,0:T(8,128)(2,1)S(1)} %pad_maximum_fusion.refs_0_, bf16[128,4224]{1,0:T(8,128)(2,1)S(1)} %collective-permute-done.refs_1_, ...), custom_call_target="tpu_custom_call" | custom-call | flops 6710886400 | bytes 17825792 | tf_op jit(solution)/shard_map/pallas_call | solution.py:173
  82.0 7.5 %shard_map.75 = f32[26,128]{1,0:T(8,128)S(1)} custom-call(f32[2,26,13]{2,1,0:T(8,128)S(1)} %select_select_fusion.w_ref, f32[26,128]{1,0:T(8,128)S(1)} %shard_map.74.in_ref, bf16[128,4224]{1,0:T(8,128)(2,1)S(1)} %pad_maximum_fusion.refs_0_, bf16[128,4224]{1,0:T(8,128)(2,1)S(1)} %collective-permute-done.refs_1_, ...), custom_call_target="tpu_custom_call" | custom-call | flops 4294967296 | bytes 18874368 | tf_op jit(solution)/shard_map/pallas_call | solution.py:173
  89.6 0.7 select_reduce_fusion
  90.2 14.5 %all_to_all.9 = f32[128,1,128]{2,1,0:T(1,128)S(1)} all-to-all(f32[128,1,128]{2,1,0:T(1,128)S(1)} %bitcast.11), channel_id=1, replica_groups=mesh['row'=8,'col'=16] {'row','col'}, dimensions={0} | all-to-all | bytes 131072 | tf_op jit(solution)/shard_map/all_to_all | solution.py:231
  104.9 0.5 broadcast_divide_fusion
  (36 shorter events, 1.7 us)
Async XLA Ops:
  0.7 45.9 %copy-start.6 = (s32[128]{0:T(128)S(1)}, s32[128]{0:T(128)}, u32[]{:S(2)}) copy-start(s32[128]{0:T(128)} %param.10) | copy-start | bytes 1540
  0.7 48.2 %copy-start.4 = (f32[2,26,13]{2,1,0:T(8,128)S(1)}, f32[2,26,13]{2,1,0:T(8,128)}, u32[]{:S(2)}) copy-start(f32[2,26,13]{2,1,0:T(8,128)} %constant.41.clone) | copy-start | bytes 8116
  0.7 48.2 %copy-start.5 = (f32[2,26,13]{2,1,0:T(8,128)S(1)}, f32[2,26,13]{2,1,0:T(8,128)}, u32[]{:S(2)}) copy-start(f32[2,26,13]{2,1,0:T(8,128)} %constant.42.clone) | copy-start | bytes 8116
  2.1 16.4 %collective-permute-start.3 = (bf16[128,4224]{1,0:T(8,128)(2,1)S(1)}, bf16[128,4224]{1,0:T(8,128)(2,1)S(1)}, u32[]{:S(2)}, u32[]{:S(2)}) collective-permute-start(bf16[128,4224]{1,0:T(8,128)(2,1)S(1)} %pad_maximum_fusion.refs_0_), channel_id=1, source_target_pairs={{96,0},{33,1},{100,4},{37,5},{104,8},{41,9},{108,12},{45,13},{98,2... | collective-permute-start | bytes 3244040 | tf_op jit(solution)/shard_map/ppermute | solution.py:76
  3.8 15.7 %collective-permute-start = (bf16[128,4224]{1,0:T(8,128)(2,1)S(1)}, bf16[128,4224]{1,0:T(8,128)(2,1)S(1)}, u32[]{:S(2)}, u32[]{:S(2)}) collective-permute-start(bf16[128,4224]{1,0:T(8,128)(2,1)S(1)} %pad_maximum_fusion.refs_0_), channel_id=1, source_target_pairs={{2,0},{13,1},{6,4},{1,5},{10,8},{5,9},{14,12},{9,13},{16,2},{15,3}... | collective-permute-start | bytes 3244040 | tf_op jit(solution)/shard_map/ppermute | solution.py:76
  6.8 16.4 %collective-permute-start.1 = (bf16[128,4224]{1,0:T(8,128)(2,1)S(1)}, bf16[128,4224]{1,0:T(8,128)(2,1)S(1)}, u32[]{:S(2)}, u32[]{:S(2)}) collective-permute-start(bf16[128,4224]{1,0:T(8,128)(2,1)S(1)} %pad_maximum_fusion.refs_0_), channel_id=1, source_target_pairs={{18,0},{5,1},{22,4},{9,5},{26,8},{13,9},{30,12},{1,13},{0,2},{7,3}... | collective-permute-start | bytes 3244040 | tf_op jit(solution)/shard_map/ppermute | solution.py:76
  19.4 17.2 %collective-permute-start.4 = (bf16[128,4224]{1,0:T(8,128)(2,1)S(1)}, bf16[128,4224]{1,0:T(8,128)(2,1)S(1)}, u32[]{:S(2)}, u32[]{:S(2)}) collective-permute-start(bf16[128,4224]{1,0:T(8,128)(2,1)S(1)} %collective-permute-done.3.refs_2_), channel_id=1, source_target_pairs={{12,0},{3,1},{0,4},{7,5},{4,8},{11,9},{8,12},{15,13},{14,2},{17,3}... | collective-permute-start | bytes 3244040 | tf_op jit(solution)/shard_map/ppermute | solution.py:76
  23.1 19.3 %copy-start = (bf16[128,4224]{1,0:T(8,128)(2,1)}, bf16[128,4224]{1,0:T(8,128)(2,1)S(1)}, u32[]{:S(2)}) copy-start(bf16[128,4224]{1,0:T(8,128)(2,1)S(1)} %collective-permute-done.1.refs_3_) | copy-start | bytes 3244036
  23.1 16.7 %collective-permute-start.2 = (bf16[128,4224]{1,0:T(8,128)(2,1)S(1)}, bf16[128,4224]{1,0:T(8,128)(2,1)}, u32[]{:S(2)}, u32[]{:S(2)}) collective-permute-start(bf16[128,4224]{1,0:T(8,128)(2,1)S(1)} %collective-permute-done.refs_1_), channel_id=1, source_target_pairs={{4,0},{19,1},{8,4},{23,5},{12,8},{27,9},{0,12},{31,13},{6,2},{1,3}... | collective-permute-start | bytes 3244040 | tf_op jit(solution)/shard_map/ppermute | solution.py:76
  27.2 15.3 %collective-permute-start.6 = (bf16[128,4224]{1,0:T(8,128)(2,1)S(1)}, bf16[128,4224]{1,0:T(8,128)(2,1)}, u32[]{:S(2)}, u32[]{:S(2)}) collective-permute-start(bf16[128,4224]{1,0:T(8,128)(2,1)S(1)} %collective-permute-done.refs_1_), channel_id=1, source_target_pairs={{32,0},{97,1},{36,4},{101,5},{40,8},{105,9},{44,12},{109,13},{34,2... | collective-permute-start | bytes 3244040 | tf_op jit(solution)/shard_map/ppermute | solution.py:76
  36.6 1.0 copy-start.2
  39.8 15.5 %collective-permute-start.5 = (bf16[128,4224]{1,0:T(8,128)(2,1)}, bf16[128,4224]{1,0:T(8,128)(2,1)}, u32[]{:S(2)}, u32[]{:S(2)}) collective-permute-start(bf16[128,4224]{1,0:T(8,128)(2,1)} %collective-permute-done.2.refs_6_), channel_id=1, source_target_pairs={{2,0},{13,1},{6,4},{1,5},{10,8},{5,9},{14,12},{9,13},{16,2},{15,3}... | collective-permute-start | bytes 3244040 | tf_op jit(solution)/shard_map/ppermute | solution.py:76
  42.4 15.9 %collective-permute-start.7 = (bf16[128,4224]{1,0:T(8,128)(2,1)}, bf16[128,4224]{1,0:T(8,128)(2,1)}, u32[]{:S(2)}, u32[]{:S(2)}) collective-permute-start(bf16[128,4224]{1,0:T(8,128)(2,1)} %collective-permute-done.6.refs_5_), channel_id=1, source_target_pairs={{32,0},{97,1},{36,4},{101,5},{40,8},{105,9},{44,12},{109,13},{34,2... | collective-permute-start | bytes 3244040 | tf_op jit(solution)/shard_map/ppermute | solution.py:76
  45.4 16.5 %collective-permute-start.8 = (bf16[128,4224]{1,0:T(8,128)(2,1)S(1)}, bf16[128,4224]{1,0:T(8,128)(2,1)}, u32[]{:S(2)}, u32[]{:S(2)}) collective-permute-start(bf16[128,4224]{1,0:T(8,128)(2,1)S(1)} %collective-permute-done.3.refs_2_), channel_id=1, source_target_pairs={{18,0},{5,1},{22,4},{9,5},{26,8},{13,9},{30,12},{1,13},{0,2},{7,3}... | collective-permute-start | bytes 3244040 | tf_op jit(solution)/shard_map/ppermute | solution.py:76
  46.1 17.5 %collective-permute-start.9 = (bf16[128,4224]{1,0:T(8,128)(2,1)S(1)}, bf16[128,4224]{1,0:T(8,128)(2,1)}, u32[]{:S(2)}, u32[]{:S(2)}) collective-permute-start(bf16[128,4224]{1,0:T(8,128)(2,1)S(1)} %collective-permute-done.3.refs_2_), channel_id=1, source_target_pairs={{1,0},{0,1},{5,4},{4,5},{9,8},{8,9},{13,12},{12,13},{3,2},{2,3},{7... | collective-permute-start | bytes 3244040 | tf_op jit(solution)/shard_map/ppermute | solution.py:81
  46.1 18.0 %collective-permute-start.10 = (bf16[128,4224]{1,0:T(8,128)(2,1)}, bf16[128,4224]{1,0:T(8,128)(2,1)}, u32[]{:S(2)}, u32[]{:S(2)}) collective-permute-start(bf16[128,4224]{1,0:T(8,128)(2,1)} %copy-done), channel_id=1, source_target_pairs={{1,0},{0,1},{5,4},{4,5},{9,8},{8,9},{13,12},{12,13},{3,2},{2,3},{7... | collective-permute-start | bytes 3244040 | tf_op jit(solution)/shard_map/ppermute | solution.py:81
  48.7 20.8 %copy-start.1 = (bf16[128,4224]{1,0:T(8,128)(2,1)S(1)}, bf16[128,4224]{1,0:T(8,128)(2,1)}, u32[]{:S(2)}) copy-start(bf16[128,4224]{1,0:T(8,128)(2,1)} %copy-done) | copy-start | bytes 3244036
  55.3 8.8 %collective-permute-start.12 = (bf16[128,4224]{1,0:T(8,128)(2,1)}, bf16[128,4224]{1,0:T(8,128)(2,1)S(1)}, u32[]{:S(2)}, u32[]{:S(2)}) collective-permute-start(bf16[128,4224]{1,0:T(8,128)(2,1)} %collective-permute-done.2.refs_6_), channel_id=1, source_target_pairs={{1,0},{0,1},{5,4},{4,5},{9,8},{8,9},{13,12},{12,13},{3,2},{2,3},{7... | collective-permute-start | bytes 3244040 | tf_op jit(solution)/shard_map/ppermute | solution.py:81
  58.4 5.8 %collective-permute-start.11 = (bf16[128,4224]{1,0:T(8,128)(2,1)}, bf16[128,4224]{1,0:T(8,128)(2,1)S(1)}, u32[]{:S(2)}, u32[]{:S(2)}) collective-permute-start(bf16[128,4224]{1,0:T(8,128)(2,1)} %collective-permute-done.6.refs_5_), channel_id=1, source_target_pairs={{1,0},{0,1},{5,4},{4,5},{9,8},{8,9},{13,12},{12,13},{3,2},{2,3},{7... | collective-permute-start | bytes 3244040 | tf_op jit(solution)/shard_map/ppermute | solution.py:81
  63.5 3.0 %collective-permute-start.15 = (bf16[128,4224]{1,0:T(8,128)(2,1)}, bf16[128,4224]{1,0:T(8,128)(2,1)S(1)}, u32[]{:S(2)}, u32[]{:S(2)}) collective-permute-start(bf16[128,4224]{1,0:T(8,128)(2,1)} %collective-permute-done.8.refs_9_.refs_8_), channel_id=1, source_target_pairs={{1,0},{0,1},{5,4},{4,5},{9,8},{8,9},{13,12},{12,13},{3,2},{2,3},{7... | collective-permute-start | bytes 3244040 | tf_op jit(solution)/shard_map/ppermute | solution.py:81
  63.6 4.5 %collective-permute-start.14 = (bf16[128,4224]{1,0:T(8,128)(2,1)}, bf16[128,4224]{1,0:T(8,128)(2,1)S(1)}, u32[]{:S(2)}, u32[]{:S(2)}) collective-permute-start(bf16[128,4224]{1,0:T(8,128)(2,1)} %collective-permute-done.7.refs_8_.refs_7_), channel_id=1, source_target_pairs={{1,0},{0,1},{5,4},{4,5},{9,8},{8,9},{13,12},{12,13},{3,2},{2,3},{7... | collective-permute-start | bytes 3244040 | tf_op jit(solution)/shard_map/ppermute | solution.py:81
  64.1 5.5 %collective-permute-start.13 = (bf16[128,4224]{1,0:T(8,128)(2,1)}, bf16[128,4224]{1,0:T(8,128)(2,1)S(1)}, u32[]{:S(2)}, u32[]{:S(2)}) collective-permute-start(bf16[128,4224]{1,0:T(8,128)(2,1)} %collective-permute-done.5.refs_7_.refs_6_), channel_id=1, source_target_pairs={{1,0},{0,1},{5,4},{4,5},{9,8},{8,9},{13,12},{12,13},{3,2},{2,3},{7... | collective-permute-start | bytes 3244040 | tf_op jit(solution)/shard_map/ppermute | solution.py:81
  64.2 17.8 %collective-permute-start.16 = (bf16[128,4224]{1,0:T(8,128)(2,1)}, bf16[128,4224]{1,0:T(8,128)(2,1)S(1)}, u32[]{:S(2)}, u32[]{:S(2)}) collective-permute-start(bf16[128,4224]{1,0:T(8,128)(2,1)} %collective-permute-done.8.refs_9_.refs_8_), channel_id=1, source_target_pairs={{12,0},{3,1},{0,4},{7,5},{4,8},{11,9},{8,12},{15,13},{14,2},{17,3}... | collective-permute-start | bytes 3244040 | tf_op jit(solution)/shard_map/ppermute | solution.py:76
  64.2 17.8 %collective-permute-start.17 = (bf16[128,4224]{1,0:T(8,128)(2,1)}, bf16[128,4224]{1,0:T(8,128)(2,1)S(1)}, u32[]{:S(2)}, u32[]{:S(2)}) collective-permute-start(bf16[128,4224]{1,0:T(8,128)(2,1)} %collective-permute-done.5.refs_7_.refs_6_), channel_id=1, source_target_pairs={{32,0},{97,1},{36,4},{101,5},{40,8},{105,9},{44,12},{109,13},{34,2... | collective-permute-start | bytes 3244040 | tf_op jit(solution)/shard_map/ppermute | solution.py:76
  66.5 15.5 %collective-permute-start.18 = (bf16[128,4224]{1,0:T(8,128)(2,1)}, bf16[128,4224]{1,0:T(8,128)(2,1)S(1)}, u32[]{:S(2)}, u32[]{:S(2)}) collective-permute-start(bf16[128,4224]{1,0:T(8,128)(2,1)} %collective-permute-done.2.refs_6_), channel_id=1, source_target_pairs={{4,0},{19,1},{8,4},{23,5},{12,8},{27,9},{0,12},{31,13},{6,2},{1,3}... | collective-permute-start | bytes 3244040 | tf_op jit(solution)/shard_map/ppermute | solution.py:76
  69.5 1.2 %copy-start.3 = (bf16[128,4224]{1,0:T(8,128)(2,1)S(1)}, bf16[128,4224]{1,0:T(8,128)(2,1)}, u32[]{:S(2)}) copy-start(bf16[128,4224]{1,0:T(8,128)(2,1)} %copy-done.2) | copy-start | bytes 3244036

commit v5 on v4

--- a/solution.py
+++ b/solution.py
@@ -12,30 +12,30 @@
 
 SLOTS = (
     (0, 0, 0),
-    (0, 1, 0), (3, 0, 0), (0, 3, 0),
-    (3, 0, 3), (1, 1, 0), (0, 1, 1),
-    (0, 2, 1), (2, 1, 0), (3, 3, 0),
-    (3, 3, 3), (1, 2, 1), (0, 1, 2),
+    (3, 0, 0), (0, 1, 0), (0, 3, 0),
+    (1, 1, 0), (3, 0, 1), (0, 3, 3),
+    (3, 3, 3), (3, 1, 1), (3, 0, 2),
+    (2, 3, 3), (1, 2, 0), (3, 1, 2),
 )
-PARENT = (None, 0, 0, 0, 2, 1, 1, 6, 5, 2, 9, 7, 6)
-ROUNDS = ((0,), (1, 2, 3), (4, 5, 6), (7, 8, 9), (10, 11, 12))
+PARENT = (None, 0, 0, 0, 2, 1, 3, 6, 5, 5, 7, 4, 8)
+ROUNDS = ((0,), (1, 2, 3), (4, 6, 5), (7, 8, 9), (10, 11, 12))
 OWN = (
-    (0, 0, True), (1, 0, False), (6, 0, False), (11, 0, False), (12, 0, False), (5, 1, False), (8, 1, True),
-    (11, 1, False), (12, 1, True), (5, 2, False), (8, 2, False), (11, 2, False), (12, 2, False), (1, 3, True),
-    (6, 3, False), (11, 3, False), (12, 3, True), (0, 4, False), (7, 4, False), (11, 4, True), (12, 4, False),
-    (0, 5, False), (4, 5, False), (7, 5, False), (12, 5, False), (5, 6, False), (8, 6, False), (10, 7, False),
-    (12, 7, False), (10, 8, False), (12, 8, True), (5, 9, True), (8, 9, False), (9, 10, False), (9, 11, False),
-    (10, 11, False),
+    (0, 0, True), (9, 0, False), (3, 1, False), (4, 1, False), (6, 1, False), (7, 1, False), (9, 1, True),
+    (3, 2, True), (4, 2, False), (6, 2, False), (7, 2, False), (9, 2, False), (9, 3, False), (0, 4, False),
+    (5, 4, False), (9, 4, False), (0, 5, False), (9, 5, False), (8, 6, False), (10, 6, True), (11, 6, False),
+    (3, 7, False), (4, 7, False), (5, 7, False), (8, 7, True), (3, 8, False), (4, 8, False), (5, 8, False),
+    (8, 9, False), (10, 9, False), (11, 9, True), (0, 10, False), (1, 10, False), (0, 11, False), (1, 11, True),
+    (4, 12, True),
 )
 CROSS = (
-    (3, 0, 0), (3, 0, 1), (8, 0, 0), (8, 0, 1), (9, 0, 0), (9, 0, 1), (2, 1, 0), (2, 1, 1), (5, 1, 1),
-    (9, 1, 0), (9, 1, 1), (2, 2, 1), (5, 2, 0), (5, 2, 1), (9, 2, 0), (9, 2, 1), (3, 3, 1), (8, 3, 0),
-    (8, 3, 1), (9, 3, 1), (5, 4, 1), (8, 4, 0), (9, 4, 0), (9, 4, 1), (5, 5, 1), (6, 5, 0), (6, 5, 1),
-    (7, 5, 1), (8, 5, 1), (9, 5, 0), (9, 5, 1), (6, 6, 0), (7, 6, 0), (7, 6, 1), (8, 6, 0), (8, 6, 1),
-    (2, 7, 0), (2, 7, 1), (8, 7, 1), (2, 8, 0), (2, 8, 1), (8, 8, 0), (7, 9, 0), (7, 9, 1), (8, 9, 0),
-    (8, 9, 1), (2, 10, 0), (3, 10, 0), (3, 10, 1), (6, 10, 0), (8, 10, 0), (8, 10, 1), (9, 10, 0), (9, 10, 1),
-    (2, 11, 0), (2, 11, 1), (3, 11, 0), (3, 11, 1), (6, 11, 0), (6, 11, 1), (7, 11, 0), (8, 11, 0), (9, 11, 0),
-    (9, 11, 1),
+    (0, 0, 1), (4, 0, 0), (4, 0, 1), (6, 0, 0), (2, 1, 0), (2, 1, 1), (8, 1, 0), (9, 1, 0), (9, 1, 1),
+    (2, 2, 0), (8, 2, 0), (8, 2, 1), (4, 3, 1), (6, 3, 0), (6, 3, 1), (7, 3, 0), (7, 3, 1), (1, 4, 0),
+    (1, 4, 1), (2, 4, 1), (3, 4, 1), (6, 4, 0), (6, 4, 1), (8, 4, 0), (8, 4, 1), (1, 5, 0), (1, 5, 1),
+    (2, 5, 0), (2, 5, 1), (3, 5, 1), (6, 5, 0), (6, 5, 1), (8, 5, 0), (8, 5, 1), (2, 6, 0), (2, 6, 1),
+    (6, 6, 0), (7, 6, 1), (0, 7, 1), (8, 7, 1), (0, 8, 1), (8, 8, 1), (7, 9, 0), (7, 9, 1), (0, 10, 0),
+    (1, 10, 1), (2, 10, 0), (2, 10, 1), (3, 10, 0), (3, 10, 1), (7, 10, 0), (8, 10, 0), (0, 11, 0), (0, 11, 1),
+    (1, 11, 0), (1, 11, 1), (2, 11, 0), (2, 11, 1), (3, 11, 0), (3, 11, 1), (8, 11, 0), (8, 11, 1), (2, 12, 0),
+    (2, 12, 1),
 )
 N_SLOTS = len(SLOTS)
 PAIRS = ((0, 3), (1, 2), (4, 5), (6, 9), (7, 8), (10, 11), (12,))
@@ -58,10 +58,6 @@
 def on_core(offset, core):
     x, y, z = offset
     return (-x, -z, -y) if core else offset
-
-
-def plus(a, b):
-    return tuple((i + j) % SIDE for i, j in zip(a, b))
 
 
 def minus(a, b):
@@ -210,6 +206,8 @@
             value, _ = lax.optimization_barrier((value, u))
         return value
 
+    if 0 in OTHERS:
+        blocks[N_SLOTS] = swap(blocks[0])
     for n in range(1, len(ROUNDS)):
         until = [blocks[slot] for slot in ROUNDS[n - 1]] if n > 1 else []
         for at, slot in enumerate(ROUNDS[n]):
@@ -217,14 +215,17 @@
             blocks[slot] = shift(
                 held_back(blocks[parent], until[at : at + 1]), minus(SLOTS[slot], SLOTS[parent])
             )
-        if n == len(ROUNDS) - 1:
-            sums = add_pairs(work[0], blocks, held_back(sums, until), weights, feats)
+        if n == 3:
+            sums = add_pairs(work[0] + work[1], blocks, sums, weights, feats)
+            until = until[:2] + [sums]
+        if n == 4:
+            sums = jnp.where(width < 0, 0.0, held_back(sums, until))
             until = until + [sums]
         for slot in ROUNDS[n - 1] if n > 1 else ():
             if slot in OTHERS:
                 blocks[N_SLOTS + slot] = swap(held_back(blocks[slot], until))
-    sums = add_pairs(sum(work[1:-1], []), blocks, sums, weights, feats)
-    sums = add_pairs(work[-1], blocks, sums, weights, feats)
+    sums = add_pairs(work[2] + work[3], blocks, sums, weights, feats)
+    sums = add_pairs(work[4], blocks, sums, weights, feats)
 
     home = held[None, :] == jnp.arange(2 * SIDE**3, dtype=jnp.int32)[:, None]
     parts = jnp.sum(jnp.where(home[:, :, None], sums[None], 0.0), axis=1)

time: 106 us -> 105 us (level)
  waiting for transfers between devices: 41.3 us -> 37.4 us
  blocking collectives: 14.5 us -> 17 us
    ppermute x12, waiting for transfers between devices: 38.4 us -> 34.3 us  [shift(): return lax.ppermute(value, AXES, pairs)]
    all_to_all x1, blocking collectives: 14.5 us -> 17 us  [on_device(): total = jnp.sum(lax.all_to_all(parts, AXES, 0, 0, tiled=True), axis=0)]
    unnamed x14 -> x16, local copies, waits for them, and re-layouts: 2.3 us -> 1.26 us
    ppermute x7 -> x9, waiting for transfers between devices: 2.92 us -> 3.13 us  [swap(): return lax.ppermute(value, AXES, pairs)]
  transfers between devices with their start and end apart: 19 -> 21, of which waited for: 11 -> 12; matrix products, arithmetic and copies ran while one was open for 2% -> 2% of each run, Pallas kernels for 12% -> 14%
where the time goes in v5:
time: 105 us; the launch traced here: 104 us
  waiting for transfers between devices  37.4 us (36%)
  starting transfers between devices  21.1 us (20%)
  Pallas kernels  20.9 us (20%)
  blocking collectives  17 us (16%)
  other arithmetic  3.85 us (4%)
  local copies, waits for them, and re-layouts  2.62 us (2%)
  between operations  1.47 us (1%)
    ppermute x12, waiting for transfers between devices, shift(): return lax.ppermute(value, AXES, pairs)  34.3 us
    pallas_call x3, Pallas kernels, add_pairs(): pl.pallas_call(body, out_shape=jax.ShapeDtypeStruct(sums.shape, jnp.float...  20.9 us
    ppermute x12, starting transfers between devices, shift(): return lax.ppermute(value, AXES, pairs)  19.4 us
    all_to_all x1, blocking collectives, on_device(): total = jnp.sum(lax.all_to_all(parts, AXES, 0, 0, tiled=True), axis=0)  17 us
    ppermute x9, waiting for transfers between devices, swap(): return lax.ppermute(value, AXES, pairs)  3.13 us
  transfers between devices with their start and end apart: 21, of which 12 were waited for; matrix products, arithmetic and copies ran while one was open for 2% of the time, Pallas kernels for 14%

profile of v5, /device:TPU:0, one launch (start us, length us, event | category | flops | bytes accessed | tf_op | source)
XLA Modules:
  0.0 104.3 jit_solution(7395961362632589789)
XLA Ops:
  0.0 0.7 pad.1.clone
  0.7 1.4 %pad_maximum_fusion.refs_0_ = bf16[128,4224]{1,0:T(8,128)(2,1)S(1)} fusion(bf16[128,4096]{1,0:T(8,128)(2,1)} %param.7, bf16[4224]{0:T(1024)(128)(2,1)S(1)} %pad.1.clone), kind=kLoop, calls=%fused_computation.1 | loop fusion | flops 2162688 | bytes 2138368 | tf_op jit(solution)/shard_map/concatenate | solution.py:200
  2.1 1.6 %collective-permute-start = (bf16[128,4224]{1,0:T(8,128)(2,1)S(1)}, bf16[128,4224]{1,0:T(8,128)(2,1)S(1)}, u32[]{:S(2)}, u32[]{:S(2)}) collective-permute-start(bf16[128,4224]{1,0:T(8,128)(2,1)S(1)} %pad_maximum_fusion.refs_0_), channel_id=1, source_target_pairs={{96,0},{33,1},{100,4},{37,5},{104,8},{41,9},{108,12},{45,13},{98,2... | collective-permute-start | bytes 3244040 | tf_op jit(solution)/shard_map/ppermute | solution.py:72
  3.8 3.0 %collective-permute-start.1 = (bf16[128,4224]{1,0:T(8,128)(2,1)S(1)}, bf16[128,4224]{1,0:T(8,128)(2,1)}, u32[]{:S(2)}, u32[]{:S(2)}) collective-permute-start(bf16[128,4224]{1,0:T(8,128)(2,1)S(1)} %pad_maximum_fusion.refs_0_), channel_id=1, source_target_pairs={{2,0},{13,1},{6,4},{1,5},{10,8},{5,9},{14,12},{9,13},{16,2},{15,3}... | collective-permute-start | bytes 3244040 | tf_op jit(solution)/shard_map/ppermute | solution.py:72
  6.8 11.8 %collective-permute-done.refs_1_ = bf16[128,4224]{1,0:T(8,128)(2,1)S(1)} collective-permute-done((bf16[128,4224]{1,0:T(8,128)(2,1)S(1)}, bf16[128,4224]{1,0:T(8,128)(2,1)S(1)}, u32[]{:S(2)}, u32[]{:S(2)}) %collective-permute-start) | collective-permute-done | bytes 1081376 | tf_op jit(solution)/shard_map/ppermute | solution.py:72
  18.5 0.9 collective-permute-done.1.refs_2_
  19.4 3.7 %collective-permute-done.2.refs_3_ = bf16[128,4224]{1,0:T(8,128)(2,1)S(1)} collective-permute-done((bf16[128,4224]{1,0:T(8,128)(2,1)S(1)}, bf16[128,4224]{1,0:T(8,128)(2,1)S(1)}, u32[]{:S(2)}, u32[]{:S(2)}) %collective-permute-start.2) | collective-permute-done | bytes 1081376 | tf_op jit(solution)/shard_map/ppermute | solution.py:72
  23.1 1.9 %collective-permute-start.5 = (bf16[128,4224]{1,0:T(8,128)(2,1)S(1)}, bf16[128,4224]{1,0:T(8,128)(2,1)}, u32[]{:S(2)}, u32[]{:S(2)}) collective-permute-start(bf16[128,4224]{1,0:T(8,128)(2,1)S(1)} %collective-permute-done.2.refs_3_), channel_id=1, source_target_pairs={{12,0},{3,1},{0,4},{7,5},{4,8},{11,9},{8,12},{15,13},{14,2},{17,3}... | collective-permute-start | bytes 3244040 | tf_op jit(solution)/shard_map/ppermute | solution.py:72
  25.1 1.7 %collective-permute-start.6 = (bf16[128,4224]{1,0:T(8,128)(2,1)}, bf16[128,4224]{1,0:T(8,128)(2,1)S(1)}, u32[]{:S(2)}, u32[]{:S(2)}) collective-permute-start(bf16[128,4224]{1,0:T(8,128)(2,1)} %collective-permute-done.1.refs_2_), channel_id=1, source_target_pairs={{32,0},{97,1},{36,4},{101,5},{40,8},{105,9},{44,12},{109,13},{34,2... | collective-permute-start | bytes 3244040 | tf_op jit(solution)/shard_map/ppermute | solution.py:72
  26.8 2.1 %collective-permute-start.8 = (bf16[128,4224]{1,0:T(8,128)(2,1)S(1)}, bf16[128,4224]{1,0:T(8,128)(2,1)}, u32[]{:S(2)}, u32[]{:S(2)}) collective-permute-start(bf16[128,4224]{1,0:T(8,128)(2,1)S(1)} %collective-permute-done.refs_1_), channel_id=1, source_target_pairs={{4,0},{19,1},{8,4},{23,5},{12,8},{27,9},{0,12},{31,13},{6,2},{1,3}... | collective-permute-start | bytes 3244040 | tf_op jit(solution)/shard_map/ppermute | solution.py:72
  28.9 0.5 collective-permute-start.4
  29.4 11.0 %collective-permute-done.5.refs_6_.refs_3_ = bf16[128,4224]{1,0:T(8,128)(2,1)} collective-permute-done((bf16[128,4224]{1,0:T(8,128)(2,1)S(1)}, bf16[128,4224]{1,0:T(8,128)(2,1)}, u32[]{:S(2)}, u32[]{:S(2)}) %collective-permute-start.5) | collective-permute-done | bytes 1081376 | tf_op jit(solution)/shard_map/ppermute | solution.py:72
  40.4 1.9 %collective-permute-start.7 = (bf16[128,4224]{1,0:T(8,128)(2,1)}, bf16[128,4224]{1,0:T(8,128)(2,1)}, u32[]{:S(2)}, u32[]{:S(2)}) collective-permute-start(bf16[128,4224]{1,0:T(8,128)(2,1)} %collective-permute-done.5.refs_6_.refs_3_), channel_id=1, source_target_pairs={{96,0},{33,1},{100,4},{37,5},{104,8},{41,9},{108,12},{45,13},{98,2... | collective-permute-start | bytes 3244040 | tf_op jit(solution)/shard_map/ppermute | solution.py:72
  42.3 3.2 %collective-permute-start.10 = (bf16[128,4224]{1,0:T(8,128)(2,1)}, bf16[128,4224]{1,0:T(8,128)(2,1)}, u32[]{:S(2)}, u32[]{:S(2)}) collective-permute-start(bf16[128,4224]{1,0:T(8,128)(2,1)} %collective-permute-done.8.refs_5_), channel_id=1, source_target_pairs={{4,0},{19,1},{8,4},{23,5},{12,8},{27,9},{0,12},{31,13},{6,2},{1,3}... | collective-permute-start | bytes 3244040 | tf_op jit(solution)/shard_map/ppermute | solution.py:72
  46.2 0.7 dynamic-slice_bitcast_fusion
  47.1 0.7 fusion
  49.2 1.2 %copy-done.1 = bf16[128,4224]{1,0:T(8,128)(2,1)S(1)} copy-done((bf16[128,4224]{1,0:T(8,128)(2,1)S(1)}, bf16[128,4224]{1,0:T(8,128)(2,1)}, u32[]{:S(2)}) %copy-start.1) | copy-done | bytes 1081368
  50.5 3.1 %shard_map.73 = f32[26,128]{1,0:T(8,128)S(1)} custom-call(f32[2,26,13]{2,1,0:T(8,128)S(1)} %select_select_fusion.w_ref, f32[26,128]{1,0:T(8,128)S(1)} %broadcast_in_dim.70.in_ref, bf16[128,4224]{1,0:T(8,128)(2,1)S(1)} %pad_maximum_fusion.refs_0_, bf16[128,4224]{1,0:T(8,128)(2,1)S(1)} %collective-permute-done.refs_1_, ...), custom_call_target="tpu_custom_call" | custom-call | flops 805306368 | bytes 6291456 | tf_op jit(solution)/shard_map/pallas_call | solution.py:169
  53.6 3.5 %collective-permute-done.7.refs_7_ = bf16[128,4224]{1,0:T(8,128)(2,1)} collective-permute-done((bf16[128,4224]{1,0:T(8,128)(2,1)}, bf16[128,4224]{1,0:T(8,128)(2,1)}, u32[]{:S(2)}, u32[]{:S(2)}) %collective-permute-start.7) | collective-permute-done | bytes 1081376 | tf_op jit(solution)/shard_map/ppermute | solution.py:72
  57.1 0.7 collective-permute-done.9.refs_8_
  57.8 0.8 collective-permute-done.10.refs_9_.refs_4_
  59.2 0.8 collective-permute-done.14.refs_15_
  60.0 2.9 %collective-permute-start.20 = (bf16[128,4224]{1,0:T(8,128)(2,1)}, bf16[128,4224]{1,0:T(8,128)(2,1)S(1)}, u32[]{:S(2)}, u32[]{:S(2)}) collective-permute-start(bf16[128,4224]{1,0:T(8,128)(2,1)} %collective-permute-done.9.refs_8_), channel_id=1, source_target_pairs={{4,0},{19,1},{8,4},{23,5},{12,8},{27,9},{0,12},{31,13},{6,2},{1,3}... | collective-permute-start | bytes 3244040 | tf_op jit(solution)/shard_map/ppermute | solution.py:72
  63.3 0.6 collective-permute-start.18
  64.0 0.7 collective-permute-done.16.refs_17_.refs_13_
  64.7 1.5 %collective-permute-done.15.refs_16_.refs_12_ = bf16[128,4224]{1,0:T(8,128)(2,1)S(1)} collective-permute-done((bf16[128,4224]{1,0:T(8,128)(2,1)}, bf16[128,4224]{1,0:T(8,128)(2,1)S(1)}, u32[]{:S(2)}, u32[]{:S(2)}) %collective-permute-start.15) | collective-permute-done | bytes 1081376 | tf_op jit(solution)/shard_map/ppermute | solution.py:77
  66.2 11.7 %shard_map.74.in_ref = f32[26,128]{1,0:T(8,128)S(1)} custom-call(f32[2,26,13]{2,1,0:T(8,128)S(1)} %select_select_fusion.w_ref, f32[26,128]{1,0:T(8,128)S(1)} %broadcast_select_fusion.in_ref, bf16[128,4224]{1,0:T(8,128)(2,1)S(1)} %pad_maximum_fusion.refs_0_, bf16[128,4224]{1,0:T(8,128)(2,1)S(1)} %collective-permute-done.refs_1_, ...), custom_call_target="tpu_custom_call" | custom-call | flops 7247757312 | bytes 19922944 | tf_op jit(solution)/shard_map/pallas_call | solution.py:169
  78.0 1.8 %collective-permute-done.18.refs_5_ = bf16[128,4224]{1,0:T(8,128)(2,1)S(1)} collective-permute-done((bf16[128,4224]{1,0:T(8,128)(2,1)}, bf16[128,4224]{1,0:T(8,128)(2,1)S(1)}, u32[]{:S(2)}, u32[]{:S(2)}) %collective-permute-start.18) | collective-permute-done | bytes 1081376 | tf_op jit(solution)/shard_map/ppermute | solution.py:72
  79.9 6.1 %shard_map.75 = f32[26,128]{1,0:T(8,128)S(1)} custom-call(f32[2,26,13]{2,1,0:T(8,128)S(1)} %select_select_fusion.w_ref, f32[26,128]{1,0:T(8,128)S(1)} %shard_map.74.in_ref, bf16[128,4224]{1,0:T(8,128)(2,1)S(1)} %pad_maximum_fusion.refs_0_, bf16[128,4224]{1,0:T(8,128)(2,1)S(1)} %collective-permute-done.refs_1_, bf16[128,4224]{1,0:T(8,128)(2,1)S(1)} %copy-done.4, ...), custom_call_target="tpu_custom_call" | custom-call | flops 2952790016 | bytes 14680064 | tf_op jit(solution)/shard_map/pallas_call | solution.py:169
  86.0 0.7 select_reduce_fusion
  86.7 17.0 %all_to_all.9 = f32[128,1,128]{2,1,0:T(1,128)S(1)} all-to-all(f32[128,1,128]{2,1,0:T(1,128)S(1)} %bitcast.12), channel_id=1, replica_groups=mesh['row'=8,'col'=16] {'row','col'}, dimensions={0} | all-to-all | bytes 131072 | tf_op jit(solution)/shard_map/all_to_all | solution.py:232
  103.8 0.5 broadcast_divide_fusion
  (43 shorter events, 2.3 us)
Async XLA Ops:
  0.7 46.3 %copy-start.7 = (s32[128]{0:T(128)S(1)}, s32[128]{0:T(128)}, u32[]{:S(2)}) copy-start(s32[128]{0:T(128)} %param.10) | copy-start | bytes 1540
  0.7 48.5 %copy-start.5 = (f32[2,26,13]{2,1,0:T(8,128)S(1)}, f32[2,26,13]{2,1,0:T(8,128)}, u32[]{:S(2)}) copy-start(f32[2,26,13]{2,1,0:T(8,128)} %constant.41.clone) | copy-start | bytes 8116
  0.7 48.5 %copy-start.6 = (f32[2,26,13]{2,1,0:T(8,128)S(1)}, f32[2,26,13]{2,1,0:T(8,128)}, u32[]{:S(2)}) copy-start(f32[2,26,13]{2,1,0:T(8,128)} %constant.42.clone) | copy-start | bytes 8116
  2.1 16.4 %collective-permute-start = (bf16[128,4224]{1,0:T(8,128)(2,1)S(1)}, bf16[128,4224]{1,0:T(8,128)(2,1)S(1)}, u32[]{:S(2)}, u32[]{:S(2)}) collective-permute-start(bf16[128,4224]{1,0:T(8,128)(2,1)S(1)} %pad_maximum_fusion.refs_0_), channel_id=1, source_target_pairs={{96,0},{33,1},{100,4},{37,5},{104,8},{41,9},{108,12},{45,13},{98,2... | collective-permute-start | bytes 3244040 | tf_op jit(solution)/shard_map/ppermute | solution.py:72
  3.8 15.7 %collective-permute-start.1 = (bf16[128,4224]{1,0:T(8,128)(2,1)S(1)}, bf16[128,4224]{1,0:T(8,128)(2,1)}, u32[]{:S(2)}, u32[]{:S(2)}) collective-permute-start(bf16[128,4224]{1,0:T(8,128)(2,1)S(1)} %pad_maximum_fusion.refs_0_), channel_id=1, source_target_pairs={{2,0},{13,1},{6,4},{1,5},{10,8},{5,9},{14,12},{9,13},{16,2},{15,3}... | collective-permute-start | bytes 3244040 | tf_op jit(solution)/shard_map/ppermute | solution.py:72
  6.8 16.4 %collective-permute-start.2 = (bf16[128,4224]{1,0:T(8,128)(2,1)S(1)}, bf16[128,4224]{1,0:T(8,128)(2,1)S(1)}, u32[]{:S(2)}, u32[]{:S(2)}) collective-permute-start(bf16[128,4224]{1,0:T(8,128)(2,1)S(1)} %pad_maximum_fusion.refs_0_), channel_id=1, source_target_pairs={{18,0},{5,1},{22,4},{9,5},{26,8},{13,9},{30,12},{1,13},{0,2},{7,3}... | collective-permute-start | bytes 3244040 | tf_op jit(solution)/shard_map/ppermute | solution.py:72
  23.1 19.2 %copy-start = (bf16[128,4224]{1,0:T(8,128)(2,1)}, bf16[128,4224]{1,0:T(8,128)(2,1)S(1)}, u32[]{:S(2)}) copy-start(bf16[128,4224]{1,0:T(8,128)(2,1)S(1)} %collective-permute-done.2.refs_3_) | copy-start | bytes 3244036
  23.1 17.3 %collective-permute-start.5 = (bf16[128,4224]{1,0:T(8,128)(2,1)S(1)}, bf16[128,4224]{1,0:T(8,128)(2,1)}, u32[]{:S(2)}, u32[]{:S(2)}) collective-permute-start(bf16[128,4224]{1,0:T(8,128)(2,1)S(1)} %collective-permute-done.2.refs_3_), channel_id=1, source_target_pairs={{12,0},{3,1},{0,4},{7,5},{4,8},{11,9},{8,12},{15,13},{14,2},{17,3}... | collective-permute-start | bytes 3244040 | tf_op jit(solution)/shard_map/ppermute | solution.py:72
  25.1 15.4 %collective-permute-start.6 = (bf16[128,4224]{1,0:T(8,128)(2,1)}, bf16[128,4224]{1,0:T(8,128)(2,1)S(1)}, u32[]{:S(2)}, u32[]{:S(2)}) collective-permute-start(bf16[128,4224]{1,0:T(8,128)(2,1)} %collective-permute-done.1.refs_2_), channel_id=1, source_target_pairs={{32,0},{97,1},{36,4},{101,5},{40,8},{105,9},{44,12},{109,13},{34,2... | collective-permute-start | bytes 3244040 | tf_op jit(solution)/shard_map/ppermute | solution.py:72
  26.8 15.5 %collective-permute-start.8 = (bf16[128,4224]{1,0:T(8,128)(2,1)S(1)}, bf16[128,4224]{1,0:T(8,128)(2,1)}, u32[]{:S(2)}, u32[]{:S(2)}) collective-permute-start(bf16[128,4224]{1,0:T(8,128)(2,1)S(1)} %collective-permute-done.refs_1_), channel_id=1, source_target_pairs={{4,0},{19,1},{8,4},{23,5},{12,8},{27,9},{0,12},{31,13},{6,2},{1,3}... | collective-permute-start | bytes 3244040 | tf_op jit(solution)/shard_map/ppermute | solution.py:72
  28.9 19.6 %collective-permute-start.3 = (bf16[128,4224]{1,0:T(8,128)(2,1)S(1)}, bf16[128,4224]{1,0:T(8,128)(2,1)S(1)}, u32[]{:S(2)}, u32[]{:S(2)}) collective-permute-start(bf16[128,4224]{1,0:T(8,128)(2,1)S(1)} %pad_maximum_fusion.refs_0_), channel_id=1, source_target_pairs={{1,0},{0,1},{5,4},{4,5},{9,8},{8,9},{13,12},{12,13},{3,2},{2,3},{7... | collective-permute-start | bytes 3244040 | tf_op jit(solution)/shard_map/ppermute | solution.py:77
  28.9 19.7 %collective-permute-start.4 = (bf16[128,4224]{1,0:T(8,128)(2,1)}, bf16[128,4224]{1,0:T(8,128)(2,1)}, u32[]{:S(2)}, u32[]{:S(2)}) collective-permute-start(bf16[128,4224]{1,0:T(8,128)(2,1)} %collective-permute-done.1.refs_2_), channel_id=1, source_target_pairs={{1,0},{0,1},{5,4},{4,5},{9,8},{8,9},{13,12},{12,13},{3,2},{2,3},{7... | collective-permute-start | bytes 3244040 | tf_op jit(solution)/shard_map/ppermute | solution.py:77
  40.4 1.9 %copy-start.3 = (bf16[128,4224]{1,0:T(8,128)(2,1)}, bf16[128,4224]{1,0:T(8,128)(2,1)S(1)}, u32[]{:S(2)}) copy-start(bf16[128,4224]{1,0:T(8,128)(2,1)S(1)} %collective-permute-done.6.refs_4_.refs_2_) | copy-start | bytes 3244036
  40.4 16.7 %collective-permute-start.7 = (bf16[128,4224]{1,0:T(8,128)(2,1)}, bf16[128,4224]{1,0:T(8,128)(2,1)}, u32[]{:S(2)}, u32[]{:S(2)}) collective-permute-start(bf16[128,4224]{1,0:T(8,128)(2,1)} %collective-permute-done.5.refs_6_.refs_3_), channel_id=1, source_target_pairs={{96,0},{33,1},{100,4},{37,5},{104,8},{41,9},{108,12},{45,13},{98,2... | collective-permute-start | bytes 3244040 | tf_op jit(solution)/shard_map/ppermute | solution.py:72
  42.3 15.5 %collective-permute-start.9 = (bf16[128,4224]{1,0:T(8,128)(2,1)}, bf16[128,4224]{1,0:T(8,128)(2,1)}, u32[]{:S(2)}, u32[]{:S(2)}) collective-permute-start(bf16[128,4224]{1,0:T(8,128)(2,1)} %collective-permute-done.8.refs_5_), channel_id=1, source_target_pairs={{2,0},{13,1},{6,4},{1,5},{10,8},{5,9},{14,12},{9,13},{16,2},{15,3}... | collective-permute-start | bytes 3244040 | tf_op jit(solution)/shard_map/ppermute | solution.py:72
  42.3 16.2 %collective-permute-start.10 = (bf16[128,4224]{1,0:T(8,128)(2,1)}, bf16[128,4224]{1,0:T(8,128)(2,1)}, u32[]{:S(2)}, u32[]{:S(2)}) collective-permute-start(bf16[128,4224]{1,0:T(8,128)(2,1)} %collective-permute-done.8.refs_5_), channel_id=1, source_target_pairs={{4,0},{19,1},{8,4},{23,5},{12,8},{27,9},{0,12},{31,13},{6,2},{1,3}... | collective-permute-start | bytes 3244040 | tf_op jit(solution)/shard_map/ppermute | solution.py:72
  48.5 10.1 %collective-permute-start.12 = (bf16[128,4224]{1,0:T(8,128)(2,1)}, bf16[128,4224]{1,0:T(8,128)(2,1)}, u32[]{:S(2)}, u32[]{:S(2)}) collective-permute-start(bf16[128,4224]{1,0:T(8,128)(2,1)} %copy-done), channel_id=1, source_target_pairs={{1,0},{0,1},{5,4},{4,5},{9,8},{8,9},{13,12},{12,13},{3,2},{2,3},{7... | collective-permute-start | bytes 3244040 | tf_op jit(solution)/shard_map/ppermute | solution.py:77
  48.6 10.5 %collective-permute-start.11 = (bf16[128,4224]{1,0:T(8,128)(2,1)S(1)}, bf16[128,4224]{1,0:T(8,128)(2,1)}, u32[]{:S(2)}, u32[]{:S(2)}) collective-permute-start(bf16[128,4224]{1,0:T(8,128)(2,1)S(1)} %collective-permute-done.refs_1_), channel_id=1, source_target_pairs={{1,0},{0,1},{5,4},{4,5},{9,8},{8,9},{13,12},{12,13},{3,2},{2,3},{7... | collective-permute-start | bytes 3244040 | tf_op jit(solution)/shard_map/ppermute | solution.py:77
  49.2 1.2 %copy-start.1 = (bf16[128,4224]{1,0:T(8,128)(2,1)S(1)}, bf16[128,4224]{1,0:T(8,128)(2,1)}, u32[]{:S(2)}) copy-start(bf16[128,4224]{1,0:T(8,128)(2,1)} %copy-done) | copy-start | bytes 3244036
  50.5 7.3 %copy-start.4 = (bf16[128,4224]{1,0:T(8,128)(2,1)S(1)}, bf16[128,4224]{1,0:T(8,128)(2,1)}, u32[]{:S(2)}) copy-start(bf16[128,4224]{1,0:T(8,128)(2,1)} %copy-done.3) | copy-start | bytes 3244036
  50.5 15.7 %copy-start.2 = (bf16[128,4224]{1,0:T(8,128)(2,1)S(1)}, bf16[128,4224]{1,0:T(8,128)(2,1)}, u32[]{:S(2)}) copy-start(bf16[128,4224]{1,0:T(8,128)(2,1)} %copy-done) | copy-start | bytes 3244036
  57.1 2.9 %collective-permute-start.14 = (bf16[128,4224]{1,0:T(8,128)(2,1)}, bf16[128,4224]{1,0:T(8,128)(2,1)S(1)}, u32[]{:S(2)}, u32[]{:S(2)}) collective-permute-start(bf16[128,4224]{1,0:T(8,128)(2,1)} %collective-permute-done.5.refs_6_.refs_3_), channel_id=1, source_target_pairs={{1,0},{0,1},{5,4},{4,5},{9,8},{8,9},{13,12},{12,13},{3,2},{2,3},{7... | collective-permute-start | bytes 3244040 | tf_op jit(solution)/shard_map/ppermute | solution.py:77
  57.8 5.1 %collective-permute-start.13 = (bf16[128,4224]{1,0:T(8,128)(2,1)S(1)}, bf16[128,4224]{1,0:T(8,128)(2,1)S(1)}, u32[]{:S(2)}, u32[]{:S(2)}) collective-permute-start(bf16[128,4224]{1,0:T(8,128)(2,1)S(1)} %copy-done.4), channel_id=1, source_target_pairs={{1,0},{0,1},{5,4},{4,5},{9,8},{8,9},{13,12},{12,13},{3,2},{2,3},{7... | collective-permute-start | bytes 3244040 | tf_op jit(solution)/shard_map/ppermute | solution.py:77
  58.6 4.7 %collective-permute-start.17 = (bf16[128,4224]{1,0:T(8,128)(2,1)}, bf16[128,4224]{1,0:T(8,128)(2,1)S(1)}, u32[]{:S(2)}, u32[]{:S(2)}) collective-permute-start(bf16[128,4224]{1,0:T(8,128)(2,1)} %collective-permute-done.10.refs_9_.refs_4_), channel_id=1, source_target_pairs={{1,0},{0,1},{5,4},{4,5},{9,8},{8,9},{13,12},{12,13},{3,2},{2,3},{7... | collective-permute-start | bytes 3244040 | tf_op jit(solution)/shard_map/ppermute | solution.py:77
  58.6 6.1 %collective-permute-start.16 = (bf16[128,4224]{1,0:T(8,128)(2,1)}, bf16[128,4224]{1,0:T(8,128)(2,1)S(1)}, u32[]{:S(2)}, u32[]{:S(2)}) collective-permute-start(bf16[128,4224]{1,0:T(8,128)(2,1)} %collective-permute-done.9.refs_8_), channel_id=1, source_target_pairs={{1,0},{0,1},{5,4},{4,5},{9,8},{8,9},{13,12},{12,13},{3,2},{2,3},{7... | collective-permute-start | bytes 3244040 | tf_op jit(solution)/shard_map/ppermute | solution.py:77
  59.1 7.1 %collective-permute-start.15 = (bf16[128,4224]{1,0:T(8,128)(2,1)}, bf16[128,4224]{1,0:T(8,128)(2,1)S(1)}, u32[]{:S(2)}, u32[]{:S(2)}) collective-permute-start(bf16[128,4224]{1,0:T(8,128)(2,1)} %collective-permute-done.7.refs_7_), channel_id=1, source_target_pairs={{1,0},{0,1},{5,4},{4,5},{9,8},{8,9},{13,12},{12,13},{3,2},{2,3},{7... | collective-permute-start | bytes 3244040 | tf_op jit(solution)/shard_map/ppermute | solution.py:77
  60.0 17.9 %collective-permute-start.20 = (bf16[128,4224]{1,0:T(8,128)(2,1)}, bf16[128,4224]{1,0:T(8,128)(2,1)S(1)}, u32[]{:S(2)}, u32[]{:S(2)}) collective-permute-start(bf16[128,4224]{1,0:T(8,128)(2,1)} %collective-permute-done.9.refs_8_), channel_id=1, source_target_pairs={{4,0},{19,1},{8,4},{23,5},{12,8},{27,9},{0,12},{31,13},{6,2},{1,3}... | collective-permute-start | bytes 3244040 | tf_op jit(solution)/shard_map/ppermute | solution.py:72
  62.9 15.2 %collective-permute-start.19 = (bf16[128,4224]{1,0:T(8,128)(2,1)S(1)}, bf16[128,4224]{1,0:T(8,128)(2,1)S(1)}, u32[]{:S(2)}, u32[]{:S(2)}) collective-permute-start(bf16[128,4224]{1,0:T(8,128)(2,1)S(1)} %copy-done.4), channel_id=1, source_target_pairs={{2,0},{13,1},{6,4},{1,5},{10,8},{5,9},{14,12},{9,13},{16,2},{15,3}... | collective-permute-start | bytes 3244040 | tf_op jit(solution)/shard_map/ppermute | solution.py:72
  63.3 16.6 %collective-permute-start.18 = (bf16[128,4224]{1,0:T(8,128)(2,1)}, bf16[128,4224]{1,0:T(8,128)(2,1)S(1)}, u32[]{:S(2)}, u32[]{:S(2)}) collective-permute-start(bf16[128,4224]{1,0:T(8,128)(2,1)} %collective-permute-done.7.refs_7_), channel_id=1, source_target_pairs={{96,0},{33,1},{100,4},{37,5},{104,8},{41,9},{108,12},{45,13},{98,2... | collective-permute-start | bytes 3244040 | tf_op jit(solution)/shard_map/ppermute | solution.py:72

commit v6 on v5

--- a/solution.py
+++ b/solution.py
@@ -119,13 +119,15 @@
     return work
 
 
-def add_pairs(work, blocks, sums, weights, feats):
+def add_pairs(work, blocks, sums, weights, feats, homes=None):
     used = sorted({b for rights, lefts, _ in work for b in (*rights, *lefts)})
     n_tiles = sum(len(rights) * len(lefts) for rights, lefts, _ in work)
     scale = 1.0 / feats**0.5
 
     def body(w_ref, in_ref, *refs):
         out = refs[-1]
+        if homes is not None:
+            home_ref, refs = refs[0], refs[1:]
         ref = dict(zip(used, refs))
         out[...] = in_ref[...]
         eye = lax.broadcasted_iota(jnp.int32, (LANES, LANES), 0) == lax.broadcasted_iota(
@@ -166,19 +168,30 @@
                     wide = jnp.broadcast_to(jnp.sum(back, axis=1, keepdims=True), (LANES, LANES))
                     out[b : b + 1, :] += along(wide)
 
+        if homes is not None:
+            laid = refs[-2]
+            laid[...] = jnp.zeros_like(laid)
+            for k in range(2 * N_SLOTS):
+                laid[pl.ds(home_ref[k], 1), :] = out[k : k + 1, :]
+
+    smem = pl.BlockSpec(memory_space=pltpu.SMEM)
+    vmem = pl.BlockSpec(memory_space=pltpu.VMEM)
+    last = homes is not None
+    kept = jax.ShapeDtypeStruct(sums.shape, jnp.float32)
+    spread = jax.ShapeDtypeStruct((2 * SIDE**3, LANES), jnp.float32)
     return pl.pallas_call(
         body,
-        out_shape=jax.ShapeDtypeStruct(sums.shape, jnp.float32),
-        in_specs=[pl.BlockSpec(memory_space=pltpu.SMEM)]
-        + [pl.BlockSpec(memory_space=pltpu.VMEM)] * (1 + len(used)),
-        out_specs=pl.BlockSpec(memory_space=pltpu.VMEM),
+        out_shape=spread if last else kept,
+        in_specs=[smem, vmem] + ([smem] if last else []) + [vmem] * len(used),
+        out_specs=vmem,
+        scratch_shapes=[pltpu.VMEM(sums.shape, jnp.float32)] if last else [],
         compiler_params=pltpu.CompilerParams(vmem_limit_bytes=24 * 2**20),
         cost_estimate=pl.CostEstimate(
             flops=2 * n_tiles * LANES * LANES * feats,
             bytes_accessed=2 * len(used) * LANES * feats,
             transcendentals=n_tiles * LANES * LANES,
         ),
-    )(weights, sums, *[blocks[b] for b in used])
+    )(weights, sums, *([homes] if last else []), *[blocks[b] for b in used])
 
 
 def on_device(grads, coeffs, band, steps):
@@ -225,10 +238,7 @@
             if slot in OTHERS:
                 blocks[N_SLOTS + slot] = swap(held_back(blocks[slot], until))
     sums = add_pairs(work[2] + work[3], blocks, sums, weights, feats)
-    sums = add_pairs(work[4], blocks, sums, weights, feats)
-
-    home = held[None, :] == jnp.arange(2 * SIDE**3, dtype=jnp.int32)[:, None]
-    parts = jnp.sum(jnp.where(home[:, :, None], sums[None], 0.0), axis=1)
+    parts = add_pairs(work[4], blocks, sums, weights, feats, held)
     total = jnp.sum(lax.all_to_all(parts, AXES, 0, 0, tiled=True), axis=0)
     return total.reshape(-1) / divisor
 

time: 105 us -> 105 us (level)
  no operation moved by 1% of the time
where the time goes in v6:
time: 105 us; the launch traced here: 104 us
  waiting for transfers between devices  37.4 us (36%)
  starting transfers between devices  21.1 us (20%)
  Pallas kernels  20.9 us (20%)
  blocking collectives  17 us (16%)
  other arithmetic  3.12 us (3%)
  local copies, waits for them, and re-layouts  2.62 us (2%)
  between operations  1.52 us (1%)
    ppermute x12, waiting for transfers between devices, shift(): return lax.ppermute(value, AXES, pairs)  34.2 us
    pallas_call x3, Pallas kernels, add_pairs(): pl.pallas_call(body, out_shape=spread if last else kept, in_specs=[smem,...  20.9 us
    ppermute x12, starting transfers between devices, shift(): return lax.ppermute(value, AXES, pairs)  19.4 us
    all_to_all x1, blocking collectives, on_device(): total = jnp.sum(lax.all_to_all(parts, AXES, 0, 0, tiled=True), axis=0)  17 us
    ppermute x9, waiting for transfers between devices, swap(): return lax.ppermute(value, AXES, pairs)  3.2 us
  transfers between devices with their start and end apart: 21, of which 12 were waited for; matrix products, arithmetic and copies ran while one was open for 2% of the time, Pallas kernels for 14%

profile of v6, /device:TPU:0, one launch (start us, length us, event | category | flops | bytes accessed | tf_op | source)
XLA Modules:
  0.0 103.7 jit_solution(1431184766595912263)
XLA Ops:
  0.0 0.7 pad.1.clone
  0.7 1.4 %pad_maximum_fusion.refs_0_.refs_1_ = bf16[128,4224]{1,0:T(8,128)(2,1)S(1)} fusion(bf16[128,4096]{1,0:T(8,128)(2,1)} %param.7, bf16[4224]{0:T(1024)(128)(2,1)S(1)} %pad.1.clone), kind=kLoop, calls=%fused_computation | loop fusion | flops 2162688 | bytes 2138368 | tf_op jit(solution)/shard_map/concatenate | solution.py:213
  2.1 1.6 %collective-permute-start = (bf16[128,4224]{1,0:T(8,128)(2,1)S(1)}, bf16[128,4224]{1,0:T(8,128)(2,1)S(1)}, u32[]{:S(2)}, u32[]{:S(2)}) collective-permute-start(bf16[128,4224]{1,0:T(8,128)(2,1)S(1)} %pad_maximum_fusion.refs_0_.refs_1_), channel_id=1, source_target_pairs={{96,0},{33,1},{100,4},{37,5},{104,8},{41,9},{108,12},{45,13},{98,2... | collective-permute-start | bytes 3244040 | tf_op jit(solution)/shard_map/ppermute | solution.py:72
  3.8 3.0 %collective-permute-start.1 = (bf16[128,4224]{1,0:T(8,128)(2,1)S(1)}, bf16[128,4224]{1,0:T(8,128)(2,1)}, u32[]{:S(2)}, u32[]{:S(2)}) collective-permute-start(bf16[128,4224]{1,0:T(8,128)(2,1)S(1)} %pad_maximum_fusion.refs_0_.refs_1_), channel_id=1, source_target_pairs={{2,0},{13,1},{6,4},{1,5},{10,8},{5,9},{14,12},{9,13},{16,2},{15,3}... | collective-permute-start | bytes 3244040 | tf_op jit(solution)/shard_map/ppermute | solution.py:72
  6.8 11.8 %collective-permute-done.refs_1_.refs_2_ = bf16[128,4224]{1,0:T(8,128)(2,1)S(1)} collective-permute-done((bf16[128,4224]{1,0:T(8,128)(2,1)S(1)}, bf16[128,4224]{1,0:T(8,128)(2,1)S(1)}, u32[]{:S(2)}, u32[]{:S(2)}) %collective-permute-start) | collective-permute-done | bytes 1081376 | tf_op jit(solution)/shard_map/ppermute | solution.py:72
  18.5 0.9 collective-permute-done.1.refs_2_
  19.4 3.7 %collective-permute-done.2.refs_3_ = bf16[128,4224]{1,0:T(8,128)(2,1)S(1)} collective-permute-done((bf16[128,4224]{1,0:T(8,128)(2,1)S(1)}, bf16[128,4224]{1,0:T(8,128)(2,1)S(1)}, u32[]{:S(2)}, u32[]{:S(2)}) %collective-permute-start.2) | collective-permute-done | bytes 1081376 | tf_op jit(solution)/shard_map/ppermute | solution.py:72
  23.1 1.9 %collective-permute-start.5 = (bf16[128,4224]{1,0:T(8,128)(2,1)S(1)}, bf16[128,4224]{1,0:T(8,128)(2,1)}, u32[]{:S(2)}, u32[]{:S(2)}) collective-permute-start(bf16[128,4224]{1,0:T(8,128)(2,1)S(1)} %collective-permute-done.2.refs_3_), channel_id=1, source_target_pairs={{12,0},{3,1},{0,4},{7,5},{4,8},{11,9},{8,12},{15,13},{14,2},{17,3}... | collective-permute-start | bytes 3244040 | tf_op jit(solution)/shard_map/ppermute | solution.py:72
  25.1 1.7 %collective-permute-start.6 = (bf16[128,4224]{1,0:T(8,128)(2,1)}, bf16[128,4224]{1,0:T(8,128)(2,1)S(1)}, u32[]{:S(2)}, u32[]{:S(2)}) collective-permute-start(bf16[128,4224]{1,0:T(8,128)(2,1)} %collective-permute-done.1.refs_2_), channel_id=1, source_target_pairs={{32,0},{97,1},{36,4},{101,5},{40,8},{105,9},{44,12},{109,13},{34,2... | collective-permute-start | bytes 3244040 | tf_op jit(solution)/shard_map/ppermute | solution.py:72
  26.8 2.1 %collective-permute-start.8 = (bf16[128,4224]{1,0:T(8,128)(2,1)S(1)}, bf16[128,4224]{1,0:T(8,128)(2,1)}, u32[]{:S(2)}, u32[]{:S(2)}) collective-permute-start(bf16[128,4224]{1,0:T(8,128)(2,1)S(1)} %collective-permute-done.refs_1_.refs_2_), channel_id=1, source_target_pairs={{4,0},{19,1},{8,4},{23,5},{12,8},{27,9},{0,12},{31,13},{6,2},{1,3}... | collective-permute-start | bytes 3244040 | tf_op jit(solution)/shard_map/ppermute | solution.py:72
  28.9 0.5 collective-permute-start.4
  29.4 11.0 %collective-permute-done.5.refs_6_.refs_4_ = bf16[128,4224]{1,0:T(8,128)(2,1)} collective-permute-done((bf16[128,4224]{1,0:T(8,128)(2,1)S(1)}, bf16[128,4224]{1,0:T(8,128)(2,1)}, u32[]{:S(2)}, u32[]{:S(2)}) %collective-permute-start.5) | collective-permute-done | bytes 1081376 | tf_op jit(solution)/shard_map/ppermute | solution.py:72
  40.4 1.9 %collective-permute-start.7 = (bf16[128,4224]{1,0:T(8,128)(2,1)}, bf16[128,4224]{1,0:T(8,128)(2,1)}, u32[]{:S(2)}, u32[]{:S(2)}) collective-permute-start(bf16[128,4224]{1,0:T(8,128)(2,1)} %collective-permute-done.5.refs_6_.refs_4_), channel_id=1, source_target_pairs={{96,0},{33,1},{100,4},{37,5},{104,8},{41,9},{108,12},{45,13},{98,2... | collective-permute-start | bytes 3244040 | tf_op jit(solution)/shard_map/ppermute | solution.py:72
  42.3 3.2 %collective-permute-start.10 = (bf16[128,4224]{1,0:T(8,128)(2,1)}, bf16[128,4224]{1,0:T(8,128)(2,1)}, u32[]{:S(2)}, u32[]{:S(2)}) collective-permute-start(bf16[128,4224]{1,0:T(8,128)(2,1)} %collective-permute-done.8.refs_5_), channel_id=1, source_target_pairs={{4,0},{19,1},{8,4},{23,5},{12,8},{27,9},{0,12},{31,13},{6,2},{1,3}... | collective-permute-start | bytes 3244040 | tf_op jit(solution)/shard_map/ppermute | solution.py:72
  46.2 0.7 dynamic-slice_bitcast_fusion.refs_0_
  47.1 0.7 fusion
  49.3 1.2 %copy-done.1 = bf16[128,4224]{1,0:T(8,128)(2,1)S(1)} copy-done((bf16[128,4224]{1,0:T(8,128)(2,1)S(1)}, bf16[128,4224]{1,0:T(8,128)(2,1)}, u32[]{:S(2)}) %copy-start.1) | copy-done | bytes 1081368
  50.6 3.1 %shard_map.73 = f32[26,128]{1,0:T(8,128)S(1)} custom-call(f32[2,26,13]{2,1,0:T(8,128)S(1)} %select_select_fusion.w_ref, f32[26,128]{1,0:T(8,128)S(1)} %broadcast_in_dim.45.in_ref, bf16[128,4224]{1,0:T(8,128)(2,1)S(1)} %pad_maximum_fusion.refs_0_.refs_1_, bf16[128,4224]{1,0:T(8,128)(2,1)S(1)} %collective-permute-done.refs_1_.refs_2_, ...), custom_call_target="tpu_custom_call" | custom-call | flops 805306368 | bytes 6291456 | tf_op jit(solution)/shard_map/pallas_call | solution.py:182
  53.6 3.5 %collective-permute-done.7.refs_7_ = bf16[128,4224]{1,0:T(8,128)(2,1)} collective-permute-done((bf16[128,4224]{1,0:T(8,128)(2,1)}, bf16[128,4224]{1,0:T(8,128)(2,1)}, u32[]{:S(2)}, u32[]{:S(2)}) %collective-permute-start.7) | collective-permute-done | bytes 1081376 | tf_op jit(solution)/shard_map/ppermute | solution.py:72
  57.1 0.7 collective-permute-done.9.refs_8_
  57.8 0.8 collective-permute-done.10.refs_9_.refs_5_
  58.6 0.5 collective-permute-start.16
  59.2 0.8 collective-permute-done.14.refs_15_
  60.0 2.9 %collective-permute-start.20 = (bf16[128,4224]{1,0:T(8,128)(2,1)}, bf16[128,4224]{1,0:T(8,128)(2,1)S(1)}, u32[]{:S(2)}, u32[]{:S(2)}) collective-permute-start(bf16[128,4224]{1,0:T(8,128)(2,1)} %collective-permute-done.9.refs_8_), channel_id=1, source_target_pairs={{4,0},{19,1},{8,4},{23,5},{12,8},{27,9},{0,12},{31,13},{6,2},{1,3}... | collective-permute-start | bytes 3244040 | tf_op jit(solution)/shard_map/ppermute | solution.py:72
  63.3 0.6 collective-permute-start.18
  63.9 0.8 collective-permute-done.16.refs_17_.refs_14_
  64.7 1.5 %collective-permute-done.15.refs_16_.refs_13_ = bf16[128,4224]{1,0:T(8,128)(2,1)S(1)} collective-permute-done((bf16[128,4224]{1,0:T(8,128)(2,1)}, bf16[128,4224]{1,0:T(8,128)(2,1)S(1)}, u32[]{:S(2)}, u32[]{:S(2)}) %collective-permute-start.15) | collective-permute-done | bytes 1081376 | tf_op jit(solution)/shard_map/ppermute | solution.py:77
  66.2 11.7 %shard_map.74.in_ref = f32[26,128]{1,0:T(8,128)S(1)} custom-call(f32[2,26,13]{2,1,0:T(8,128)S(1)} %select_select_fusion.w_ref, f32[26,128]{1,0:T(8,128)S(1)} %broadcast_select_fusion.in_ref, bf16[128,4224]{1,0:T(8,128)(2,1)S(1)} %pad_maximum_fusion.refs_0_.refs_1_, bf16[128,4224]{1,0:T(8,128)(2,1)S(1)} %collective-permute-done.refs_1_.refs_2_, ...), custom_call_target="tpu_custom_call" | custom-call | flops 7247757312 | bytes 19922944 | tf_op jit(solution)/shard_map/pallas_call | solution.py:182
  78.0 1.8 %collective-permute-done.18.refs_6_ = bf16[128,4224]{1,0:T(8,128)(2,1)S(1)} collective-permute-done((bf16[128,4224]{1,0:T(8,128)(2,1)}, bf16[128,4224]{1,0:T(8,128)(2,1)S(1)}, u32[]{:S(2)}, u32[]{:S(2)}) %collective-permute-start.18) | collective-permute-done | bytes 1081376 | tf_op jit(solution)/shard_map/ppermute | solution.py:72
  79.9 6.1 %shard_map.75 = f32[128,128]{1,0:T(8,128)S(1)} custom-call(f32[2,26,13]{2,1,0:T(8,128)S(1)} %select_select_fusion.w_ref, f32[26,128]{1,0:T(8,128)S(1)} %shard_map.74.in_ref, s32[26]{0:T(128)S(1)} %dynamic-slice_bitcast_fusion.refs_0_, bf16[128,4224]{1,0:T(8,128)(2,1)S(1)} %pad_maximum_fusion.refs_0_.refs_1_, ...), custom_call_target="tpu_custom_call" | custom-call | flops 2952790016 | bytes 14680064 | tf_op jit(solution)/shard_map/pallas_call | solution.py:182
  86.0 17.0 %all_to_all.9 = f32[128,1,128]{2,1,0:T(1,128)S(1)} all-to-all(f32[128,1,128]{2,1,0:T(1,128)S(1)} %bitcast.12), channel_id=1, replica_groups=mesh['row'=8,'col'=16] {'row','col'}, dimensions={0} | all-to-all | bytes 131072 | tf_op jit(solution)/shard_map/all_to_all | solution.py:242
  103.2 0.5 broadcast_divide_fusion
  (41 shorter events, 1.7 us)
Async XLA Ops:
  0.7 46.3 %copy-start.7 = (s32[128]{0:T(128)S(1)}, s32[128]{0:T(128)}, u32[]{:S(2)}) copy-start(s32[128]{0:T(128)} %param.10) | copy-start | bytes 1540
  0.7 48.6 %copy-start.5 = (f32[2,26,13]{2,1,0:T(8,128)S(1)}, f32[2,26,13]{2,1,0:T(8,128)}, u32[]{:S(2)}) copy-start(f32[2,26,13]{2,1,0:T(8,128)} %constant.41.clone) | copy-start | bytes 8116
  0.7 48.6 %copy-start.6 = (f32[2,26,13]{2,1,0:T(8,128)S(1)}, f32[2,26,13]{2,1,0:T(8,128)}, u32[]{:S(2)}) copy-start(f32[2,26,13]{2,1,0:T(8,128)} %constant.42.clone) | copy-start | bytes 8116
  2.1 16.4 %collective-permute-start = (bf16[128,4224]{1,0:T(8,128)(2,1)S(1)}, bf16[128,4224]{1,0:T(8,128)(2,1)S(1)}, u32[]{:S(2)}, u32[]{:S(2)}) collective-permute-start(bf16[128,4224]{1,0:T(8,128)(2,1)S(1)} %pad_maximum_fusion.refs_0_.refs_1_), channel_id=1, source_target_pairs={{96,0},{33,1},{100,4},{37,5},{104,8},{41,9},{108,12},{45,13},{98,2... | collective-permute-start | bytes 3244040 | tf_op jit(solution)/shard_map/ppermute | solution.py:72
  3.8 15.7 %collective-permute-start.1 = (bf16[128,4224]{1,0:T(8,128)(2,1)S(1)}, bf16[128,4224]{1,0:T(8,128)(2,1)}, u32[]{:S(2)}, u32[]{:S(2)}) collective-permute-start(bf16[128,4224]{1,0:T(8,128)(2,1)S(1)} %pad_maximum_fusion.refs_0_.refs_1_), channel_id=1, source_target_pairs={{2,0},{13,1},{6,4},{1,5},{10,8},{5,9},{14,12},{9,13},{16,2},{15,3}... | collective-permute-start | bytes 3244040 | tf_op jit(solution)/shard_map/ppermute | solution.py:72
  6.8 16.4 %collective-permute-start.2 = (bf16[128,4224]{1,0:T(8,128)(2,1)S(1)}, bf16[128,4224]{1,0:T(8,128)(2,1)S(1)}, u32[]{:S(2)}, u32[]{:S(2)}) collective-permute-start(bf16[128,4224]{1,0:T(8,128)(2,1)S(1)} %pad_maximum_fusion.refs_0_.refs_1_), channel_id=1, source_target_pairs={{18,0},{5,1},{22,4},{9,5},{26,8},{13,9},{30,12},{1,13},{0,2},{7,3}... | collective-permute-start | bytes 3244040 | tf_op jit(solution)/shard_map/ppermute | solution.py:72
  23.1 19.2 %copy-start = (bf16[128,4224]{1,0:T(8,128)(2,1)}, bf16[128,4224]{1,0:T(8,128)(2,1)S(1)}, u32[]{:S(2)}) copy-start(bf16[128,4224]{1,0:T(8,128)(2,1)S(1)} %collective-permute-done.2.refs_3_) | copy-start | bytes 3244036
  23.1 17.3 %collective-permute-start.5 = (bf16[128,4224]{1,0:T(8,128)(2,1)S(1)}, bf16[128,4224]{1,0:T(8,128)(2,1)}, u32[]{:S(2)}, u32[]{:S(2)}) collective-permute-start(bf16[128,4224]{1,0:T(8,128)(2,1)S(1)} %collective-permute-done.2.refs_3_), channel_id=1, source_target_pairs={{12,0},{3,1},{0,4},{7,5},{4,8},{11,9},{8,12},{15,13},{14,2},{17,3}... | collective-permute-start | bytes 3244040 | tf_op jit(solution)/shard_map/ppermute | solution.py:72
  25.1 15.4 %collective-permute-start.6 = (bf16[128,4224]{1,0:T(8,128)(2,1)}, bf16[128,4224]{1,0:T(8,128)(2,1)S(1)}, u32[]{:S(2)}, u32[]{:S(2)}) collective-permute-start(bf16[128,4224]{1,0:T(8,128)(2,1)} %collective-permute-done.1.refs_2_), channel_id=1, source_target_pairs={{32,0},{97,1},{36,4},{101,5},{40,8},{105,9},{44,12},{109,13},{34,2... | collective-permute-start | bytes 3244040 | tf_op jit(solution)/shard_map/ppermute | solution.py:72
  26.8 15.5 %collective-permute-start.8 = (bf16[128,4224]{1,0:T(8,128)(2,1)S(1)}, bf16[128,4224]{1,0:T(8,128)(2,1)}, u32[]{:S(2)}, u32[]{:S(2)}) collective-permute-start(bf16[128,4224]{1,0:T(8,128)(2,1)S(1)} %collective-permute-done.refs_1_.refs_2_), channel_id=1, source_target_pairs={{4,0},{19,1},{8,4},{23,5},{12,8},{27,9},{0,12},{31,13},{6,2},{1,3}... | collective-permute-start | bytes 3244040 | tf_op jit(solution)/shard_map/ppermute | solution.py:72
  28.9 19.7 %collective-permute-start.3 = (bf16[128,4224]{1,0:T(8,128)(2,1)S(1)}, bf16[128,4224]{1,0:T(8,128)(2,1)S(1)}, u32[]{:S(2)}, u32[]{:S(2)}) collective-permute-start(bf16[128,4224]{1,0:T(8,128)(2,1)S(1)} %pad_maximum_fusion.refs_0_.refs_1_), channel_id=1, source_target_pairs={{1,0},{0,1},{5,4},{4,5},{9,8},{8,9},{13,12},{12,13},{3,2},{2,3},{7... | collective-permute-start | bytes 3244040 | tf_op jit(solution)/shard_map/ppermute | solution.py:77
  28.9 19.8 %collective-permute-start.4 = (bf16[128,4224]{1,0:T(8,128)(2,1)}, bf16[128,4224]{1,0:T(8,128)(2,1)}, u32[]{:S(2)}, u32[]{:S(2)}) collective-permute-start(bf16[128,4224]{1,0:T(8,128)(2,1)} %collective-permute-done.1.refs_2_), channel_id=1, source_target_pairs={{1,0},{0,1},{5,4},{4,5},{9,8},{8,9},{13,12},{12,13},{3,2},{2,3},{7... | collective-permute-start | bytes 3244040 | tf_op jit(solution)/shard_map/ppermute | solution.py:77
  40.4 1.9 %copy-start.3 = (bf16[128,4224]{1,0:T(8,128)(2,1)}, bf16[128,4224]{1,0:T(8,128)(2,1)S(1)}, u32[]{:S(2)}) copy-start(bf16[128,4224]{1,0:T(8,128)(2,1)S(1)} %collective-permute-done.6.refs_4_.refs_3_) | copy-start | bytes 3244036
  40.4 16.7 %collective-permute-start.7 = (bf16[128,4224]{1,0:T(8,128)(2,1)}, bf16[128,4224]{1,0:T(8,128)(2,1)}, u32[]{:S(2)}, u32[]{:S(2)}) collective-permute-start(bf16[128,4224]{1,0:T(8,128)(2,1)} %collective-permute-done.5.refs_6_.refs_4_), channel_id=1, source_target_pairs={{96,0},{33,1},{100,4},{37,5},{104,8},{41,9},{108,12},{45,13},{98,2... | collective-permute-start | bytes 3244040 | tf_op jit(solution)/shard_map/ppermute | solution.py:72
  42.3 15.5 %collective-permute-start.9 = (bf16[128,4224]{1,0:T(8,128)(2,1)}, bf16[128,4224]{1,0:T(8,128)(2,1)}, u32[]{:S(2)}, u32[]{:S(2)}) collective-permute-start(bf16[128,4224]{1,0:T(8,128)(2,1)} %collective-permute-done.8.refs_5_), channel_id=1, source_target_pairs={{2,0},{13,1},{6,4},{1,5},{10,8},{5,9},{14,12},{9,13},{16,2},{15,3}... | collective-permute-start | bytes 3244040 | tf_op jit(solution)/shard_map/ppermute | solution.py:72
  42.3 16.2 %collective-permute-start.10 = (bf16[128,4224]{1,0:T(8,128)(2,1)}, bf16[128,4224]{1,0:T(8,128)(2,1)}, u32[]{:S(2)}, u32[]{:S(2)}) collective-permute-start(bf16[128,4224]{1,0:T(8,128)(2,1)} %collective-permute-done.8.refs_5_), channel_id=1, source_target_pairs={{4,0},{19,1},{8,4},{23,5},{12,8},{27,9},{0,12},{31,13},{6,2},{1,3}... | collective-permute-start | bytes 3244040 | tf_op jit(solution)/shard_map/ppermute | solution.py:72
  48.6 10.0 %collective-permute-start.12 = (bf16[128,4224]{1,0:T(8,128)(2,1)}, bf16[128,4224]{1,0:T(8,128)(2,1)}, u32[]{:S(2)}, u32[]{:S(2)}) collective-permute-start(bf16[128,4224]{1,0:T(8,128)(2,1)} %copy-done), channel_id=1, source_target_pairs={{1,0},{0,1},{5,4},{4,5},{9,8},{8,9},{13,12},{12,13},{3,2},{2,3},{7... | collective-permute-start | bytes 3244040 | tf_op jit(solution)/shard_map/ppermute | solution.py:77
  48.7 10.4 %collective-permute-start.11 = (bf16[128,4224]{1,0:T(8,128)(2,1)S(1)}, bf16[128,4224]{1,0:T(8,128)(2,1)}, u32[]{:S(2)}, u32[]{:S(2)}) collective-permute-start(bf16[128,4224]{1,0:T(8,128)(2,1)S(1)} %collective-permute-done.refs_1_.refs_2_), channel_id=1, source_target_pairs={{1,0},{0,1},{5,4},{4,5},{9,8},{8,9},{13,12},{12,13},{3,2},{2,3},{7... | collective-permute-start | bytes 3244040 | tf_op jit(solution)/shard_map/ppermute | solution.py:77
  49.3 1.2 %copy-start.1 = (bf16[128,4224]{1,0:T(8,128)(2,1)S(1)}, bf16[128,4224]{1,0:T(8,128)(2,1)}, u32[]{:S(2)}) copy-start(bf16[128,4224]{1,0:T(8,128)(2,1)} %copy-done) | copy-start | bytes 3244036
  50.5 7.3 %copy-start.4 = (bf16[128,4224]{1,0:T(8,128)(2,1)S(1)}, bf16[128,4224]{1,0:T(8,128)(2,1)}, u32[]{:S(2)}) copy-start(bf16[128,4224]{1,0:T(8,128)(2,1)} %copy-done.3) | copy-start | bytes 3244036
  50.6 15.7 %copy-start.2 = (bf16[128,4224]{1,0:T(8,128)(2,1)S(1)}, bf16[128,4224]{1,0:T(8,128)(2,1)}, u32[]{:S(2)}) copy-start(bf16[128,4224]{1,0:T(8,128)(2,1)} %copy-done) | copy-start | bytes 3244036
  57.1 2.9 %collective-permute-start.14 = (bf16[128,4224]{1,0:T(8,128)(2,1)}, bf16[128,4224]{1,0:T(8,128)(2,1)S(1)}, u32[]{:S(2)}, u32[]{:S(2)}) collective-permute-start(bf16[128,4224]{1,0:T(8,128)(2,1)} %collective-permute-done.5.refs_6_.refs_4_), channel_id=1, source_target_pairs={{1,0},{0,1},{5,4},{4,5},{9,8},{8,9},{13,12},{12,13},{3,2},{2,3},{7... | collective-permute-start | bytes 3244040 | tf_op jit(solution)/shard_map/ppermute | solution.py:77
  57.8 5.1 %collective-permute-start.13 = (bf16[128,4224]{1,0:T(8,128)(2,1)S(1)}, bf16[128,4224]{1,0:T(8,128)(2,1)S(1)}, u32[]{:S(2)}, u32[]{:S(2)}) collective-permute-start(bf16[128,4224]{1,0:T(8,128)(2,1)S(1)} %copy-done.4), channel_id=1, source_target_pairs={{1,0},{0,1},{5,4},{4,5},{9,8},{8,9},{13,12},{12,13},{3,2},{2,3},{7... | collective-permute-start | bytes 3244040 | tf_op jit(solution)/shard_map/ppermute | solution.py:77
  58.6 4.7 %collective-permute-start.17 = (bf16[128,4224]{1,0:T(8,128)(2,1)}, bf16[128,4224]{1,0:T(8,128)(2,1)S(1)}, u32[]{:S(2)}, u32[]{:S(2)}) collective-permute-start(bf16[128,4224]{1,0:T(8,128)(2,1)} %collective-permute-done.10.refs_9_.refs_5_), channel_id=1, source_target_pairs={{1,0},{0,1},{5,4},{4,5},{9,8},{8,9},{13,12},{12,13},{3,2},{2,3},{7... | collective-permute-start | bytes 3244040 | tf_op jit(solution)/shard_map/ppermute | solution.py:77
  58.6 6.1 %collective-permute-start.16 = (bf16[128,4224]{1,0:T(8,128)(2,1)}, bf16[128,4224]{1,0:T(8,128)(2,1)S(1)}, u32[]{:S(2)}, u32[]{:S(2)}) collective-permute-start(bf16[128,4224]{1,0:T(8,128)(2,1)} %collective-permute-done.9.refs_8_), channel_id=1, source_target_pairs={{1,0},{0,1},{5,4},{4,5},{9,8},{8,9},{13,12},{12,13},{3,2},{2,3},{7... | collective-permute-start | bytes 3244040 | tf_op jit(solution)/shard_map/ppermute | solution.py:77
  59.1 7.1 %collective-permute-start.15 = (bf16[128,4224]{1,0:T(8,128)(2,1)}, bf16[128,4224]{1,0:T(8,128)(2,1)S(1)}, u32[]{:S(2)}, u32[]{:S(2)}) collective-permute-start(bf16[128,4224]{1,0:T(8,128)(2,1)} %collective-permute-done.7.refs_7_), channel_id=1, source_target_pairs={{1,0},{0,1},{5,4},{4,5},{9,8},{8,9},{13,12},{12,13},{3,2},{2,3},{7... | collective-permute-start | bytes 3244040 | tf_op jit(solution)/shard_map/ppermute | solution.py:77
  60.0 17.9 %collective-permute-start.20 = (bf16[128,4224]{1,0:T(8,128)(2,1)}, bf16[128,4224]{1,0:T(8,128)(2,1)S(1)}, u32[]{:S(2)}, u32[]{:S(2)}) collective-permute-start(bf16[128,4224]{1,0:T(8,128)(2,1)} %collective-permute-done.9.refs_8_), channel_id=1, source_target_pairs={{4,0},{19,1},{8,4},{23,5},{12,8},{27,9},{0,12},{31,13},{6,2},{1,3}... | collective-permute-start | bytes 3244040 | tf_op jit(solution)/shard_map/ppermute | solution.py:72
  62.9 15.2 %collective-permute-start.19 = (bf16[128,4224]{1,0:T(8,128)(2,1)S(1)}, bf16[128,4224]{1,0:T(8,128)(2,1)S(1)}, u32[]{:S(2)}, u32[]{:S(2)}) collective-permute-start(bf16[128,4224]{1,0:T(8,128)(2,1)S(1)} %copy-done.4), channel_id=1, source_target_pairs={{2,0},{13,1},{6,4},{1,5},{10,8},{5,9},{14,12},{9,13},{16,2},{15,3}... | collective-permute-start | bytes 3244040 | tf_op jit(solution)/shard_map/ppermute | solution.py:72
  63.3 16.6 %collective-permute-start.18 = (bf16[128,4224]{1,0:T(8,128)(2,1)}, bf16[128,4224]{1,0:T(8,128)(2,1)S(1)}, u32[]{:S(2)}, u32[]{:S(2)}) collective-permute-start(bf16[128,4224]{1,0:T(8,128)(2,1)} %collective-permute-done.7.refs_7_), channel_id=1, source_target_pairs={{96,0},{33,1},{100,4},{37,5},{104,8},{41,9},{108,12},{45,13},{98,2... | collective-permute-start | bytes 3244040 | tf_op jit(solution)/shard_map/ppermute | solution.py:72
